TPU v7x, 256 devices: a whole 4x4x8 slice. The times are simulated.
256 devices in a mesh: grp: 8 (over x, core), dev: 32 (over y, z).
Axes of the slice: x: 4, y: 4, z: 8, core: 2. Of those that a mesh axis runs over, the one named last changes fastest.
Arguments:
- enc_tokens: bfloat16 [8, 64, 192, 1024], P('grp', 'dev'), may hold values from -8 to 8
- focal_len: bfloat16 [8, 64], P('grp', 'dev'), may hold values from 6 to 20
- depth_map: bfloat16 [8, 64, 192], P('grp', 'dev'), may hold values from 0.5 to 4
- cameras: bfloat16 [8, 64, 12], P('grp', 'dev'), may hold values from -3 to 3
- pair_graph: int32 [8, 128, 2], P('grp'), may hold values from 0 to 63, as said below
- pair_params: float32 [8, 128, 13], P('grp', 'dev'), may hold values from -3 to 3
- embed_weight: bfloat16 [1024, 768], replicated, may hold values from -0.1875 to 0.1875
- cross_query: bfloat16 [2, 768, 768], replicated, may hold values from -4 to 4
- cross_keyval: bfloat16 [2, 768, 1536], replicated, may hold values from -4 to 4
- cross_out: bfloat16 [2, 768, 768], replicated, may hold values from -0.21875 to 0.21875
- point_heads: bfloat16 [2, 768, 4], replicated, may hold values from -0.21875 to 0.21875
Outputs:
- pair_points: float32 [8, 128, 2, 4, 192], P('grp', 'dev')
- new_depth: float32 [8, 64, 192], P('grp', 'dev')
- new_cameras: float32 [8, 64, 12], P('grp', 'dev')
- new_pair_params: float32 [8, 128, 13], P('grp', 'dev')
Inputs may be any that keep to these rules, and one draw needn't show every extreme that they name: `pair_graph`: pair e of a group is served by device e // 4 of that group's dev axis; image i lies with device i // 2. The 8 images named by one device's 4 pairs lie with 8 different devices.
All inputs are finite; a program needn't handle non-finite values.
Results may differ from a plain program's by a relative error of at most 0.014.
Values may be sent and summed in bfloat16 or wider, within the bound.
No kernel may reach another device: no remote copies, remote signals or barrier semaphores. Data moves between devices by JAX's collectives and lax.ppermute only.
A program may use at most 128 MiB of HBM per device.

v0:
```python
import math

import jax
import jax.numpy as jnp
from jax import lax
from jax.sharding import PartitionSpec as P

HD = 64
GW = 16


norm_eps = 1e-06
stat_eps = 1e-06
step_rate = 0.3


def layer_norm(values_in):
    centre = jnp.mean(values_in, axis=-1, keepdims=True)
    centred = values_in - centre
    spread = jnp.mean(centred * centred, axis=-1, keepdims=True)
    return centred * lax.rsqrt(spread + norm_eps)


def ray_table(focal_in, tok_count, grid_width):
    patch = jnp.arange(tok_count, dtype=jnp.int32)
    column = (patch % grid_width).astype(jnp.float32) - (grid_width - 1) / 2.0
    row_pos = (patch // grid_width).astype(jnp.float32) - (tok_count // grid_width - 1) / 2.0
    focal_col = focal_in[..., None]
    across = column / focal_col
    down = row_pos / focal_col
    return jnp.stack([across, down, jnp.ones_like(across)], axis=-2)


def view_terms(depth_row, camera, focal_in, points, confidence, params):
    tok_count = depth_row.shape[-1]
    ray = ray_table(focal_in, tok_count, GW)
    cam_mat = camera[..., :9].reshape(camera.shape[:-1] + (3, 3))
    cam_shift = camera[..., 9:12]
    cam_points = depth_row[..., None, :] * ray
    world = (
        jnp.sum(cam_mat[..., :, :, None] * cam_points[..., None, :, :], axis=-2)
        + cam_shift[..., None]
    )
    pair_scale = params[..., 0]
    pair_mat = params[..., 1:10].reshape(params.shape[:-1] + (3, 3))
    pair_shift = params[..., 10:13]
    fitted = (
        jnp.sum(pair_mat[..., :, :, None] * points[..., None, :, :], axis=-2)
        + pair_shift[..., None]
    )
    residual = world - pair_scale[..., None, None] * fitted
    weighted = (2.0 * confidence)[..., None, :] * residual
    ray_image = jnp.sum(cam_mat[..., :, :, None] * ray[..., None, :, :], axis=-2)
    grad_depth = jnp.sum(weighted * ray_image, axis=-2)
    grad_mat = jnp.sum(weighted[..., :, None, :] * cam_points[..., None, :, :], axis=-1)
    grad_shift = jnp.sum(weighted, axis=-1)
    grad_scale = -jnp.sum(weighted * fitted, axis=(-2, -1))
    grad_pmat = -pair_scale[..., None, None] * jnp.sum(
        weighted[..., :, None, :] * points[..., None, :, :], axis=-1
    )
    grad_pshift = -pair_scale[..., None] * jnp.sum(weighted, axis=-1)
    grad_cam = jnp.concatenate([grad_mat.reshape(grad_mat.shape[:-2] + (9,)), grad_shift], axis=-1)
    grad_pair = jnp.concatenate(
        [grad_scale[..., None], grad_pmat.reshape(grad_pmat.shape[:-2] + (9,)), grad_pshift],
        axis=-1,
    )
    return (grad_depth, grad_cam, grad_pair)


def decode(query, memory, w_query, w_keyval, w_out, w_head):
    pcount, tok_count, dec_width = query.shape
    normed_query = layer_norm(query.astype(jnp.float32)).astype(jnp.bfloat16).reshape(-1, dec_width)
    normed_memory = (
        layer_norm(memory.astype(jnp.float32)).astype(jnp.bfloat16).reshape(-1, dec_width)
    )
    query_proj = jnp.dot(normed_query, w_query, preferred_element_type=jnp.float32).astype(
        jnp.bfloat16
    )
    keyval = jnp.dot(normed_memory, w_keyval, preferred_element_type=jnp.float32).astype(
        jnp.bfloat16
    )
    query_heads = query_proj.reshape(pcount, tok_count, -1, HD)
    key_heads = keyval[:, :dec_width].reshape(pcount, tok_count, -1, HD)
    value_heads = keyval[:, dec_width:].reshape(pcount, tok_count, -1, HD)
    scores = jnp.einsum(
        "pqhd,pkhd->phqk", query_heads, key_heads, preferred_element_type=jnp.float32
    )
    scores = scores * (1.0 / math.sqrt(HD))
    attn_probs = jax.nn.softmax(scores, axis=-1).astype(jnp.bfloat16)
    context = jnp.einsum(
        "phqk,pkhd->pqhd", attn_probs, value_heads, preferred_element_type=jnp.float32
    )
    context = context.astype(jnp.bfloat16).reshape(-1, dec_width)
    updated = query.astype(jnp.float32).reshape(-1, dec_width) + jnp.dot(
        context, w_out, preferred_element_type=jnp.float32
    )
    decoded = updated.astype(jnp.bfloat16)
    return jnp.dot(decoded, w_head, preferred_element_type=jnp.float32).reshape(
        pcount, tok_count, -1
    )


def on_device(
    enc_tokens,
    focal_len,
    depth_map,
    cameras,
    pair_graph,
    pair_params,
    embed_weight,
    cross_query,
    cross_keyval,
    cross_out,
    point_heads,
):
    device = lax.axis_index("dev")
    peers = lax.axis_size("dev")
    images = enc_tokens[0]
    img_dev, tok_count, enc_width = images.shape
    pair_count = pair_params.shape[1]
    endpoints = pair_graph[0].reshape(peers, 2 * pair_count)
    owner_of = endpoints // img_dev
    mine = owner_of == device
    needed = jnp.any(mine, axis=1)
    local_idx = jnp.sum(jnp.where(mine, endpoints % img_dev, 0), axis=1)
    needed_flag = needed.astype(jnp.bfloat16)

    def select(table):
        picked = jnp.take(table, local_idx, axis=0)
        return picked * needed_flag.reshape((-1,) + (1,) * (table.ndim - 1))

    geo_depth = depth_map[0]
    geo_cam = jnp.concatenate([cameras[0], focal_len[0][:, None]], axis=1)
    my_ends = lax.dynamic_index_in_dim(endpoints, device, 0, keepdims=False)
    slot_of = my_ends // img_dev
    got_tokens, got_depth, got_cam = (
        lax.all_to_all(select(images), "dev", split_axis=0, concat_axis=0, tiled=True),
        lax.all_to_all(select(geo_depth), "dev", split_axis=0, concat_axis=0, tiled=True),
        lax.all_to_all(select(geo_cam), "dev", split_axis=0, concat_axis=0, tiled=True),
    )
    raw_rows = jnp.take(got_tokens, slot_of, axis=0)
    end_emb = jnp.dot(
        raw_rows.reshape(-1, enc_width), embed_weight, preferred_element_type=jnp.float32
    )
    end_emb = end_emb.astype(jnp.bfloat16).reshape(2 * pair_count, tok_count, -1)
    end_depth = (
        jnp.take(got_depth, slot_of, axis=0).astype(jnp.float32).reshape(pair_count, 2, tok_count)
    )
    end_cam = jnp.take(got_cam, slot_of, axis=0).astype(jnp.float32).reshape(pair_count, 2, 13)
    query_emb = end_emb[0::2]
    memory_emb = end_emb[1::2]
    outs_first = decode(
        query_emb, memory_emb, cross_query[0], cross_keyval[0], cross_out[0], point_heads[0]
    )
    outs_second = decode(
        memory_emb, query_emb, cross_query[1], cross_keyval[1], cross_out[1], point_heads[1]
    )
    head_rows = jnp.swapaxes(jnp.stack([outs_first, outs_second], axis=1), 2, 3)
    points = head_rows[:, :, :3]
    confidence = 1.0 + jnp.exp(head_rows[:, :, 3])
    points_out = jnp.concatenate([points, confidence[:, :, None]], axis=2)
    grad_depth, grad_cam, grad_pair = view_terms(
        end_depth,
        end_cam[..., :12],
        end_cam[..., 12],
        points,
        confidence,
        pair_params[0][:, None, :],
    )
    pair_grad = jnp.sum(grad_pair, axis=1)
    flat_depth = grad_depth.reshape(2 * pair_count, tok_count)
    flat_cam = grad_cam.reshape(2 * pair_count, 12)
    hit_table = (slot_of[:, None] == jnp.arange(peers, dtype=jnp.int32)[None, :]).astype(
        jnp.float32
    )
    slot_depth = jnp.sum(hit_table[:, :, None] * flat_depth[:, None, :], axis=0)
    slot_cam = jnp.sum(hit_table[:, :, None] * flat_cam[:, None, :], axis=0)
    back_depth, back_cam = (
        lax.all_to_all(slot_depth, "dev", split_axis=0, concat_axis=0, tiled=True),
        lax.all_to_all(slot_cam, "dev", split_axis=0, concat_axis=0, tiled=True),
    )
    own_table = (
        (local_idx[:, None] == jnp.arange(img_dev, dtype=jnp.int32)[None, :]) & needed[:, None]
    ).astype(jnp.float32)
    image_depth = jnp.sum(own_table[:, :, None] * back_depth[:, None, :], axis=0)
    image_cam = jnp.sum(own_table[:, :, None] * back_cam[:, None, :], axis=0)
    local_square = (
        jnp.sum(image_depth * image_depth)
        + jnp.sum(image_cam * image_cam)
        + jnp.sum(pair_grad * pair_grad)
    )
    grad_total = lax.psum(local_square, ("grp", "dev"))
    param_count = lax.axis_size("grp") * peers * (img_dev * (tok_count + 12) + 13 * pair_count)
    step_size = step_rate / jnp.sqrt(grad_total / param_count + stat_eps)
    new_depth = depth_map[0].astype(jnp.float32) - step_size * image_depth
    new_cameras = cameras[0].astype(jnp.float32) - step_size * image_cam
    new_pair_params = pair_params[0] - step_size * pair_grad
    return (points_out[None], new_depth[None], new_cameras[None], new_pair_params[None])


def solution(mesh):
    placed = (
        P("grp", "dev", None, None),
        P("grp", "dev"),
        P("grp", "dev", None),
        P("grp", "dev", None),
        P("grp", None, None),
        P("grp", "dev", None),
        P(),
        P(),
        P(),
        P(),
        P(),
    )
    return jax.shard_map(
        on_device,
        mesh=mesh,
        in_specs=placed,
        out_specs=(
            P("grp", "dev", None, None, None),
            P("grp", "dev", None),
            P("grp", "dev", None),
            P("grp", "dev", None),
        ),
        check_vma=False,
    )
```

profile of v0, /device:TPU:1, one launch (start us, length us, event | category | flops | bytes accessed | tf_op | source)
XLA Modules:
  0.0 553.5 jit_solution(12824831844035683867)
XLA Ops:
  0.7 0.8 fusion.72
  1.5 0.7 fusion.64
  2.7 0.8 copy.242
  3.4 0.7 pad_maximum_fusion.1
  4.9 0.7 copy.244
  5.6 12.0 %all-to-all-start.1 = ((bf16[32,1,13]{2,1,0:T(2,128)(2,1)}), bf16[32,1,13]{2,1,0:T(2,128)(2,1)S(1)}, u32[]{:S(2)}, u32[]{:S(2)}) async-start(bf16[32,1,13]{2,1,0:T(2,128)(2,1)} %copy.244), calls=%async_computation.1 | async-start | bytes 32768 | tf_op jit(solution)/shard_map/all_to_all | solution.py:139
  17.6 1.3 gather_fusion.4
  19.0 7.6 %gather_fusion = bf16[32,192,1024]{2,1,0:T(8,128)(2,1)} fusion(bf16[2,192,1024]{2,1,0:T(8,128)(2,1)} %bitcast.143, s32[1024]{0:T(1024)S(1)} %pad_clamp_fusion.1), kind=kCustom, calls=%fused_computation | custom fusion | bytes 25165952 | tf_op jit(solution)/shard_map/jit(_take)/gather | solution.py:129
  27.2 9.0 %all-to-all-start.2 = ((bf16[32,1,192]{2,1,0:T(2,128)(2,1)}), bf16[32,1,192]{2,1,0:T(2,128)(2,1)S(1)}, u32[]{:S(2)}, u32[]{:S(2)}) async-start(bf16[32,1,192]{2,1,0:T(2,128)(2,1)} %copy.250), calls=%async_computation.2 | async-start | bytes 65536 | tf_op jit(solution)/shard_map/all_to_all | solution.py:138
  36.3 10.9 %select_multiply_fusion = bf16[32,192,1024]{2,1,0:T(8,128)(2,1)} fusion(bf16[32,192,1024]{2,1,0:T(8,128)(2,1)} %gather_fusion, pred[32]{0:T(512)(128)(4,1)S(1)} %compare_and_fusion.1, bf16[32]{0:T(256)(128)(2,1)S(1)} %convert_element_type.115), kind=kLoop, calls=%fused_computation.8 | loop fusion | flops 12582912 | bytes 25165920 | tf_op jit(solution)/shard_map/mul | solution.py:130
  47.1 9.7 %all-to-all-start = ((bf16[32,192,1024]{2,1,0:T(8,128)(2,1)}), bf16[32,192,1024]{2,1,0:T(8,128)(2,1)}, u32[]{:S(2)}, u32[]{:S(2)}) async-start(bf16[32,192,1024]{2,1,0:T(8,128)(2,1)} %select_multiply_fusion), calls=%async_computation | async-start | bytes 25165824 | tf_op jit(solution)/shard_map/all_to_all | solution.py:137
  60.2 276.4 %all-to-all-done = bf16[32,192,1024]{2,1,0:T(8,128)(2,1)} async-done(((bf16[32,192,1024]{2,1,0:T(8,128)(2,1)}), bf16[32,192,1024]{2,1,0:T(8,128)(2,1)}, u32[]{:S(2)}, u32[]{:S(2)}) %all-to-all-start) | async-done | bytes 12582944 | tf_op jit(solution)/shard_map/all_to_all | solution.py:137
  336.6 7.0 %gather_fusion.1 = bf16[8,192,1024]{2,1,0:T(8,128)(2,1)} fusion(bf16[32,192,1024]{2,1,0:T(8,128)(2,1)} %all-to-all-done, s32[1024]{0:T(1024)S(1)} %pad_clamp_fusion), kind=kCustom, calls=%fused_computation.1 | custom fusion | bytes 6291488 | tf_op jit(solution)/shard_map/jit(_take)/gather | solution.py:141
  343.6 2.5 bitcast_select_fusion
  346.2 2.8 convolution_convert_fusion
  349.4 1.6 fusion.75
  351.0 0.8 multiply_reduce_fusion.3
  351.8 0.7 multiply_convert_fusion.1
  352.6 2.0 convolution_convert_fusion.2
  354.6 3.4 convolution_convert_fusion.1
  358.0 2.1 convolution_convert_fusion.4
  360.1 2.1 convolution_convert_fusion.3
  362.4 3.3 reshape.572
  365.7 4.7 reshape.571
  370.4 4.3 fusion.18
  374.6 5.0 fusion.78
  379.6 3.2 reshape.570
  382.9 5.8 %fusion.32 = bf16[4,192,12,64]{1,3,2,0:T(8,128)(2,1)S(1)} fusion(f32[4,12,192,192]{2,3,1,0:T(8,128)} %get-tuple-element.67, f32[4,12,192]{2,1,0:T(8,128)S(1)} %get-tuple-element.66, bf16[4,192,12,64]{3,2,1,0:T(8,128)(2,1)} %reshape.570), kind=kOutput, calls=%fused_computation.51 | convolution fusion | flops 230621184 | bytes 9474048 | tf_op jit(solution)/shard_map/phqk,pkhd->pqhd/dot_general | solution.py:90
  388.7 1.2 copy.233
  390.0 2.3 reshape.512
  392.2 1.8 fusion.76
  394.0 3.3 reshape.575
  397.2 4.7 reshape.574
  402.0 4.3 fusion.12
  406.2 5.0 fusion.77
  411.2 3.2 reshape.573
  414.5 5.8 %fusion.35 = bf16[4,192,12,64]{1,3,2,0:T(8,128)(2,1)S(1)} fusion(f32[4,12,192,192]{2,3,1,0:T(8,128)} %get-tuple-element.65, f32[4,12,192]{2,1,0:T(8,128)S(1)} %get-tuple-element.64, bf16[4,192,12,64]{3,2,1,0:T(8,128)(2,1)} %reshape.573), kind=kOutput, calls=%fused_computation.52 | convolution fusion | flops 230621184 | bytes 9474048 | tf_op jit(solution)/shard_map/phqk,pkhd->pqhd/dot_general | solution.py:90
  420.3 1.2 copy.241
  421.6 2.3 reshape.518
  423.8 2.9 fusion.23
  427.2 1.1 fusion.17
  429.9 0.7 copy.264
  430.6 16.5 %all-to-all-start.4 = ((f32[32,1,12]{2,1,0:T(1,128)}), f32[32,1,12]{2,1,0:T(1,128)S(1)}, u32[]{:S(2)}, u32[]{:S(2)}) async-start(f32[32,1,12]{2,1,0:T(1,128)} %copy.264), calls=%async_computation.4 | async-start | bytes 32768 | tf_op jit(solution)/shard_map/all_to_all | solution.py:180
  447.9 0.6 copy.260
  448.5 7.2 %all-to-all-done.4 = f32[32,1,12]{2,1,0:T(1,128)S(1)} async-done(((f32[32,1,12]{2,1,0:T(1,128)}), f32[32,1,12]{2,1,0:T(1,128)S(1)}, u32[]{:S(2)}, u32[]{:S(2)}) %all-to-all-start.4) | async-done | bytes 1568 | tf_op jit(solution)/shard_map/all_to_all | solution.py:180
  455.7 3.9 all-to-all-start.3
  460.3 7.9 %all-to-all-done.3 = f32[32,1,192]{2,1,0:T(1,128)S(1)} async-done(((f32[32,1,192]{2,1,0:T(1,128)}), f32[32,1,192]{2,1,0:T(1,128)S(1)}, u32[]{:S(2)}, u32[]{:S(2)}) %all-to-all-start.3) | async-done | bytes 24608 | tf_op jit(solution)/shard_map/all_to_all | solution.py:179
  471.5 79.4 %psum.7 = f32[]{:T(128)} all-reduce(f32[]{:T(128)S(6)} %add.195), channel_id=1, replica_groups=mesh['grp'=8,'dev'=32] {'grp','dev'}, use_global_device_ids=true, to_apply=%region_28.29 | all-reduce | flops 1 | bytes 8 | tf_op jit(solution)/shard_map/psum | solution.py:192
  (129 shorter events, 12.5 us)
Async XLA Ops:
  0.6 345.5 %copy-start = (bf16[1024,768]{1,0:T(8,128)(2,1)S(1)}, bf16[1024,768]{1,0:T(8,128)(2,1)}, u32[]{:S(2)}) copy-start(bf16[1024,768]{1,0:T(8,128)(2,1)} %param.17) | copy-start | bytes 4718596
  5.6 21.7 %all-to-all-start.1 = ((bf16[32,1,13]{2,1,0:T(2,128)(2,1)}), bf16[32,1,13]{2,1,0:T(2,128)(2,1)S(1)}, u32[]{:S(2)}, u32[]{:S(2)}) async-start(bf16[32,1,13]{2,1,0:T(2,128)(2,1)} %copy.244), calls=%async_computation.1 | async-start | bytes 32768 | tf_op jit(solution)/shard_map/all_to_all | solution.py:139
  27.2 19.9 %all-to-all-start.2 = ((bf16[32,1,192]{2,1,0:T(2,128)(2,1)}), bf16[32,1,192]{2,1,0:T(2,128)(2,1)S(1)}, u32[]{:S(2)}, u32[]{:S(2)}) async-start(bf16[32,1,192]{2,1,0:T(2,128)(2,1)} %copy.250), calls=%async_computation.2 | async-start | bytes 65536 | tf_op jit(solution)/shard_map/all_to_all | solution.py:138
  47.1 9.7 %copy-start.8 = (s32[1,128,2]{1,2,0:T(2,128)S(1)}, s32[1,128,2]{1,2,0:T(2,128)}, u32[]{:S(2)}) copy-start(s32[1,128,2]{1,2,0:T(2,128)} %param.15) | copy-start | bytes 3076
  47.1 10.1 %copy-start.6 = (f32[1,4,13]{2,1,0:T(4,128)S(1)}, f32[1,4,13]{2,1,0:T(4,128)}, u32[]{:S(2)}) copy-start(f32[1,4,13]{2,1,0:T(4,128)} %param.16) | copy-start | bytes 628
  47.1 289.5 %all-to-all-start = ((bf16[32,192,1024]{2,1,0:T(8,128)(2,1)}), bf16[32,192,1024]{2,1,0:T(8,128)(2,1)}, u32[]{:S(2)}, u32[]{:S(2)}) async-start(bf16[32,192,1024]{2,1,0:T(8,128)(2,1)} %select_multiply_fusion), calls=%async_computation | async-start | bytes 25165824 | tf_op jit(solution)/shard_map/all_to_all | solution.py:137
  343.6 8.9 %slice-start = ((s8[4718592]{0:T(1024)(128)(4,1)}), s8[4194304]{0:T(1024)(128)(4,1)S(1)}, s32[]{:S(2)}) async-start(s8[4718592]{0:T(1024)(128)(4,1)} %bitcast.173), calls=%async_computation.5 | async-start | bytes 8388608
  346.1 6.4 %slice-start.1 = ((s8[4718592]{0:T(1024)(128)(4,1)}), s8[524288]{0:T(1024)(128)(4,1)S(1)}, s32[]{:S(2)}) async-start(s8[4718592]{0:T(1024)(128)(4,1)} %bitcast.173), calls=%async_computation.6 | async-start | bytes 1048576
  354.6 3.4 copy-start.10
  420.3 3.5 copy-start.4
  423.8 2.9 copy-start.7
  423.8 3.3 copy-start.3
  423.8 3.3 copy-start.5
  423.8 3.3 copy-start.11
  427.2 126.4 %copy-start.1 = (bf16[1024,768]{1,0:T(8,128)(2,1)S(1)}, bf16[1024,768]{1,0:T(8,128)(2,1)}, u32[]{:S(2)}) copy-start(bf16[1024,768]{1,0:T(8,128)(2,1)} %param.17) | copy-start | bytes 4718596
  428.4 123.3 %copy-start.2 = (bf16[1,2,192]{2,1,0:T(2,128)(2,1)S(1)}, bf16[1,2,192]{2,1,0:T(2,128)(2,1)}, u32[]{:S(2)}) copy-start(bf16[1,2,192]{2,1,0:T(2,128)(2,1)} %param.13) | copy-start | bytes 2308
  428.4 124.6 %copy-start.9 = (bf16[1,2,12]{2,1,0:T(2,128)(2,1)S(1)}, bf16[1,2,12]{2,1,0:T(2,128)(2,1)}, u32[]{:S(2)}) copy-start(bf16[1,2,12]{2,1,0:T(2,128)(2,1)} %param.14) | copy-start | bytes 148
  430.6 25.1 %all-to-all-start.4 = ((f32[32,1,12]{2,1,0:T(1,128)}), f32[32,1,12]{2,1,0:T(1,128)S(1)}, u32[]{:S(2)}, u32[]{:S(2)}) async-start(f32[32,1,12]{2,1,0:T(1,128)} %copy.264), calls=%async_computation.4 | async-start | bytes 32768 | tf_op jit(solution)/shard_map/all_to_all | solution.py:180
  455.7 12.6 %all-to-all-start.3 = ((f32[32,1,192]{2,1,0:T(1,128)}), f32[32,1,192]{2,1,0:T(1,128)S(1)}, u32[]{:S(2)}, u32[]{:S(2)}) async-start(f32[32,1,192]{2,1,0:T(1,128)} %copy.260), calls=%async_computation.3 | async-start | bytes 65536 | tf_op jit(solution)/shard_map/all_to_all | solution.py:179
where the time goes:
time: 553 us; the launch traced here: 554 us
  waiting for transfers between devices  292 us (53%)
  blocking collectives  79.4 us (14%)
  local copies, waits for them, and re-layouts  57.1 us (10%)
  starting transfers between devices  51 us (9%)
  matrix products  37.5 us (7%)
  other arithmetic  33.2 us (6%)
    all_to_all x1, waiting for transfers between devices, on_device(): lax.all_to_all(select(images), 'dev', split_axis=0, concat_axis=0, tiled=...  276 us
    psum x1, blocking collectives, on_device(): grad_total = lax.psum(local_square, ('grp', 'dev'))  79.4 us
    all_to_all x1, starting transfers between devices, on_device(): lax.all_to_all(slot_cam, 'dev', split_axis=0, concat_axis=0, tiled=True)  16.5 us
    all_to_all x1, starting transfers between devices, on_device(): lax.all_to_all(select(geo_cam), 'dev', split_axis=0, concat_axis=0, tiled...  12 us
    dot_general x2, matrix products, decode(): jnp.einsum('phqk,pkhd->pqhd', attn_probs, value_heads, preferred_element_...  11.7 us
  transfers between devices with their start and end apart: 5, of which 3 were waited for; matrix products, arithmetic and copies ran while one was open for 5% of the time, Pallas kernels for 0%

commit v1 on v0

v1 whole, which is shorter than its diff:
```python
import functools
import math

import jax
import jax.numpy as jnp
import numpy as np
from jax import lax
from jax.experimental import pallas as pl
from jax.experimental.pallas import tpu as pltpu
from jax.sharding import PartitionSpec as P

HEADS = 12
HD = 64
DD = 768
TOK = 192
GW = 16
PEERS = 32
ROWS = TOK // PEERS
SPREAD = 16
REFS = 8
PAIRS = 4

norm_eps = 1e-06
stat_eps = 1e-06
step_rate = 0.3

F32 = jnp.float32
BF16 = jnp.bfloat16
NT = (((1,), (1,)), ((), ()))
MIB = 1024 * 1024


def params_for(mib):
    return pltpu.CompilerParams(vmem_limit_bytes=mib * MIB)


def dot(left, right):
    return jnp.dot(left, right, preferred_element_type=F32)


def dot_nt(left, right):
    return lax.dot_general(left, right, NT, preferred_element_type=F32)


def spread_order():
    table = np.zeros((8 * SPREAD, 112), np.float32)
    for peer in range(8):
        for row in range(ROWS):
            table[peer * SPREAD + row, peer * ROWS + row] = 1
            table[peer * SPREAD + ROWS + row, 48 + peer * ROWS + row] = 1
        table[peer * SPREAD + 2 * ROWS, 96] = 1
        table[peer * SPREAD + 2 * ROWS + 1, 97] = 1
    return jnp.asarray(table, BF16)


def gather_order():
    table = np.zeros((384, 384), np.float32)
    for image in range(REFS):
        for source in range(8):
            for row in range(ROWS):
                table[image * 48 + source * ROWS + row, source * 48 + image * ROWS + row] = 1
    return jnp.asarray(table, BF16)


def embed_kernel(tokens_ref, weight_ref, geo_ref, order_ref, out_ref, emb_ref):
    emb_ref[...] = dot(tokens_ref[...], weight_ref[...]).astype(BF16)
    for part in range(4):
        rows = jnp.concatenate(
            [emb_ref[part * 48 : part * 48 + 48], emb_ref[TOK + part * 48 : TOK + part * 48 + 48], geo_ref[...]],
            axis=0,
        )
        out_ref[part * 128 : (part + 1) * 128] = dot(order_ref[...], rows).astype(BF16)


def select_kernel(rows_ref, where_ref, own_ref, out_ref, geo_ref):
    total = rows_ref.shape[0]
    lane = lax.broadcasted_iota(jnp.int32, (TOK, total), 1)

    @pl.loop(0, PEERS * REFS * ROWS // TOK)
    def _(step):
        at = pl.ds(pl.multiple_of(step * TOK, TOK), TOK)
        pick = jnp.where(where_ref[at, :][:, :1] == lane, 1.0, 0.0).astype(BF16)
        out_ref[at, :] = dot(pick, rows_ref[...]).astype(BF16)

    own_lane = lax.broadcasted_iota(jnp.int32, (16, total), 1)
    own = jnp.where(own_ref[...][:, :1] == own_lane, 1.0, 0.0).astype(BF16)
    geo_ref[...] = dot(own, rows_ref[:, 0:256])[0:REFS]


def fold_kernel(head_ref, out_ref, value_ref, fold_ref):
    sub = lax.broadcasted_iota(jnp.int32, (16, DD), 0)
    lane = lax.broadcasted_iota(jnp.int32, (16, DD), 1)
    for view in range(2):
        both = dot_nt(head_ref[view], out_ref[view])
        high = both.astype(BF16).astype(F32)
        low = (both - high).astype(BF16).astype(F32)
        pair = jnp.concatenate([high[0:8], low[0:8]], axis=0)
        left = jnp.concatenate(
            [jnp.where(lane // HD == head, pair, 0.0).astype(BF16) for head in range(HEADS)], axis=0
        )
        full = dot_nt(left, value_ref[view])
        for head in range(HEADS):
            term = full[head * 16 : head * 16 + 8] + full[head * 16 + 8 : head * 16 + 16]
            top = term.astype(BF16).astype(F32)
            rest = term - top
            fold_ref[view, head * 16 : head * 16 + 16] = jnp.concatenate([top, rest], axis=0).astype(BF16)


def view_gradients(outs, geo, par):
    token = lax.broadcasted_iota(jnp.int32, (REFS, TOK), 1)
    column = (token & (GW - 1)).astype(F32) - (GW - 1) / 2.0
    row_pos = (token >> 4).astype(F32) - (TOK // GW - 1) / 2.0
    depth = geo[:, 0:TOK]
    cam = [geo[:, TOK + i : TOK + i + 1] for i in range(12)]
    focal = geo[:, TOK + 12 : TOK + 13]
    ray = [column / focal, row_pos / focal, jnp.ones_like(column)]
    cam_points = [depth * ray[0], depth * ray[1], depth]
    scale = par[:, 0:1]
    mat = [par[:, 1 + i : 2 + i] for i in range(9)]
    shift = [par[:, 10 + i : 11 + i] for i in range(3)]
    points = outs[:3]
    confidence = outs[3]
    fitted, weighted, ray_image = [], [], []
    for r in range(3):
        world = cam[3 * r] * cam_points[0] + cam[3 * r + 1] * cam_points[1] + cam[3 * r + 2] * cam_points[2]
        world = world + cam[9 + r]
        fit = mat[3 * r] * points[0] + mat[3 * r + 1] * points[1] + mat[3 * r + 2] * points[2] + shift[r]
        fitted.append(fit)
        weighted.append((2.0 * confidence) * (world - scale * fit))
        ray_image.append(cam[3 * r] * ray[0] + cam[3 * r + 1] * ray[1] + cam[3 * r + 2])
    grad_depth = weighted[0] * ray_image[0] + weighted[1] * ray_image[1] + weighted[2] * ray_image[2]

    def total(x):
        return jnp.sum(x, axis=1, keepdims=True)

    sums = [total(w) for w in weighted]
    entries = [total(weighted[r] * cam_points[c]) for r in range(3) for c in range(3)] + sums
    entries.append(-total(weighted[0] * fitted[0] + weighted[1] * fitted[1] + weighted[2] * fitted[2]))
    entries += [-scale * total(weighted[r] * points[c]) for r in range(3) for c in range(3)]
    entries += [-scale * s for s in sums]
    lane = lax.broadcasted_iota(jnp.int32, (REFS, 64), 1)
    tail = jnp.zeros((REFS, 64), F32)
    for i, entry in enumerate(entries):
        tail = jnp.where(lane == i, entry, tail)
    return grad_depth, tail


def decode_kernel(
    rows_ref, order_ref, query_ref, key_ref, fold_ref, head_ref, geo_ref, par_ref,
    points_ref, grad_ref, x_ref, n_ref, q_ref, k_ref, u_ref, e_ref, o_ref,
):
    for part in range(4):
        mixed = dot(order_ref[...], rows_ref[part * 384 : (part + 1) * 384]).astype(BF16)
        for image in range(REFS):
            at = (image // 2) * TOK + part * 48
            x_ref[image % 2, at : at + 48] = mixed[image * 48 : image * 48 + 48]

    for slot in range(2):
        @pl.loop(0, PAIRS)
        def _(pair):
            at = pl.ds(pl.multiple_of(pair * TOK, TOK), TOK)
            wide = x_ref[slot, at, :].astype(F32)
            centred = wide - jnp.mean(wide, axis=-1, keepdims=True)
            spread = jnp.mean(centred * centred, axis=-1, keepdims=True)
            n_ref[slot, at, :] = (centred * lax.rsqrt(spread + norm_eps)).astype(BF16)

    ones_row = jnp.where(lax.broadcasted_iota(jnp.int32, (8, TOK), 0) == 4, 1.0, 0.0)
    for view in range(2):
        @pl.loop(0, PAIRS)
        def _(pair):
            at = pl.ds(pl.multiple_of(pair * TOK, TOK), TOK)
            query = n_ref[view, at, :]
            memory = n_ref[1 - view, at, :]
            q_ref[view, at, :] = dot(query, query_ref[view]).astype(BF16)
            k_ref[view, at, :] = dot(memory, key_ref[view]).astype(BF16)
            value = dot_nt(fold_ref[view], memory)
            for head in range(HEADS):
                term = value[head * 16 : head * 16 + 8] + value[head * 16 + 8 : head * 16 + 16] + ones_row
                u_ref[view, pair, head * 16 : head * 16 + 16] = jnp.concatenate(
                    [term, jnp.zeros_like(term)], axis=0
                ).astype(BF16)
            e_ref[view, pair] = dot_nt(head_ref[view], x_ref[view, at, :])[0:8]

    upper = lax.broadcasted_iota(jnp.int32, (TOK, 2 * HD), 1) >= HD
    factor = math.log2(math.e) / math.sqrt(HD)
    for view in range(2):
        @pl.loop(0, PAIRS)
        def _(pair):
            at = pl.ds(pl.multiple_of(pair * TOK, TOK), TOK)
            acc = e_ref[view, pair]
            for two in range(HEADS // 2):
                cols = slice(two * 2 * HD, (two + 1) * 2 * HD)
                keys = k_ref[view, at, cols]
                queries = q_ref[view, at, cols]
                for half in range(2):
                    head = 2 * two + half
                    part = jnp.where(upper if half else jnp.logical_not(upper), queries, jnp.zeros_like(queries))
                    scores = dot_nt(keys, part)
                    top = jnp.max(scores, axis=0, keepdims=True)
                    probs = jnp.exp2((scores - top) * factor).astype(BF16)
                    mixed = dot(u_ref[view, pair, head * 16 : head * 16 + 16], probs)[0:8]
                    acc = acc + mixed * (1.0 / mixed[4:5])
            sub = lax.broadcasted_iota(jnp.int32, (8, TOK), 0)
            acc = jnp.where(sub == 3, 1.0 + jnp.exp(acc), acc)
            points_ref[2 * pair + view] = acc[0:4]
            for c in range(4):
                o_ref[c, pl.ds(2 * pair + view, 1), :] = acc[c : c + 1]

    grad_depth, tail = view_gradients([o_ref[c] for c in range(4)], geo_ref[...], par_ref[...])
    both = jnp.concatenate([grad_depth, tail], axis=1)
    for peer in range(PEERS):
        grad_ref[peer * REFS : (peer + 1) * REFS] = both


def split_dot(pick, wide):
    high = wide.astype(BF16)
    rest = wide - high.astype(F32)
    middle = rest.astype(BF16)
    low = (rest - middle.astype(F32)).astype(BF16)
    return dot(pick, high) + dot(pick, middle) + dot(pick, low)


def combine_kernel(me_ref, graph_ref, grad_ref, own_ref, square_ref):
    refs = PEERS * REFS
    me = me_ref[0]
    graph = graph_ref[...]
    grads = grad_ref[...]
    image = lax.broadcasted_iota(jnp.int32, (2 * PEERS, refs), 0)
    image_sum = split_dot(jnp.where(graph == image, 1.0, 0.0).astype(BF16), grads)
    pair = lax.broadcasted_iota(jnp.int32, (refs // 2, refs), 0)
    view = lax.broadcasted_iota(jnp.int32, (refs // 2, refs), 1)
    pair_sum = split_dot(jnp.where((view >> 1) == pair, 1.0, 0.0).astype(BF16), grads)
    image_lane = lax.broadcasted_iota(jnp.int32, (2 * PEERS, 256), 1)
    pair_lane = lax.broadcasted_iota(jnp.int32, (refs // 2, 256), 1)
    image_sq = jnp.where(image_lane < TOK + 12, image_sum * image_sum, 0.0)
    pair_sq = jnp.where((pair_lane >= TOK + 12) & (pair_lane < TOK + 25), pair_sum * pair_sum, 0.0)
    square = jnp.sum(image_sq) + jnp.sum(pair_sq)
    square_ref[...] = jnp.full((1, 128), square, F32)
    row = lax.broadcasted_iota(jnp.int32, (16, refs), 0)
    ref = lax.broadcasted_iota(jnp.int32, (16, refs), 1)
    own_image = (row < 2) & (graph == 2 * me + row)
    own_pair = (row >= 8) & (row < 8 + PAIRS) & ((ref >> 1) == PAIRS * me + row - 8)
    own_ref[...] = split_dot(jnp.where(own_image | own_pair, 1.0, 0.0).astype(BF16), grads)


def update_kernel(count, square_ref, own_ref, depth_ref, camera_ref, par_ref, depth_out, camera_out, par_out):
    total = jnp.sum(square_ref[...], axis=0, keepdims=True)[:, 0:1]
    step = step_rate / jnp.sqrt(total / count + stat_eps)
    depth_out[...] = depth_ref[...].astype(F32) - step * own_ref[0:2, 0:TOK]
    camera_out[...] = camera_ref[...].astype(F32) - step * own_ref[0:2, TOK : TOK + 12]
    par_out[...] = par_ref[...] - step * own_ref[8 : 8 + PAIRS, TOK + 12 : TOK + 25]


def shape(dims, kind):
    return jax.ShapeDtypeStruct(dims, kind)


def whole():
    return pl.BlockSpec(memory_space=pltpu.VMEM)


def on_device(
    enc_tokens, focal_len, depth_map, cameras, pair_graph, pair_params,
    embed_weight, cross_query, cross_keyval, cross_out, point_heads,
):
    me = lax.axis_index("dev")
    tokens = enc_tokens[0].reshape(2 * TOK, -1)
    geo = jnp.concatenate([depth_map[0], cameras[0], focal_len[0][:, None]], axis=1)
    geo = jnp.pad(geo, ((0, 14), (0, DD - geo.shape[1])))
    message = pl.pallas_call(
        embed_kernel,
        out_shape=shape((PEERS * SPREAD, DD), BF16),
        scratch_shapes=[pltpu.VMEM((2 * TOK, DD), BF16)],
        compiler_params=params_for(24),
        name="embed",
    )(tokens, embed_weight, geo, spread_order())
    spread = lax.all_to_all(message, "dev", split_axis=0, concat_axis=0, tiled=True)

    graph = pair_graph[0].reshape(PEERS * REFS)
    first = (graph // 2) * SPREAD + (graph % 2) * ROWS
    where = (first[:, None] + jnp.arange(ROWS, dtype=jnp.int32)[None, :]).reshape(-1, 1)
    mine = lax.dynamic_slice_in_dim(graph, me * REFS, REFS)
    own = jnp.pad((mine // 2) * SPREAD + 2 * ROWS + mine % 2, (0, 8))[:, None]
    head_rows = jnp.pad(jnp.swapaxes(point_heads, 1, 2), ((0, 0), (0, 12), (0, 0)))
    outgoing, my_geo = pl.pallas_call(
        select_kernel,
        out_shape=(shape((PEERS * REFS * ROWS, DD), BF16), shape((REFS, 256), F32)),
        compiler_params=params_for(24),
        name="select",
    )(spread, where, own)
    rows = lax.all_to_all(outgoing, "dev", split_axis=0, concat_axis=0, tiled=True)

    half = pl.BlockSpec((2, DD, DD), lambda i: (0, 0, 0))
    other = pl.BlockSpec((2, DD, DD), lambda i: (0, 0, 1))

    def fixed(dims):
        return pl.BlockSpec(dims, lambda i: (0,) * len(dims))

    fold = pl.pallas_call(
        fold_kernel,
        grid=(1,),
        in_specs=[fixed((2, 16, DD)), half, other],
        out_specs=fixed((2, HEADS * 16, DD)),
        out_shape=shape((2, HEADS * 16, DD), BF16),
        compiler_params=params_for(32),
        cost_estimate=pl.CostEstimate(flops=2000000000, bytes_accessed=6000000, transcendentals=0),
        name="fold",
    )(head_rows, cross_out, cross_keyval)

    view_par = jnp.repeat(pair_params[0], 2, axis=0)
    points, grads = pl.pallas_call(
        decode_kernel,
        grid=(1,),
        in_specs=[
            fixed((PEERS * REFS * ROWS, DD)), fixed((384, 384)), half, half, fixed((2, HEADS * 16, DD)),
            fixed((2, 16, DD)), fixed((REFS, 256)), fixed((REFS, 13)),
        ],
        out_specs=(fixed((REFS, 4, TOK)), fixed((PEERS * REFS, 256))),
        out_shape=(shape((REFS, 4, TOK), F32), shape((PEERS * REFS, 256), F32)),
        scratch_shapes=[
            pltpu.VMEM((2, PAIRS * TOK, DD), BF16),
            pltpu.VMEM((2, PAIRS * TOK, DD), BF16),
            pltpu.VMEM((2, PAIRS * TOK, DD), BF16),
            pltpu.VMEM((2, PAIRS * TOK, DD), BF16),
            pltpu.VMEM((2, PAIRS, HEADS * 16, TOK), BF16),
            pltpu.VMEM((2, PAIRS, 8, TOK), F32),
            pltpu.VMEM((4, REFS, TOK), F32),
        ],
        compiler_params=params_for(48),
        name="decode",
    )(rows, gather_order(), cross_query, cross_keyval, fold, head_rows, my_geo, view_par)

    grads = lax.all_to_all(grads, "dev", split_axis=0, concat_axis=0, tiled=True)
    smem = pl.BlockSpec(memory_space=pltpu.SMEM)
    own_grad, square = pl.pallas_call(
        combine_kernel,
        in_specs=[smem, whole(), whole()],
        out_shape=(shape((16, 256), F32), shape((1, 128), F32)),
        name="combine",
    )(me.reshape(1), graph.reshape(1, -1), grads)
    squares = lax.all_gather(square, "grp", axis=0, tiled=True)
    count = lax.axis_size("grp") * PEERS * (2 * (TOK + 12) + 13 * PAIRS)
    new_depth, new_cameras, new_params = pl.pallas_call(
        functools.partial(update_kernel, float(count)),
        out_shape=(shape((2, TOK), F32), shape((2, 12), F32), shape((PAIRS, 13), F32)),
        name="update",
    )(squares, own_grad, depth_map[0], cameras[0], pair_params[0])
    return (
        points.reshape(1, PAIRS, 2, 4, TOK),
        new_depth[None],
        new_cameras[None],
        new_params[None],
    )


def solution(mesh):
    placed = (
        P("grp", "dev", None, None),
        P("grp", "dev"),
        P("grp", "dev", None),
        P("grp", "dev", None),
        P("grp", None, None),
        P("grp", "dev", None),
        P(),
        P(),
        P(),
        P(),
        P(),
    )
    return jax.shard_map(
        on_device,
        mesh=mesh,
        in_specs=placed,
        out_specs=(
            P("grp", "dev", None, None, None),
            P("grp", "dev", None),
            P("grp", "dev", None),
            P("grp", "dev", None),
        ),
        check_vma=False,
    )
```

time: 553 us -> 173 us (0.31)
  waiting for transfers between devices: 292 us -> 76 us
  blocking collectives: 79.4 us -> 14.2 us
  local copies, waits for them, and re-layouts: 57.1 us -> 13.2 us
  Pallas kernels: 0 us -> 39.6 us
  matrix products: 37.5 us -> 0 us
  other arithmetic: 33.2 us -> 0.97 us
  starting transfers between devices: 51 us -> 27.8 us
    all_to_all x5 -> x3, waiting for transfers between devices: 292 us -> 76 us  [the longest x1 48.6 us: on_device(): lax.all_to_all(outgoing, 'dev', split_axis=0, concat_axis=0, tiled=True)]
    psum x1 -> x0, blocking collectives: 79.4 us -> none  [on_device(): grad_total = lax.psum(local_square, ('grp', 'dev'))]
    pallas_call x0 -> x6, Pallas kernels: none -> 39.6 us  [the longest x1 29.4 us: on_device(): pl.pallas_call(decode_kernel, grid=(1,), in_specs=[fixed((PEERS * REFS *...]
    dot_general x13 -> x0, matrix products: 37.5 us -> none  [the longest x2 11.7 us: decode(): jnp.einsum('phqk,pkhd->pqhd', attn_probs, value_heads, preferred_element_...]
    reshape x8 -> x0, local copies, waits for them, and re-layouts: 26.9 us -> none  [the longest x2 9.42 us: decode(): query_heads = query_proj.reshape(pcount, tok_count, -1, HD)]
    all_to_all x5 -> x3, starting transfers between devices: 51 us -> 27.8 us  [the longest x1 12 us: on_device(): lax.all_to_all(message, 'dev', split_axis=0, concat_axis=0, tiled=True)]
    gather x8 -> x0, local copies, waits for them, and re-layouts: 17.7 us -> none  [the longest x4 9.58 us: select(): picked = jnp.take(table, local_idx, axis=0)]
    all_gather x0 -> x1, blocking collectives: none -> 14.2 us  [on_device(): squares = lax.all_gather(square, 'grp', axis=0, tiled=True)]
  transfers between devices with their start and end apart: 5 -> 3, of which waited for: 3 -> 3; matrix products, arithmetic and copies ran while one was open for 5% -> 1% of each run, Pallas kernels for 0% -> 1%
where the time goes in v1:
time: 173 us; the launch traced here: 172 us
  waiting for transfers between devices  76 us (44%)
  Pallas kernels  39.6 us (23%)
  starting transfers between devices  27.8 us (16%)
  blocking collectives  14.2 us (8%)
  local copies, waits for them, and re-layouts  13.2 us (8%)
    all_to_all x1, waiting for transfers between devices, on_device(): lax.all_to_all(outgoing, 'dev', split_axis=0, concat_axis=0, tiled=True)  48.6 us
    pallas_call x1, Pallas kernels, on_device(): pl.pallas_call(decode_kernel, grid=(1,), in_specs=[fixed((PEERS * REFS *...  29.4 us
    all_to_all x1, waiting for transfers between devices, on_device(): lax.all_to_all(message, 'dev', split_axis=0, concat_axis=0, tiled=True)  18.4 us
    all_gather x1, blocking collectives, on_device(): squares = lax.all_gather(square, 'grp', axis=0, tiled=True)  14.2 us
    all_to_all x1, starting transfers between devices, on_device(): lax.all_to_all(message, 'dev', split_axis=0, concat_axis=0, tiled=True)  12 us
    unnamed x25, local copies, waits for them, and re-layouts  11.2 us
    all_to_all x1, waiting for transfers between devices, on_device(): lax.all_to_all(grads, 'dev', split_axis=0, concat_axis=0, tiled=True)  8.96 us
    all_to_all x1, starting transfers between devices, on_device(): lax.all_to_all(outgoing, 'dev', split_axis=0, concat_axis=0, tiled=True)  8.48 us
  transfers between devices with their start and end apart: 3, of which 3 were waited for; matrix products, arithmetic and copies ran while one was open for 1% of the time, Pallas kernels for 1%

profile of v1, /device:TPU:1, one launch (start us, length us, event | category | flops | bytes accessed | tf_op | source)
XLA Modules:
  0.0 172.5 jit_solution(15946457630917660860)
XLA Ops:
  0.6 0.8 copy.27
  1.4 0.8 fusion.8.geo_ref
  2.2 0.0 copy-start.4
  2.2 1.4 copy-done.4
  3.6 0.0 copy-start.5
  3.6 1.1 copy-done.5
  4.7 0.0 copy-start.7
  4.7 0.8 copy-done.7
  5.5 0.0 copy-start.11
  5.5 2.3 %embed.1 = bf16[512,768]{1,0:T(8,128)(2,1)} custom-call(bf16[384,1024]{1,0:T(8,128)(2,1)S(1)} %bitcast.25, bf16[1024,768]{1,0:T(8,128)(2,1)S(1)} %copy-done.4, bf16[16,768]{1,0:T(8,128)(2,1)S(1)} %fusion.8.geo_ref, bf16[128,112]{1,0:T(8,128)(2,1)S(1)} %copy-done.7), custom_call_target="tpu_custom_call" | custom-call | tf_op jit(solution)/shard_map/embed/pallas_call | solution.py:270
  7.7 12.0 %all-to-all-start = ((bf16[32,16,768]{2,1,0:T(8,128)(2,1)}), bf16[32,16,768]{2,1,0:T(8,128)(2,1)S(1)}, u32[]{:S(2)}, u32[]{:S(2)}) async-start(bf16[32,16,768]{2,1,0:T(8,128)(2,1)} %bitcast.4), calls=%async_computation | async-start | bytes 1572864 | tf_op jit(solution)/shard_map/all_to_all | solution.py:277
  19.8 0.0 copy-done.11
  19.8 0.1 copy.28
  19.9 0.1 reshape_squeeze.7
  20.0 0.1 fusion.11
  20.1 0.1 copy.30.own_ref
  20.2 0.1 iota_add_fusion
  20.4 0.2 add.77.where_ref
  20.6 18.4 %all-to-all-done = bf16[32,16,768]{2,1,0:T(8,128)(2,1)S(1)} async-done(((bf16[32,16,768]{2,1,0:T(8,128)(2,1)}), bf16[32,16,768]{2,1,0:T(8,128)(2,1)S(1)}, u32[]{:S(2)}, u32[]{:S(2)}) %all-to-all-start) | async-done | bytes 786464 | tf_op jit(solution)/shard_map/all_to_all | solution.py:277
  39.0 3.1 %select.61 = (bf16[1536,768]{1,0:T(8,128)(2,1)S(1)}, f32[8,256]{1,0:T(8,128)S(1)}) custom-call(bf16[512,768]{1,0:T(8,128)(2,1)S(1)} %bitcast.23, s32[1536,1]{1,0:T(8,128)S(1)} %add.77.where_ref, s32[16,1]{1,0:T(8,128)S(1)} %copy.30.own_ref), custom_call_target="tpu_custom_call" | custom-call | tf_op jit(solution)/shard_map/select/pallas_call | solution.py:285
  42.1 0.0 copy-start.1
  42.1 1.4 copy-done.1
  43.6 0.0 copy-start.9
  43.6 8.5 %all-to-all-start.1 = ((bf16[32,48,768]{2,1,0:T(8,128)(2,1)}), bf16[32,48,768]{2,1,0:T(8,128)(2,1)S(1)}, u32[]{:S(2)}, u32[]{:S(2)}) async-start(bf16[32,48,768]{2,1,0:T(8,128)(2,1)} %bitcast.24), calls=%async_computation.1 | async-start | bytes 4718592 | tf_op jit(solution)/shard_map/all_to_all | solution.py:291
  52.1 0.0 copy-done.9
  52.1 0.0 copy-start
  52.1 2.3 %copy-done = bf16[2,768,1536]{2,1,0:T(8,128)(2,1)S(1)} copy-done((bf16[2,768,1536]{2,1,0:T(8,128)(2,1)S(1)}, bf16[2,768,1536]{2,1,0:T(8,128)(2,1)}, u32[]{:S(2)}) %copy-start) | copy-done | bytes 4718616
  54.4 0.0 copy-start.2
  54.4 1.7 copy-done.2
  56.1 0.0 copy-start.10
  56.1 0.0 copy-start.6
  56.1 1.5 fold.1.fold_ref
  57.6 48.6 %all-to-all-done.1 = bf16[32,48,768]{2,1,0:T(8,128)(2,1)S(1)} async-done(((bf16[32,48,768]{2,1,0:T(8,128)(2,1)}), bf16[32,48,768]{2,1,0:T(8,128)(2,1)S(1)}, u32[]{:S(2)}, u32[]{:S(2)}) %all-to-all-start.1) | async-done | bytes 2359328 | tf_op jit(solution)/shard_map/all_to_all | solution.py:291
  106.2 0.0 copy-done.10
  106.2 0.0 copy-done.6
  106.2 0.0 copy-start.3
  106.2 1.7 copy-done.3
  107.9 29.4 %decode.1 = (f32[8,4,192]{2,1,0:T(4,128)}, f32[256,256]{1,0:T(8,128)}) custom-call(bf16[1536,768]{1,0:T(8,128)(2,1)S(1)} %bitcast.22, bf16[384,384]{1,0:T(8,128)(2,1)S(1)} %copy-done.6, bf16[2,768,768]{2,1,0:T(8,128)(2,1)S(1)} %copy-done.3, bf16[2,768,1536]{2,1,0:T(8,128)(2,1)} %key_ref.1, bf16[2,192,768]{2,1,0:T(8,128)(2,1)S(1)} %fold.1.fold_ref, ...), custom_call_target="tpu_custom_call" | custom-call | tf_op jit(solution)/shard_map/decode/pallas_call | solution.py:311
  137.3 7.3 %all-to-all-start.2 = ((f32[32,8,256]{2,1,0:T(8,128)}), f32[32,8,256]{2,1,0:T(8,128)S(1)}, u32[]{:S(2)}, u32[]{:S(2)}) async-start(f32[32,8,256]{2,1,0:T(8,128)} %bitcast.14), calls=%async_computation.2 | async-start | bytes 524288 | tf_op jit(solution)/shard_map/all_to_all | solution.py:333
  144.5 0.7 reshape_reshape_squeeze.3.graph_ref
  145.2 9.0 %all-to-all-done.2 = f32[32,8,256]{2,1,0:T(8,128)S(1)} async-done(((f32[32,8,256]{2,1,0:T(8,128)}), f32[32,8,256]{2,1,0:T(8,128)S(1)}, u32[]{:S(2)}, u32[]{:S(2)}) %all-to-all-start.2) | async-done | bytes 262176 | tf_op jit(solution)/shard_map/all_to_all | solution.py:333
  154.2 0.0 copy-start.8
  154.2 0.7 copy-done.8
  154.9 1.9 %combine.1 = (f32[16,256]{1,0:T(8,128)}, f32[1,128]{1,0:T(1,128)}) custom-call(s32[1]{0:T(128)} %bitcast.13.me_ref, s32[1,256]{1,0:T(1,128)} %reshape_reshape_squeeze.3.graph_ref, f32[256,256]{1,0:T(8,128)} %bitcast.27), custom_call_target="tpu_custom_call" | custom-call | tf_op jit(solution)/shard_map/combine/pallas_call | solution.py:335
  156.8 14.2 %all-gather = f32[8,1,128]{2,1,0:T(1,128)} all-gather(f32[1,1,128]{2,1,0:T(1,128)} %bitcast.36), channel_id=1, replica_groups=mesh['grp'=8,'dev'=32] {'grp'}, dimensions={0}, use_global_device_ids=true | all-gather | bytes 4608 | tf_op jit(solution)/shard_map/all_gather | solution.py:341
  171.0 1.5 update.1
  (4 shorter events, 0.0 us)
Async XLA Ops:
  2.2 1.4 copy-start.4
  3.6 1.1 copy-start.5
  4.7 0.8 copy-start.7
  5.5 14.3 %copy-start.11 = (s32[1,128,2]{1,2,0:T(2,128)S(1)}, s32[1,128,2]{1,2,0:T(2,128)}, u32[]{:S(2)}) copy-start(s32[1,128,2]{1,2,0:T(2,128)} %param.17) | copy-start | bytes 3076
  7.7 31.3 %all-to-all-start = ((bf16[32,16,768]{2,1,0:T(8,128)(2,1)}), bf16[32,16,768]{2,1,0:T(8,128)(2,1)S(1)}, u32[]{:S(2)}, u32[]{:S(2)}) async-start(bf16[32,16,768]{2,1,0:T(8,128)(2,1)} %bitcast.4), calls=%async_computation | async-start | bytes 1572864 | tf_op jit(solution)/shard_map/all_to_all | solution.py:277
  42.1 1.4 copy-start.1
  43.6 8.5 %copy-start.9 = (bf16[2,768,4]{1,2,0:T(4,128)(2,1)S(1)}, bf16[2,768,4]{1,2,0:T(4,128)(2,1)}, u32[]{:S(2)}) copy-start(bf16[2,768,4]{1,2,0:T(4,128)(2,1)} %param.23) | copy-start | bytes 36868
  43.6 62.6 %all-to-all-start.1 = ((bf16[32,48,768]{2,1,0:T(8,128)(2,1)}), bf16[32,48,768]{2,1,0:T(8,128)(2,1)S(1)}, u32[]{:S(2)}, u32[]{:S(2)}) async-start(bf16[32,48,768]{2,1,0:T(8,128)(2,1)} %bitcast.24), calls=%async_computation.1 | async-start | bytes 4718592 | tf_op jit(solution)/shard_map/all_to_all | solution.py:291
  52.1 2.3 %copy-start = (bf16[2,768,1536]{2,1,0:T(8,128)(2,1)S(1)}, bf16[2,768,1536]{2,1,0:T(8,128)(2,1)}, u32[]{:S(2)}) copy-start(bf16[2,768,1536]{2,1,0:T(8,128)(2,1)} %key_ref.1) | copy-start | bytes 14155780
  54.4 1.7 copy-start.2
  56.1 50.1 %copy-start.10 = (f32[1,4,13]{2,1,0:T(4,128)S(1)}, f32[1,4,13]{2,1,0:T(4,128)}, u32[]{:S(2)}) copy-start(f32[1,4,13]{2,1,0:T(4,128)} %param.18) | copy-start | bytes 628
  56.1 50.1 %copy-start.6 = (bf16[384,384]{1,0:T(8,128)(2,1)S(1)}, bf16[384,384]{1,0:T(8,128)(2,1)}, u32[]{:S(2)}) copy-start(bf16[384,384]{1,0:T(8,128)(2,1)} %constant.66.clone.order_ref) | copy-start | bytes 884740
  106.2 1.7 copy-start.3
  137.3 16.9 %all-to-all-start.2 = ((f32[32,8,256]{2,1,0:T(8,128)}), f32[32,8,256]{2,1,0:T(8,128)S(1)}, u32[]{:S(2)}, u32[]{:S(2)}) async-start(f32[32,8,256]{2,1,0:T(8,128)} %bitcast.14), calls=%async_computation.2 | async-start | bytes 524288 | tf_op jit(solution)/shard_map/all_to_all | solution.py:333
  154.2 0.7 copy-start.8

commit v2 on v1

v2 whole, which is shorter than its diff:
```python
import functools
import math

import jax
import jax.numpy as jnp
from jax import lax
from jax.experimental import pallas as pl
from jax.experimental.pallas import tpu as pltpu
from jax.sharding import PartitionSpec as P

HEADS = 12
HD = 64
DD = 768
TOK = 192
GW = 16
PEERS = 32
REFS = 8
PAIRS = 4
SPLIT = (3, 1)
PIECE = 12
WIDE = 384
SLOTS = 32
LOW = 32

norm_eps = 1e-06
stat_eps = 1e-06
step_rate = 0.3

F32 = jnp.float32
BF16 = jnp.bfloat16
NT = (((1,), (1,)), ((), ()))
MIB = 1024 * 1024


def params_for(mib):
    return pltpu.CompilerParams(vmem_limit_bytes=mib * MIB)


def dot(left, right):
    return jnp.dot(left, right, preferred_element_type=F32)


def dot_nt(left, right):
    return lax.dot_general(left, right, NT, preferred_element_type=F32)


def one_hot(pick):
    return jnp.where(pick, 1.0, 0.0).astype(BF16)


def spread_order():
    row = lax.broadcasted_iota(jnp.int32, (8 * SLOTS, 208), 0)
    slot = row & (SLOTS - 1)
    first = (row >> 5) * PIECE + slot
    source = jnp.where(slot < PIECE, first, first + (96 - PIECE))
    source = jnp.where(slot < 2 * PIECE, source, slot + (192 - 2 * PIECE))
    source = jnp.where(slot < 2 * PIECE + 2, source, -1)
    return one_hot(source == lax.broadcasted_iota(jnp.int32, (8 * SLOTS, 208), 1))


def gather_order(images):
    size = 8 * images * PIECE
    row = lax.broadcasted_iota(jnp.int32, (size, size), 0)
    image = (row * 683) >> 16
    rest = row - image * 96
    source = (rest * 43) >> 9
    came = source * (images * PIECE) + image * PIECE + rest - source * PIECE
    return one_hot(came == lax.broadcasted_iota(jnp.int32, (size, size), 1))


def embed_kernel(tokens_hbm, weight_hbm, depth_hbm, camera_hbm, focal_hbm, out_ref,
                 tokens_ref, weight_ref, depth_ref, camera_ref, focal_ref, emb_ref, sems):
    depth_of = weight_hbm.shape[0] // 2
    parts = [pl.ds(0, depth_of), pl.ds(depth_of, depth_of)]
    copies = [
        pltpu.make_async_copy(depth_hbm, depth_ref, sems.at[0]),
        pltpu.make_async_copy(camera_hbm, camera_ref, sems.at[1]),
        pltpu.make_async_copy(focal_hbm, focal_ref, sems.at[2]),
        pltpu.make_async_copy(tokens_hbm, tokens_ref, sems.at[3]),
    ]
    copies += [
        pltpu.make_async_copy(weight_hbm.at[part], weight_ref.at[part], sems.at[4 + i])
        for i, part in enumerate(parts)
    ]
    for copy in copies:
        copy.start()
    order = spread_order()
    for copy in copies[:3]:
        copy.wait()
    blank = jnp.zeros((2, WIDE - TOK), F32)
    geo = jnp.concatenate([depth_ref[...].astype(F32), blank], axis=1)
    lane = lax.broadcasted_iota(jnp.int32, (2, WIDE), 1)
    camera = camera_ref[...].astype(F32)
    focal = focal_ref[...].astype(F32)
    upper = lax.broadcasted_iota(jnp.int32, (2, WIDE), 0) == 0
    for i in range(12):
        geo = jnp.where(lane == TOK + i, camera[:, i : i + 1], geo)
    geo = jnp.where(lane == TOK + 12, jnp.where(upper, focal[:, 0:1], focal[:, 1:2]), geo)
    geo = jnp.concatenate([geo, jnp.zeros((14, WIDE), F32)], axis=0).astype(BF16)
    copies[3].wait()
    copies[4].wait()
    first = dot(tokens_ref[:, 0:depth_of], weight_ref[0:depth_of])
    copies[5].wait()
    emb_ref[...] = (first + dot(tokens_ref[:, depth_of:], weight_ref[depth_of:])).astype(BF16)
    for part in range(4):
        cols = slice((part // 2) * WIDE, (part // 2 + 1) * WIDE)
        at = (part % 2) * 96
        rows = jnp.concatenate(
            [emb_ref[at : at + 96, cols], emb_ref[TOK + at : TOK + at + 96, cols], geo], axis=0
        )
        out_ref[part * 8 * SLOTS : (part + 1) * 8 * SLOTS] = dot(order, rows).astype(BF16)


def select_kernel(with_geo, rows_ref, where_ref, own_ref, after_ref, *rest):
    if with_geo:
        out_hbm, geo_ref, out_ref, sems = rest
    else:
        out_hbm, out_ref, sems = rest
    total = rows_ref.shape[0]
    lane = lax.broadcasted_iota(jnp.int32, (TOK, total), 1)
    copies = []
    for step in range(out_ref.shape[0] // TOK):
        at = pl.ds(step * TOK, TOK)
        pick = one_hot(where_ref[at, :][:, :1] == lane)
        out_ref[at, :] = dot(pick, rows_ref[...]).astype(BF16)
        copies.append(pltpu.make_async_copy(out_ref.at[at], out_hbm.at[at], sems.at[step]))
        copies[-1].start()
    if with_geo:
        own_lane = lax.broadcasted_iota(jnp.int32, (16, total), 1)
        own = one_hot(own_ref[...][:, :1] == own_lane)
        geo_ref[...] = dot(own, rows_ref[:, 0:256])[0:REFS]
    for copy in copies:
        copy.wait()


def fold_kernel(head_ref, out_hbm, value_hbm, fold_ref, out_ref, value_ref, sems):
    copies = []
    for view in range(2):
        copies.append(pltpu.make_async_copy(out_hbm.at[view], out_ref.at[view], sems.at[2 * view]))
        copies.append(
            pltpu.make_async_copy(value_hbm.at[view, :, pl.ds(DD, DD)], value_ref.at[view], sems.at[2 * view + 1])
        )
    for copy in copies:
        copy.start()
    lane = lax.broadcasted_iota(jnp.int32, (16, DD), 1)
    for view in range(2):
        copies[2 * view].wait()
        both = dot_nt(head_ref[view], out_ref[view])
        high = both.astype(BF16).astype(F32)
        low = (both - high).astype(BF16).astype(F32)
        pair = jnp.concatenate([high[0:8], low[0:8]], axis=0)
        left = jnp.concatenate(
            [jnp.where(lane // HD == head, pair, 0.0).astype(BF16) for head in range(HEADS)], axis=0
        )
        copies[2 * view + 1].wait()
        full = dot_nt(left, value_ref[view])
        for head in range(HEADS):
            term = full[head * 16 : head * 16 + 8] + full[head * 16 + 8 : head * 16 + 16]
            top = term.astype(BF16).astype(F32)
            rest = term - top
            fold_ref[view, head * 16 : head * 16 + 16] = jnp.concatenate([top, rest], axis=0).astype(BF16)


def view_gradients(outs, geo, par):
    token = lax.broadcasted_iota(jnp.int32, (REFS, TOK), 1)
    column = (token & (GW - 1)).astype(F32) - (GW - 1) / 2.0
    row_pos = (token >> 4).astype(F32) - (TOK // GW - 1) / 2.0
    depth = geo[:, 0:TOK]
    cam = [geo[:, TOK + i : TOK + i + 1] for i in range(12)]
    focal = geo[:, TOK + 12 : TOK + 13]
    ray = [column / focal, row_pos / focal, jnp.ones_like(column)]
    cam_points = [depth * ray[0], depth * ray[1], depth]
    scale = par[:, 0:1]
    mat = [par[:, 1 + i : 2 + i] for i in range(9)]
    shift = [par[:, 10 + i : 11 + i] for i in range(3)]
    points = outs[:3]
    confidence = outs[3]
    fitted, weighted, ray_image = [], [], []
    for r in range(3):
        world = cam[3 * r] * cam_points[0] + cam[3 * r + 1] * cam_points[1] + cam[3 * r + 2] * cam_points[2]
        world = world + cam[9 + r]
        fit = mat[3 * r] * points[0] + mat[3 * r + 1] * points[1] + mat[3 * r + 2] * points[2] + shift[r]
        fitted.append(fit)
        weighted.append((2.0 * confidence) * (world - scale * fit))
        ray_image.append(cam[3 * r] * ray[0] + cam[3 * r + 1] * ray[1] + cam[3 * r + 2])
    grad_depth = weighted[0] * ray_image[0] + weighted[1] * ray_image[1] + weighted[2] * ray_image[2]

    def total(x):
        return jnp.sum(x, axis=1, keepdims=True)

    sums = [total(w) for w in weighted]
    entries = [total(weighted[r] * cam_points[c]) for r in range(3) for c in range(3)] + sums
    entries.append(-total(weighted[0] * fitted[0] + weighted[1] * fitted[1] + weighted[2] * fitted[2]))
    entries += [-scale * total(weighted[r] * points[c]) for r in range(3) for c in range(3)]
    entries += [-scale * s for s in sums]
    lane = lax.broadcasted_iota(jnp.int32, (REFS, 64), 1)
    tail = jnp.zeros((REFS, 64), F32)
    for i, entry in enumerate(entries):
        high = entry.astype(BF16).astype(F32)
        tail = jnp.where(lane == i, high, jnp.where(lane == LOW + i, entry - high, tail))
    return grad_depth, tail


def decode_kernel(last, pairs, rows_ref, query_hbm, key_hbm, fold_ref, head_ref, *rest):
    if last:
        geo_ref, par_ref, past_ref, points_ref, grad_ref, o_ref, *rest = rest
    else:
        o_ref, *rest = rest
    query_ref, key_ref, x_ref, n_ref, q_ref, k_ref, u_ref, e_ref, sems = rest
    copies = []
    for view in range(2):
        copies.append(pltpu.make_async_copy(query_hbm.at[view], query_ref.at[view], sems.at[2 * view]))
        copies.append(
            pltpu.make_async_copy(key_hbm.at[view, :, pl.ds(0, DD)], key_ref.at[view], sems.at[2 * view + 1])
        )
    for copy in copies:
        copy.start()
    order = gather_order(2 * pairs)
    size = 8 * 2 * pairs * PIECE
    for part in range(4):
        mixed = dot(order, rows_ref[part * size : (part + 1) * size]).astype(BF16)
        cols = slice((part // 2) * WIDE, (part // 2 + 1) * WIDE)
        for image in range(2 * pairs):
            at = (image // 2) * TOK + (part % 2) * 96
            x_ref[image % 2, at : at + 96, cols] = mixed[image * 96 : image * 96 + 96]

    for slot in range(2):
        for pair in range(pairs):
            at = pl.ds(pair * TOK, TOK)
            wide = x_ref[slot, at, :].astype(F32)
            centred = wide - jnp.mean(wide, axis=-1, keepdims=True)
            spread = jnp.mean(centred * centred, axis=-1, keepdims=True)
            n_ref[slot, at, :] = (centred * lax.rsqrt(spread + norm_eps)).astype(BF16)

    ones_row = jnp.where(lax.broadcasted_iota(jnp.int32, (8, TOK), 0) == 4, 1.0, 0.0)
    for view in range(2):
        copies[2 * view].wait()
        q_ref[view] = dot(n_ref[view], query_ref[view]).astype(BF16)
        copies[2 * view + 1].wait()
        k_ref[view] = dot(n_ref[1 - view], key_ref[view]).astype(BF16)
        for pair in range(pairs):
            at = pl.ds(pair * TOK, TOK)
            value = dot_nt(fold_ref[view], n_ref[1 - view, at, :])
            for head in range(HEADS):
                term = value[head * 16 : head * 16 + 8] + value[head * 16 + 8 : head * 16 + 16] + ones_row
                u_ref[view, pair, head * 16 : head * 16 + 16] = jnp.concatenate(
                    [term, jnp.zeros_like(term)], axis=0
                ).astype(BF16)
            e_ref[view, pair] = dot_nt(head_ref[view], x_ref[view, at, :])[0:8]

    upper = lax.broadcasted_iota(jnp.int32, (TOK, 2 * HD), 1) >= HD
    factor = math.log2(math.e) / math.sqrt(HD)
    for view in range(2):
        @pl.loop(0, pairs)
        def _(pair):
            at = pl.ds(pl.multiple_of(pair * TOK, TOK), TOK)
            acc = e_ref[view, pair]
            for two in range(HEADS // 2):
                cols = slice(two * 2 * HD, (two + 1) * 2 * HD)
                keys = k_ref[view, at, cols]
                queries = q_ref[view, at, cols]
                for half in range(2):
                    head = 2 * two + half
                    part = jnp.where(upper if half else jnp.logical_not(upper), queries, jnp.zeros_like(queries))
                    scores = dot_nt(keys, part)
                    top = jnp.max(scores, axis=0, keepdims=True)
                    probs = jnp.exp2((scores - top) * factor).astype(BF16)
                    mixed = dot(u_ref[view, pair, head * 16 : head * 16 + 16], probs)[0:8]
                    acc = acc + mixed * (1.0 / mixed[4:5])
            sub = lax.broadcasted_iota(jnp.int32, (8, TOK), 0)
            acc = jnp.where(sub == 3, 1.0 + jnp.exp(acc), acc)
            for c in range(4):
                o_ref[c, pl.ds(2 * pair + view, 1), :] = acc[c : c + 1]

    if last:
        outs = [jnp.concatenate([past_ref[c], o_ref[c]], axis=0) for c in range(4)]
        for c in range(4):
            for view in range(REFS):
                points_ref[view, c : c + 1] = outs[c][view : view + 1]
        grad_depth, tail = view_gradients(outs, geo_ref[...], par_ref[...])
        both = jnp.concatenate([grad_depth, tail], axis=1)
        twice = jnp.concatenate([both, both], axis=0).astype(BF16)
        for peer in range(0, PEERS, 2):
            grad_ref[peer * REFS : (peer + 2) * REFS] = twice


def combine_kernel(me_ref, graph_ref, grad_ref, own_ref, square_ref):
    refs = PEERS * REFS
    me = me_ref[0]
    graph = graph_ref[...]
    grads = grad_ref[...]

    def summed(pick):
        sums = dot(jnp.where(pick, 1.0, 0.0).astype(BF16), grads)
        lane = lax.broadcasted_iota(jnp.int32, sums.shape, 1)
        return jnp.where(lane < TOK, sums, sums + pltpu.roll(sums, 256 - LOW, 1)), lane

    image = lax.broadcasted_iota(jnp.int32, (2 * PEERS, refs), 0)
    image_sum, image_lane = summed(graph == image)
    pair = lax.broadcasted_iota(jnp.int32, (refs // 2, refs), 0)
    view = lax.broadcasted_iota(jnp.int32, (refs // 2, refs), 1)
    pair_sum, pair_lane = summed((view >> 1) == pair)
    image_sq = jnp.where(image_lane < TOK + 12, image_sum * image_sum, 0.0)
    pair_sq = jnp.where((pair_lane >= TOK + 12) & (pair_lane < TOK + 25), pair_sum * pair_sum, 0.0)
    square_ref[...] = jnp.full(square_ref.shape, jnp.sum(image_sq) + jnp.sum(pair_sq), F32)
    row = lax.broadcasted_iota(jnp.int32, (16, refs), 0)
    ref = lax.broadcasted_iota(jnp.int32, (16, refs), 1)
    own_image = (row < 2) & (graph == 2 * me + row)
    own_pair = (row >= 8) & (row < 8 + PAIRS) & ((ref >> 1) == PAIRS * me + row - 8)
    own_ref[...] = summed(own_image | own_pair)[0]


def update_kernel(count, square_ref, own_ref, depth_ref, camera_ref, par_ref, depth_out, camera_out, par_out):
    total = jnp.sum(square_ref[...], axis=0, keepdims=True)[:, 0:1]
    step = step_rate / jnp.sqrt(total / count + stat_eps)
    depth_out[...] = depth_ref[...].astype(F32) - step * own_ref[0:2, 0:TOK]
    camera_out[...] = camera_ref[...].astype(F32) - step * own_ref[0:2, TOK : TOK + 12]
    par_out[...] = par_ref[...] - step * own_ref[8 : 8 + PAIRS, TOK + 12 : TOK + 25]


def shape(dims, kind):
    return jax.ShapeDtypeStruct(dims, kind)


def hbm(x):
    return pltpu.with_memory_space_constraint(x, pltpu.HBM)


def on_device(
    enc_tokens, focal_len, depth_map, cameras, pair_graph, pair_params,
    embed_weight, cross_query, cross_keyval, cross_out, point_heads,
):
    me = lax.axis_index("dev")
    groups = lax.axis_size("grp")
    inside = pl.BlockSpec(memory_space=pltpu.VMEM)
    outside = pl.BlockSpec(memory_space=pltpu.HBM)
    scalar = pl.BlockSpec(memory_space=pltpu.SMEM)

    def exchange(x, axis):
        return lax.all_to_all(x, axis, split_axis=0, concat_axis=0, tiled=True)

    tokens = enc_tokens[0].reshape(2 * TOK, -1)
    message = pl.pallas_call(
        embed_kernel,
        in_specs=[outside] * 5,
        out_specs=inside,
        out_shape=shape((PEERS * SLOTS, WIDE), BF16),
        scratch_shapes=[
            pltpu.VMEM(tokens.shape, BF16),
            pltpu.VMEM(embed_weight.shape, BF16),
            pltpu.VMEM((2, TOK), BF16),
            pltpu.VMEM((2, 12), BF16),
            pltpu.VMEM((1, 2), BF16),
            pltpu.VMEM((2 * TOK, DD), BF16),
            pltpu.SemaphoreType.DMA((6,)),
        ],
        compiler_params=params_for(24),
        name="embed",
    )(hbm(tokens), hbm(embed_weight), hbm(depth_map[0]), hbm(cameras[0]), hbm(focal_len))
    spread = exchange(message, "dev")

    head_rows = jnp.pad(jnp.swapaxes(point_heads, 1, 2), ((0, 0), (0, 12), (0, 0)))
    fold = pl.pallas_call(
        fold_kernel,
        in_specs=[inside, outside, outside],
        out_specs=inside,
        out_shape=shape((2, HEADS * 16, DD), BF16),
        scratch_shapes=[
            pltpu.VMEM((2, DD, DD), BF16),
            pltpu.VMEM((2, DD, DD), BF16),
            pltpu.SemaphoreType.DMA((4,)),
        ],
        compiler_params=params_for(20),
        cost_estimate=pl.CostEstimate(flops=2000000000, bytes_accessed=6000000, transcendentals=0),
        name="fold",
    )(head_rows, hbm(cross_out), hbm(cross_keyval))

    graph = pair_graph[0].reshape(PEERS * REFS)
    first = (graph // 2) * SLOTS + (graph % 2) * PIECE
    where = first.reshape(PEERS, REFS, 1) + jnp.arange(PIECE, dtype=jnp.int32)
    mine = lax.dynamic_slice_in_dim(graph, me * REFS, REFS)
    own = jnp.pad((mine // 2) * SLOTS + 2 * PIECE + mine % 2, (0, 8))[:, None]
    rows = []
    done = 0
    for pairs in SPLIT:
        count = PEERS * 2 * pairs * PIECE
        last = done + pairs == PAIRS
        moved = shape((count, WIDE), BF16)
        outgoing = pl.pallas_call(
            functools.partial(select_kernel, last),
            in_specs=[inside] * 3 + [pl.BlockSpec(memory_space=pl.ANY)],
            out_specs=(outside, inside) if last else outside,
            out_shape=(moved, shape((REFS, 256), F32)) if last else moved,
            scratch_shapes=[pltpu.VMEM((count, WIDE), BF16), pltpu.SemaphoreType.DMA((count // TOK,))],
            compiler_params=params_for(20),
            cost_estimate=pl.CostEstimate(flops=count * 800000, bytes_accessed=4 * count * WIDE, transcendentals=0),
            name="select",
        )(spread, where[:, 2 * done : 2 * (done + pairs)].reshape(count, 1), own, fold)
        if last:
            outgoing, my_geo = outgoing
        rows.append(exchange(outgoing, "dev"))
        done += pairs

    view_par = jnp.repeat(pair_params[0], 2, axis=0)
    for part, pairs in enumerate(SPLIT):
        last = part == len(SPLIT) - 1
        weights = pltpu.VMEM((2, DD, DD), BF16)
        tokens_of = pltpu.VMEM((2, pairs * TOK, DD), BF16)
        scratch = [weights] * 2 + [tokens_of] * 4
        scratch += [pltpu.VMEM((2, pairs, HEADS * 16, TOK), BF16), pltpu.VMEM((2, pairs, 8, TOK), F32)]
        scratch.append(pltpu.SemaphoreType.DMA((4,)))
        if last:
            extra = (my_geo, view_par, past)
            outs = (shape((REFS, 4, TOK), F32), shape((PEERS * REFS, 256), BF16))
            scratch = [pltpu.VMEM((4, 2 * pairs, TOK), F32)] + scratch
        else:
            extra = ()
            outs = (shape((4, 2 * pairs, TOK), F32),)
        past = pl.pallas_call(
            functools.partial(decode_kernel, last, pairs),
            in_specs=[inside] + [outside] * 2 + [inside] * (2 + len(extra)),
            out_specs=(inside,) * len(outs),
            out_shape=outs,
            scratch_shapes=scratch,
            compiler_params=params_for(28),
            cost_estimate=pl.CostEstimate(flops=4000000000 * pairs, bytes_accessed=8000000, transcendentals=0),
            name="decode",
        )(rows[part], hbm(cross_query), hbm(cross_keyval), fold, head_rows, *extra)
        past = past if last else past[0]
    points, grads = past

    own_grad, square = pl.pallas_call(
        combine_kernel,
        in_specs=[scalar, inside, inside],
        out_shape=(shape((16, 256), F32), shape((groups, 128), F32)),
        compiler_params=params_for(16),
        name="combine",
    )(me.reshape(1), graph.reshape(1, -1), exchange(grads, "dev"))
    total = groups * PEERS * (2 * (TOK + 12) + 13 * PAIRS)
    new_depth, new_cameras, new_params = pl.pallas_call(
        functools.partial(update_kernel, float(total)),
        out_shape=(shape((2, TOK), F32), shape((2, 12), F32), shape((PAIRS, 13), F32)),
        compiler_params=params_for(16),
        name="update",
    )(exchange(square, "grp"), own_grad, depth_map[0], cameras[0], pair_params[0])
    return (
        points.reshape(1, PAIRS, 2, 4, TOK),
        new_depth[None],
        new_cameras[None],
        new_params[None],
    )


def solution(mesh):
    placed = (
        P("grp", "dev", None, None),
        P("grp", "dev"),
        P("grp", "dev", None),
        P("grp", "dev", None),
        P("grp", None, None),
        P("grp", "dev", None),
        P(),
        P(),
        P(),
        P(),
        P(),
    )
    return jax.shard_map(
        on_device,
        mesh=mesh,
        in_specs=placed,
        out_specs=(
            P("grp", "dev", None, None, None),
            P("grp", "dev", None),
            P("grp", "dev", None),
            P("grp", "dev", None),
        ),
        check_vma=False,
    )
```

time: 173 us -> 159 us (0.919)
  waiting for transfers between devices: 76 us -> 61.4 us
  local copies, waits for them, and re-layouts: 13.2 us -> 3.39 us
  starting transfers between devices: 27.8 us -> 37 us
  Pallas kernels: 39.6 us -> 43.9 us
  blocking collectives: 14.2 us -> 11.9 us
    all_to_all x3 -> x4, waiting for transfers between devices: 76 us -> 61.4 us  [exchange(): return lax.all_to_all(x, axis, split_axis=0, concat_axis=0, tiled=True)]
    all_gather x1 -> x0, blocking collectives: 14.2 us -> none  [on_device(): squares = lax.all_gather(square, 'grp', axis=0, tiled=True)]
    all_to_all x0 -> x1, blocking collectives: none -> 11.9 us  [exchange(): return lax.all_to_all(x, axis, split_axis=0, concat_axis=0, tiled=True)]
    unnamed x25 -> x19, local copies, waits for them, and re-layouts: 11.2 us -> 1.03 us
    all_to_all x3 -> x4, starting transfers between devices: 27.8 us -> 37 us  [exchange(): return lax.all_to_all(x, axis, split_axis=0, concat_axis=0, tiled=True)]
    pallas_call x6 -> x8, Pallas kernels: 39.6 us -> 43.9 us  [the longest x2 29.9 us: on_device(): pl.pallas_call(functools.partial(decode_kernel, last, pairs), in_specs=[i...]
  transfers between devices with their start and end apart: 3 -> 4, of which waited for: 3 -> 3; matrix products, arithmetic and copies ran while one was open for 1% -> 2% of each run, Pallas kernels for 1% -> 17%
where the time goes in v2:
time: 159 us
  waiting for transfers between devices  61.4 us (39%)
  Pallas kernels  43.9 us (28%)
  starting transfers between devices  37 us (23%)
  blocking collectives  11.9 us (7%)
  local copies, waits for them, and re-layouts  3.39 us (2%)
    all_to_all x4, waiting for transfers between devices, exchange(): return lax.all_to_all(x, axis, split_axis=0, concat_axis=0, tiled=True)  61.4 us
    all_to_all x4, starting transfers between devices, exchange(): return lax.all_to_all(x, axis, split_axis=0, concat_axis=0, tiled=True)  37 us
    pallas_call x2, Pallas kernels, on_device(): pl.pallas_call(functools.partial(decode_kernel, last, pairs), in_specs=[i...  29.9 us
    all_to_all x1, blocking collectives, exchange(): return lax.all_to_all(x, axis, split_axis=0, concat_axis=0, tiled=True)  11.9 us
    pallas_call x2, Pallas kernels, on_device(): pl.pallas_call(functools.partial(select_kernel, last), in_specs=[inside]...  5.31 us
    pallas_call x1, Pallas kernels, on_device(): pl.pallas_call(embed_kernel, in_specs=[outside] * 5, out_specs=inside, ou...  3.98 us
    pallas_call x1, Pallas kernels, on_device(): pl.pallas_call(fold_kernel, in_specs=[inside, outside, outside], out_spec...  3.63 us
  transfers between devices with their start and end apart: 4, of which 3 were waited for; matrix products, arithmetic and copies ran while one was open for 2% of the time, Pallas kernels for 17%

profile of v2, /device:TPU:1, one launch (start us, length us, event | category | flops | bytes accessed | tf_op | source)
XLA Modules:
  0.0 158.7 jit_solution(13369788641810426215)
XLA Ops:
  0.6 0.0 copy-start.8
  0.6 4.0 %embed.1 = bf16[1024,384]{1,0:T(8,128)(2,1)} custom-call(bf16[384,1024]{1,0:T(8,128)(2,1)} %bitcast.40, bf16[1024,768]{1,0:T(8,128)(2,1)} %weight_hbm.1, bf16[2,192]{1,0:T(2,128)(2,1)} %bitcast.34, bf16[2,12]{1,0:T(2,128)(2,1)} %bitcast.38, bf16[1,2]{1,0:T(2,128)(2,1)} %focal_hbm.1), custom_call_target="tpu_custom_call" | custom-call | tf_op jit(solution)/shard_map/embed/pallas_call | solution.py:343
  4.6 0.0 copy-start.7
  4.6 12.0 %all-to-all-start = ((bf16[32,32,384]{2,1,0:T(8,128)(2,1)}), bf16[32,32,384]{2,1,0:T(8,128)(2,1)S(1)}, u32[]{:S(2)}, u32[]{:S(2)}) async-start(bf16[32,32,384]{2,1,0:T(8,128)(2,1)} %bitcast.3), calls=%async_computation | async-start | bytes 1572864 | tf_op jit(solution)/shard_map/all_to_all | solution.py:340
  16.7 0.0 copy-done.8
  16.7 0.1 copy.25
  16.8 0.0 copy-start.5
  16.8 0.1 reshape_squeeze.10
  17.0 0.1 reshape_squeeze.9
  17.0 0.1 fusion.7
  17.1 0.1 copy.28.own_ref
  17.3 0.1 iota_add_fusion
  17.4 0.1 copy-done.5
  17.4 0.3 reshape.91.where_ref
  17.8 0.0 copy-done.7
  17.8 0.0 copy-start
  17.8 3.6 %fold.1.after_ref.fold_ref = bf16[2,192,768]{2,1,0:T(8,128)(2,1)S(1)} custom-call(bf16[2,16,768]{2,1,0:T(8,128)(2,1)S(1)} %pad.9.head_ref, bf16[2,768,768]{2,1,0:T(8,128)(2,1)} %out_hbm.1, bf16[2,768,1536]{2,1,0:T(8,128)(2,1)} %key_hbm.3), custom_call_target="tpu_custom_call" | custom-call | flops 2000000000 | bytes 6000000 | tf_op jit(solution)/shard_map/fold/pallas_call | solution.py:363
  21.5 0.0 copy-done
  21.5 14.5 %all-to-all-done = bf16[32,32,384]{2,1,0:T(8,128)(2,1)S(1)} async-done(((bf16[32,32,384]{2,1,0:T(8,128)(2,1)}), bf16[32,32,384]{2,1,0:T(8,128)(2,1)S(1)}, u32[]{:S(2)}, u32[]{:S(2)}) %all-to-all-start) | async-done | bytes 786464 | tf_op jit(solution)/shard_map/all_to_all | solution.py:340
  36.0 3.5 %select.36 = bf16[2304,384]{1,0:T(8,128)(2,1)} custom-call(bf16[1024,384]{1,0:T(8,128)(2,1)S(1)} %bitcast.27, s32[2304,1]{1,0:T(8,128)S(1)} %reshape.91.where_ref, s32[16,1]{1,0:T(8,128)S(1)} %copy.28.own_ref, bf16[2,192,768]{2,1,0:T(8,128)(2,1)S(1)} %fold.1.after_ref.fold_ref), custom_call_target="tpu_custom_call" | custom-call | flops 1843200000 | bytes 3538944 | tf_op jit(solution)/shard_map/select/pallas_call | solution.py:389
  39.4 8.4 %all-to-all-start.2 = ((bf16[32,72,384]{2,1,0:T(8,128)(2,1)}), bf16[32,72,384]{2,1,0:T(8,128)(2,1)S(1)}, u32[]{:S(2)}, u32[]{:S(2)}) async-start(bf16[32,72,384]{2,1,0:T(8,128)(2,1)} %bitcast.11), calls=%async_computation.2 | async-start | bytes 3538944 | tf_op jit(solution)/shard_map/all_to_all | solution.py:340
  47.8 0.6 slice.8
  48.4 0.9 reshape.90.where_ref
  49.4 1.9 %select.35 = (bf16[768,384]{1,0:T(8,128)(2,1)}, f32[8,256]{1,0:T(8,128)S(1)}) custom-call(bf16[1024,384]{1,0:T(8,128)(2,1)S(1)} %bitcast.28, s32[768,1]{1,0:T(8,128)S(1)} %reshape.90.where_ref, s32[16,1]{1,0:T(8,128)S(1)} %copy.28.own_ref, bf16[2,192,768]{2,1,0:T(8,128)(2,1)S(1)} %fold.1.after_ref.fold_ref), custom_call_target="tpu_custom_call" | custom-call | flops 614400000 | bytes 1179648 | tf_op jit(solution)/shard_map/select/pallas_call | solution.py:389
  51.2 37.9 %all-to-all-done.2 = bf16[32,72,384]{2,1,0:T(8,128)(2,1)S(1)} async-done(((bf16[32,72,384]{2,1,0:T(8,128)(2,1)}), bf16[32,72,384]{2,1,0:T(8,128)(2,1)S(1)}, u32[]{:S(2)}, u32[]{:S(2)}) %all-to-all-start.2) | async-done | bytes 1769504 | tf_op jit(solution)/shard_map/all_to_all | solution.py:340
  89.1 7.5 %all-to-all-start.1 = ((bf16[32,24,384]{2,1,0:T(8,128)(2,1)}), bf16[32,24,384]{2,1,0:T(8,128)(2,1)S(1)}, u32[]{:S(2)}, u32[]{:S(2)}) async-start(bf16[32,24,384]{2,1,0:T(8,128)(2,1)} %bitcast.7), calls=%async_computation.1 | async-start | bytes 1179648 | tf_op jit(solution)/shard_map/all_to_all | solution.py:340
  96.6 0.0 copy-start.1
  96.6 0.8 copy-done.1
  97.4 0.0 copy-start.2
  97.4 21.5 %decode.2.rest_2_ = f32[4,6,192]{2,1,0:T(8,128)S(1)} custom-call(bf16[2304,384]{1,0:T(8,128)(2,1)S(1)} %bitcast.26, bf16[2,768,768]{2,1,0:T(8,128)(2,1)} %query_hbm.3, bf16[2,768,1536]{2,1,0:T(8,128)(2,1)} %key_hbm.3, bf16[2,192,768]{2,1,0:T(8,128)(2,1)S(1)} %fold.1.after_ref.fold_ref, bf16[2,16,768]{2,1,0:T(8,128)(2,1)S(1)} %copy-done.1), custom_call_target="tpu_custom_call" | custom-call | flops 12000000000 | bytes 8000000 | tf_op jit(solution)/shard_map/decode/pallas_call | solution.py:419
  119.0 0.0 all-to-all-done.1
  119.0 0.0 copy-done.2
  119.0 0.0 copy-start.6
  119.0 0.0 copy-start.3
  119.0 0.0 copy-start.4
  119.0 8.3 %decode.3 = (f32[8,4,192]{2,1,0:T(4,128)}, bf16[256,256]{1,0:T(8,128)(2,1)}) custom-call(bf16[768,384]{1,0:T(8,128)(2,1)S(1)} %bitcast.29, bf16[2,768,768]{2,1,0:T(8,128)(2,1)} %query_hbm.3, bf16[2,768,1536]{2,1,0:T(8,128)(2,1)} %key_hbm.3, bf16[2,192,768]{2,1,0:T(8,128)(2,1)S(1)} %fold.1.after_ref.fold_ref, bf16[2,16,768]{2,1,0:T(8,128)(2,1)S(1)} %copy-done.1, ...), custom_call_target="tpu_custom_call" | custom-call | flops 4000000000 | bytes 8000000 | tf_op jit(solution)/shard_map/decode/pallas_call | solution.py:419
  127.4 9.1 %all-to-all-start.3 = ((bf16[32,8,256]{2,1,0:T(8,128)(2,1)}), bf16[32,8,256]{2,1,0:T(8,128)(2,1)S(1)}, u32[]{:S(2)}, u32[]{:S(2)}) async-start(bf16[32,8,256]{2,1,0:T(8,128)(2,1)} %bitcast.15), calls=%async_computation.3 | async-start | bytes 262144 | tf_op jit(solution)/shard_map/all_to_all | solution.py:340
  136.5 0.0 copy-done.6
  136.5 0.1 reshape_reshape_squeeze.3.graph_ref
  136.6 9.0 %all-to-all-done.3 = bf16[32,8,256]{2,1,0:T(8,128)(2,1)S(1)} async-done(((bf16[32,8,256]{2,1,0:T(8,128)(2,1)}), bf16[32,8,256]{2,1,0:T(8,128)(2,1)S(1)}, u32[]{:S(2)}, u32[]{:S(2)}) %all-to-all-start.3) | async-done | bytes 131104 | tf_op jit(solution)/shard_map/all_to_all | solution.py:340
  145.6 0.4 combine.1
  146.0 11.9 %all_to_all.55 = f32[8,1,128]{2,1,0:T(1,128)S(1)} all-to-all(f32[8,1,128]{2,1,0:T(1,128)S(1)} %bitcast.37), channel_id=1, replica_groups=mesh['grp'=8,'dev'=32] {'grp'}, dimensions={0} | all-to-all | bytes 8192 | tf_op jit(solution)/shard_map/all_to_all | solution.py:340
  157.9 0.0 copy-done.3
  157.9 0.0 copy-done.4
  157.9 0.7 update.1
  (4 shorter events, 0.0 us)
Async XLA Ops:
  0.6 16.1 %copy-start.8 = (s32[1,128,2]{1,2,0:T(2,128)S(1)}, s32[1,128,2]{1,2,0:T(2,128)}, u32[]{:S(2)}) copy-start(s32[1,128,2]{1,2,0:T(2,128)} %param.15) | copy-start | bytes 3076
  4.6 13.2 %copy-start.7 = (bf16[2,768,4]{1,2,0:T(4,128)(2,1)S(1)}, bf16[2,768,4]{1,2,0:T(4,128)(2,1)}, u32[]{:S(2)}) copy-start(bf16[2,768,4]{1,2,0:T(4,128)(2,1)} %param.21) | copy-start | bytes 36868
  4.6 31.3 %all-to-all-start = ((bf16[32,32,384]{2,1,0:T(8,128)(2,1)}), bf16[32,32,384]{2,1,0:T(8,128)(2,1)S(1)}, u32[]{:S(2)}, u32[]{:S(2)}) async-start(bf16[32,32,384]{2,1,0:T(8,128)(2,1)} %bitcast.3), calls=%async_computation | async-start | bytes 1572864 | tf_op jit(solution)/shard_map/all_to_all | solution.py:340
  16.8 0.6 copy-start.5
  17.8 3.7 %copy-start = (bf16[2,16,768]{2,1,0:T(8,128)(2,1)}, bf16[2,16,768]{2,1,0:T(8,128)(2,1)S(1)}, u32[]{:S(2)}) copy-start(bf16[2,16,768]{2,1,0:T(8,128)(2,1)S(1)} %pad.9.head_ref) | copy-start | bytes 147460
  39.4 49.7 %all-to-all-start.2 = ((bf16[32,72,384]{2,1,0:T(8,128)(2,1)}), bf16[32,72,384]{2,1,0:T(8,128)(2,1)S(1)}, u32[]{:S(2)}, u32[]{:S(2)}) async-start(bf16[32,72,384]{2,1,0:T(8,128)(2,1)} %bitcast.11), calls=%async_computation.2 | async-start | bytes 3538944 | tf_op jit(solution)/shard_map/all_to_all | solution.py:340
  89.1 29.8 %all-to-all-start.1 = ((bf16[32,24,384]{2,1,0:T(8,128)(2,1)}), bf16[32,24,384]{2,1,0:T(8,128)(2,1)S(1)}, u32[]{:S(2)}, u32[]{:S(2)}) async-start(bf16[32,24,384]{2,1,0:T(8,128)(2,1)} %bitcast.7), calls=%async_computation.1 | async-start | bytes 1179648 | tf_op jit(solution)/shard_map/all_to_all | solution.py:340
  96.6 0.8 copy-start.1
  97.4 21.5 %copy-start.2 = (f32[1,4,13]{2,1,0:T(4,128)S(1)}, f32[1,4,13]{2,1,0:T(4,128)}, u32[]{:S(2)}) copy-start(f32[1,4,13]{2,1,0:T(4,128)} %param.16) | copy-start | bytes 628
  119.0 17.5 %copy-start.6 = (s32[1,128,2]{2,1,0:T(8,128)S(1)}, s32[1,128,2]{2,1,0:T(8,128)}, u32[]{:S(2)}) copy-start(s32[1,128,2]{2,1,0:T(8,128)} %copy-done.5) | copy-start | bytes 3076
  119.0 38.9 %copy-start.3 = (bf16[1,2,192]{2,1,0:T(2,128)(2,1)S(1)}, bf16[1,2,192]{2,1,0:T(2,128)(2,1)}, u32[]{:S(2)}) copy-start(bf16[1,2,192]{2,1,0:T(2,128)(2,1)} %param.13) | copy-start | bytes 2308
  119.0 38.9 %copy-start.4 = (bf16[1,2,12]{2,1,0:T(2,128)(2,1)S(1)}, bf16[1,2,12]{2,1,0:T(2,128)(2,1)}, u32[]{:S(2)}) copy-start(bf16[1,2,12]{2,1,0:T(2,128)(2,1)} %param.14) | copy-start | bytes 148
  127.4 18.2 %all-to-all-start.3 = ((bf16[32,8,256]{2,1,0:T(8,128)(2,1)}), bf16[32,8,256]{2,1,0:T(8,128)(2,1)S(1)}, u32[]{:S(2)}, u32[]{:S(2)}) async-start(bf16[32,8,256]{2,1,0:T(8,128)(2,1)} %bitcast.15), calls=%async_computation.3 | async-start | bytes 262144 | tf_op jit(solution)/shard_map/all_to_all | solution.py:340

commit v3 on v2

--- a/solution.py
+++ b/solution.py
@@ -19,7 +19,7 @@
 SPLIT = (3, 1)
 PIECE = 12
 WIDE = 384
-SLOTS = 32
+GROUPS = 3
 LOW = 32
 
 norm_eps = 1e-06
@@ -48,14 +48,12 @@
     return jnp.where(pick, 1.0, 0.0).astype(BF16)
 
 
-def spread_order():
-    row = lax.broadcasted_iota(jnp.int32, (8 * SLOTS, 208), 0)
-    slot = row & (SLOTS - 1)
-    first = (row >> 5) * PIECE + slot
+def spread_order(group):
+    row = lax.broadcasted_iota(jnp.int32, (64, TOK), 0)
+    slot = group * 8 + (row & 7)
+    first = (row >> 3) * PIECE + slot
     source = jnp.where(slot < PIECE, first, first + (96 - PIECE))
-    source = jnp.where(slot < 2 * PIECE, source, slot + (192 - 2 * PIECE))
-    source = jnp.where(slot < 2 * PIECE + 2, source, -1)
-    return one_hot(source == lax.broadcasted_iota(jnp.int32, (8 * SLOTS, 208), 1))
+    return one_hot(source == lax.broadcasted_iota(jnp.int32, (64, TOK), 1))
 
 
 def gather_order(images):
@@ -84,19 +82,23 @@
     ]
     for copy in copies:
         copy.start()
-    order = spread_order()
+    orders = [spread_order(group) for group in range(GROUPS)]
     for copy in copies[:3]:
         copy.wait()
-    blank = jnp.zeros((2, WIDE - TOK), F32)
-    geo = jnp.concatenate([depth_ref[...].astype(F32), blank], axis=1)
-    lane = lax.broadcasted_iota(jnp.int32, (2, WIDE), 1)
+    depth = depth_ref[...].astype(F32)
+    tail = jnp.concatenate([depth[:, 128:TOK], jnp.zeros((2, 64), F32)], axis=1)
+    lane = lax.broadcasted_iota(jnp.int32, (2, 128), 1)
     camera = camera_ref[...].astype(F32)
     focal = focal_ref[...].astype(F32)
-    upper = lax.broadcasted_iota(jnp.int32, (2, WIDE), 0) == 0
+    upper = lax.broadcasted_iota(jnp.int32, (2, 128), 0) == 0
     for i in range(12):
-        geo = jnp.where(lane == TOK + i, camera[:, i : i + 1], geo)
-    geo = jnp.where(lane == TOK + 12, jnp.where(upper, focal[:, 0:1], focal[:, 1:2]), geo)
-    geo = jnp.concatenate([geo, jnp.zeros((14, WIDE), F32)], axis=0).astype(BF16)
+        tail = jnp.where(lane == 64 + i, camera[:, i : i + 1], tail)
+    tail = jnp.where(lane == 76, jnp.where(upper, focal[:, 0:1], focal[:, 1:2]), tail)
+    head = depth[:, 0:128]
+    geo = jnp.concatenate([head[0:1], tail[0:1], head[1:2], tail[1:2], jnp.zeros((4, 128), F32)], axis=0)
+    geo = jnp.concatenate([geo, geo], axis=0).astype(BF16)
+    for two in range(PEERS // 2):
+        out_ref[two * 16 : two * 16 + 16, GROUPS * WIDE :] = geo
     copies[3].wait()
     copies[4].wait()
     first = dot(tokens_ref[:, 0:depth_of], weight_ref[0:depth_of])
@@ -105,10 +107,9 @@
     for part in range(4):
         cols = slice((part // 2) * WIDE, (part // 2 + 1) * WIDE)
         at = (part % 2) * 96
-        rows = jnp.concatenate(
-            [emb_ref[at : at + 96, cols], emb_ref[TOK + at : TOK + at + 96, cols], geo], axis=0
-        )
-        out_ref[part * 8 * SLOTS : (part + 1) * 8 * SLOTS] = dot(order, rows).astype(BF16)
+        rows = jnp.concatenate([emb_ref[at : at + 96, cols], emb_ref[TOK + at : TOK + at + 96, cols]], axis=0)
+        for group in range(GROUPS):
+            out_ref[part * 64 : part * 64 + 64, group * WIDE : (group + 1) * WIDE] = dot(orders[group], rows).astype(BF16)
 
 
 def select_kernel(with_geo, rows_ref, where_ref, own_ref, after_ref, *rest):
@@ -117,18 +118,21 @@
     else:
         out_hbm, out_ref, sems = rest
     total = rows_ref.shape[0]
-    lane = lax.broadcasted_iota(jnp.int32, (TOK, total), 1)
+    rows = jnp.concatenate([rows_ref[:, group * WIDE : (group + 1) * WIDE] for group in range(GROUPS)], axis=0)
+    lane = lax.broadcasted_iota(jnp.int32, (TOK, GROUPS * total), 1)
     copies = []
     for step in range(out_ref.shape[0] // TOK):
         at = pl.ds(step * TOK, TOK)
         pick = one_hot(where_ref[at, :][:, :1] == lane)
-        out_ref[at, :] = dot(pick, rows_ref[...]).astype(BF16)
+        out_ref[at, :] = dot(pick, rows).astype(BF16)
         copies.append(pltpu.make_async_copy(out_ref.at[at], out_hbm.at[at], sems.at[step]))
         copies[-1].start()
     if with_geo:
         own_lane = lax.broadcasted_iota(jnp.int32, (16, total), 1)
-        own = one_hot(own_ref[...][:, :1] == own_lane)
-        geo_ref[...] = dot(own, rows_ref[:, 0:256])[0:REFS]
+        own = own_ref[...][:, :1]
+        for half in range(2):
+            found = dot(one_hot(own + half == own_lane), rows_ref[:, GROUPS * WIDE :])
+            geo_ref[:, half * 128 : half * 128 + 128] = found[0:REFS]
     for copy in copies:
         copy.wait()
 
@@ -203,7 +207,10 @@
 
 def decode_kernel(last, pairs, rows_ref, query_hbm, key_hbm, fold_ref, head_ref, *rest):
     if last:
-        geo_ref, par_ref, past_ref, points_ref, grad_ref, o_ref, *rest = rest
+        past_ref = None
+        if pairs < PAIRS:
+            past_ref, *rest = rest
+        geo_ref, par_ref, points_ref, grad_ref, o_ref, *rest = rest
     else:
         o_ref, *rest = rest
     query_ref, key_ref, x_ref, n_ref, q_ref, k_ref, u_ref, e_ref, sems = rest
@@ -248,32 +255,38 @@
                 ).astype(BF16)
             e_ref[view, pair] = dot_nt(head_ref[view], x_ref[view, at, :])[0:8]
 
-    upper = lax.broadcasted_iota(jnp.int32, (TOK, 2 * HD), 1) >= HD
+    four_of = lax.broadcasted_iota(jnp.int32, (TOK, 4 * HD), 1) // HD
+    block_of = lax.broadcasted_iota(jnp.int32, (8, 4 * TOK), 1) // TOK
     factor = math.log2(math.e) / math.sqrt(HD)
     for view in range(2):
-        @pl.loop(0, pairs)
+        @pl.loop(0, pairs, unroll=True)
         def _(pair):
             at = pl.ds(pl.multiple_of(pair * TOK, TOK), TOK)
-            acc = e_ref[view, pair]
-            for two in range(HEADS // 2):
-                cols = slice(two * 2 * HD, (two + 1) * 2 * HD)
+            acc = jnp.zeros((8, 4 * TOK), F32)
+            for four in range(HEADS // 4):
+                cols = slice(four * 4 * HD, (four + 1) * 4 * HD)
                 keys = k_ref[view, at, cols]
                 queries = q_ref[view, at, cols]
-                for half in range(2):
-                    head = 2 * two + half
-                    part = jnp.where(upper if half else jnp.logical_not(upper), queries, jnp.zeros_like(queries))
-                    scores = dot_nt(keys, part)
-                    top = jnp.max(scores, axis=0, keepdims=True)
-                    probs = jnp.exp2((scores - top) * factor).astype(BF16)
-                    mixed = dot(u_ref[view, pair, head * 16 : head * 16 + 16], probs)[0:8]
-                    acc = acc + mixed * (1.0 / mixed[4:5])
+                blocks = jnp.concatenate(
+                    [jnp.where(four_of == head, queries, jnp.zeros_like(queries)) for head in range(4)], axis=0
+                )
+                scores = dot_nt(keys, blocks)
+                top = jnp.max(scores, axis=0, keepdims=True)
+                probs = jnp.exp2((scores - top) * factor).astype(BF16)
+                mixed = dot(u_ref[view, pair, four * 64 : four * 64 + 64], probs)
+                own = mixed[0:8]
+                for head in range(1, 4):
+                    own = jnp.where(block_of == head, mixed[head * 16 : head * 16 + 8], own)
+                acc = acc + own * (1.0 / own[4:5])
+            acc = acc[:, 0:TOK] + acc[:, TOK : 2 * TOK] + acc[:, 2 * TOK : 3 * TOK] + acc[:, 3 * TOK :]
+            acc = acc + e_ref[view, pair]
             sub = lax.broadcasted_iota(jnp.int32, (8, TOK), 0)
             acc = jnp.where(sub == 3, 1.0 + jnp.exp(acc), acc)
             for c in range(4):
                 o_ref[c, pl.ds(2 * pair + view, 1), :] = acc[c : c + 1]
 
     if last:
-        outs = [jnp.concatenate([past_ref[c], o_ref[c]], axis=0) for c in range(4)]
+        outs = [o_ref[c] if past_ref is None else jnp.concatenate([past_ref[c], o_ref[c]], axis=0) for c in range(4)]
         for c in range(4):
             for view in range(REFS):
                 points_ref[view, c : c + 1] = outs[c][view : view + 1]
@@ -344,7 +357,7 @@
         embed_kernel,
         in_specs=[outside] * 5,
         out_specs=inside,
-        out_shape=shape((PEERS * SLOTS, WIDE), BF16),
+        out_shape=shape((PEERS * 8, GROUPS * WIDE + 128), BF16),
         scratch_shapes=[
             pltpu.VMEM(tokens.shape, BF16),
             pltpu.VMEM(embed_weight.shape, BF16),
@@ -376,10 +389,11 @@
     )(head_rows, hbm(cross_out), hbm(cross_keyval))
 
     graph = pair_graph[0].reshape(PEERS * REFS)
-    first = (graph // 2) * SLOTS + (graph % 2) * PIECE
-    where = first.reshape(PEERS, REFS, 1) + jnp.arange(PIECE, dtype=jnp.int32)
+    slot = (graph % 2)[:, None] * PIECE + jnp.arange(PIECE, dtype=jnp.int32)
+    where = (slot // 8) * (PEERS * 8) + (graph // 2)[:, None] * 8 + slot % 8
+    where = where.reshape(PEERS, REFS, PIECE)
     mine = lax.dynamic_slice_in_dim(graph, me * REFS, REFS)
-    own = jnp.pad((mine // 2) * SLOTS + 2 * PIECE + mine % 2, (0, 8))[:, None]
+    own = jnp.pad((mine // 2) * 8 + 2 * (mine % 2), (0, 8))[:, None]
     rows = []
     done = 0
     for pairs in SPLIT:
@@ -402,6 +416,7 @@
         done += pairs
 
     view_par = jnp.repeat(pair_params[0], 2, axis=0)
+    past = ()
     for part, pairs in enumerate(SPLIT):
         last = part == len(SPLIT) - 1
         weights = pltpu.VMEM((2, DD, DD), BF16)
@@ -410,7 +425,7 @@
         scratch += [pltpu.VMEM((2, pairs, HEADS * 16, TOK), BF16), pltpu.VMEM((2, pairs, 8, TOK), F32)]
         scratch.append(pltpu.SemaphoreType.DMA((4,)))
         if last:
-            extra = (my_geo, view_par, past)
+            extra = (*past, my_geo, view_par)
             outs = (shape((REFS, 4, TOK), F32), shape((PEERS * REFS, 256), BF16))
             scratch = [pltpu.VMEM((4, 2 * pairs, TOK), F32)] + scratch
         else:
@@ -426,7 +441,6 @@
             cost_estimate=pl.CostEstimate(flops=4000000000 * pairs, bytes_accessed=8000000, transcendentals=0),
             name="decode",
         )(rows[part], hbm(cross_query), hbm(cross_keyval), fold, head_rows, *extra)
-        past = past if last else past[0]
     points, grads = past
 
     own_grad, square = pl.pallas_call(

time: 159 us -> 146 us (0.918)
  Pallas kernels: 43.9 us -> 34.2 us
  waiting for transfers between devices: 61.4 us -> 59.4 us
    pallas_call x2, Pallas kernels: 29.9 us -> 21 us  [on_device(): pl.pallas_call(functools.partial(decode_kernel, last, pairs), in_specs=[i...]
    all_to_all x4, waiting for transfers between devices: 61.4 us -> 59.4 us  [exchange(): return lax.all_to_all(x, axis, split_axis=0, concat_axis=0, tiled=True)]
  transfers between devices with their start and end apart: 4 -> 4, of which waited for: 3 -> 4; matrix products, arithmetic and copies ran while one was open for 2% -> 2% of each run, Pallas kernels for 17% -> 13%
where the time goes in v3:
time: 146 us
  waiting for transfers between devices  59.4 us (41%)
  starting transfers between devices  36.6 us (25%)
  Pallas kernels  34.2 us (23%)
  blocking collectives  11.9 us (8%)
  local copies, waits for them, and re-layouts  2.5 us (2%)
    all_to_all x4, waiting for transfers between devices, exchange(): return lax.all_to_all(x, axis, split_axis=0, concat_axis=0, tiled=True)  59.4 us
    all_to_all x4, starting transfers between devices, exchange(): return lax.all_to_all(x, axis, split_axis=0, concat_axis=0, tiled=True)  36.6 us
    pallas_call x2, Pallas kernels, on_device(): pl.pallas_call(functools.partial(decode_kernel, last, pairs), in_specs=[i...  21 us
    all_to_all x1, blocking collectives, exchange(): return lax.all_to_all(x, axis, split_axis=0, concat_axis=0, tiled=True)  11.9 us
    pallas_call x2, Pallas kernels, on_device(): pl.pallas_call(functools.partial(select_kernel, last), in_specs=[inside]...  4.48 us
    pallas_call x1, Pallas kernels, on_device(): pl.pallas_call(embed_kernel, in_specs=[outside] * 5, out_specs=inside, ou...  3.99 us
    pallas_call x1, Pallas kernels, on_device(): pl.pallas_call(fold_kernel, in_specs=[inside, outside, outside], out_spec...  3.59 us
  transfers between devices with their start and end apart: 4, of which 4 were waited for; matrix products, arithmetic and copies ran while one was open for 2% of the time, Pallas kernels for 13%

profile of v3, /device:TPU:1, one launch (start us, length us, event | category | flops | bytes accessed | tf_op | source)
XLA Modules:
  0.0 145.8 jit_solution(15004436807820443174)
XLA Ops:
  0.6 0.0 copy-start.4
  0.6 4.0 %embed.1 = bf16[256,1280]{1,0:T(8,128)(2,1)} custom-call(bf16[384,1024]{1,0:T(8,128)(2,1)} %bitcast.40, bf16[1024,768]{1,0:T(8,128)(2,1)} %weight_hbm.1, bf16[2,192]{1,0:T(2,128)(2,1)} %bitcast.34, bf16[2,12]{1,0:T(2,128)(2,1)} %bitcast.38, bf16[1,2]{1,0:T(2,128)(2,1)} %focal_hbm.1), custom_call_target="tpu_custom_call" | custom-call | tf_op jit(solution)/shard_map/embed/pallas_call | solution.py:356
  4.6 0.0 copy-start.3
  4.7 12.0 %all-to-all-start = ((bf16[32,8,1280]{2,1,0:T(8,128)(2,1)}), bf16[32,8,1280]{2,1,0:T(8,128)(2,1)S(1)}, u32[]{:S(2)}, u32[]{:S(2)}) async-start(bf16[32,8,1280]{2,1,0:T(8,128)(2,1)} %bitcast.3), calls=%async_computation | async-start | bytes 1310720 | tf_op jit(solution)/shard_map/all_to_all | solution.py:353
  16.7 0.0 copy-done.4
  16.7 0.1 copy.25
  16.8 0.1 reshape_squeeze.10
  17.0 0.1 reshape_squeeze.9
  17.1 0.1 fusion.13
  17.2 0.1 copy.28.own_ref
  17.3 0.2 fusion.2
  17.5 0.3 reshape.106.where_ref
  17.8 0.0 copy-done.3
  17.9 3.6 %fold.1.after_ref.fold_ref = bf16[2,192,768]{2,1,0:T(8,128)(2,1)S(1)} custom-call(bf16[2,16,768]{2,1,0:T(8,128)(2,1)S(1)} %pad.9.head_ref, bf16[2,768,768]{2,1,0:T(8,128)(2,1)} %out_hbm.1, bf16[2,768,1536]{2,1,0:T(8,128)(2,1)} %key_hbm.3), custom_call_target="tpu_custom_call" | custom-call | flops 2000000000 | bytes 6000000 | tf_op jit(solution)/shard_map/fold/pallas_call | solution.py:376
  21.5 11.6 %all-to-all-done = bf16[32,8,1280]{2,1,0:T(8,128)(2,1)S(1)} async-done(((bf16[32,8,1280]{2,1,0:T(8,128)(2,1)}), bf16[32,8,1280]{2,1,0:T(8,128)(2,1)S(1)}, u32[]{:S(2)}, u32[]{:S(2)}) %all-to-all-start) | async-done | bytes 655392 | tf_op jit(solution)/shard_map/all_to_all | solution.py:353
  33.1 2.8 %select.46 = bf16[2304,384]{1,0:T(8,128)(2,1)} custom-call(bf16[256,1280]{1,0:T(8,128)(2,1)S(1)} %bitcast.27, s32[2304,1]{1,0:T(8,128)S(1)} %reshape.106.where_ref, s32[16,1]{1,0:T(8,128)S(1)} %copy.28.own_ref, bf16[2,192,768]{2,1,0:T(8,128)(2,1)S(1)} %fold.1.after_ref.fold_ref), custom_call_target="tpu_custom_call" | custom-call | flops 1843200000 | bytes 3538944 | tf_op jit(solution)/shard_map/select/pallas_call | solution.py:403
  36.0 8.4 %all-to-all-start.2 = ((bf16[32,72,384]{2,1,0:T(8,128)(2,1)}), bf16[32,72,384]{2,1,0:T(8,128)(2,1)S(1)}, u32[]{:S(2)}, u32[]{:S(2)}) async-start(bf16[32,72,384]{2,1,0:T(8,128)(2,1)} %bitcast.9), calls=%async_computation.2 | async-start | bytes 3538944 | tf_op jit(solution)/shard_map/all_to_all | solution.py:353
  44.4 0.6 slice.8
  45.0 0.9 reshape.105.where_ref
  45.9 1.6 %select.45 = (bf16[768,384]{1,0:T(8,128)(2,1)}, f32[8,256]{1,0:T(8,128)S(1)}) custom-call(bf16[256,1280]{1,0:T(8,128)(2,1)S(1)} %bitcast.28, s32[768,1]{1,0:T(8,128)S(1)} %reshape.105.where_ref, s32[16,1]{1,0:T(8,128)S(1)} %copy.28.own_ref, bf16[2,192,768]{2,1,0:T(8,128)(2,1)S(1)} %fold.1.after_ref.fold_ref), custom_call_target="tpu_custom_call" | custom-call | flops 614400000 | bytes 1179648 | tf_op jit(solution)/shard_map/select/pallas_call | solution.py:403
  47.6 38.1 %all-to-all-done.2 = bf16[32,72,384]{2,1,0:T(8,128)(2,1)S(1)} async-done(((bf16[32,72,384]{2,1,0:T(8,128)(2,1)}), bf16[32,72,384]{2,1,0:T(8,128)(2,1)S(1)}, u32[]{:S(2)}, u32[]{:S(2)}) %all-to-all-start.2) | async-done | bytes 1769504 | tf_op jit(solution)/shard_map/all_to_all | solution.py:353
  85.7 7.5 %all-to-all-start.1 = ((bf16[32,24,384]{2,1,0:T(8,128)(2,1)}), bf16[32,24,384]{2,1,0:T(8,128)(2,1)S(1)}, u32[]{:S(2)}, u32[]{:S(2)}) async-start(bf16[32,24,384]{2,1,0:T(8,128)(2,1)} %bitcast.7), calls=%async_computation.1 | async-start | bytes 1179648 | tf_op jit(solution)/shard_map/all_to_all | solution.py:353
  93.2 0.0 copy-start
  93.2 14.3 %decode.2.rest_0_ = f32[4,6,192]{2,1,0:T(8,128)S(1)} custom-call(bf16[2304,384]{1,0:T(8,128)(2,1)S(1)} %bitcast.26, bf16[2,768,768]{2,1,0:T(8,128)(2,1)} %query_hbm.3, bf16[2,768,1536]{2,1,0:T(8,128)(2,1)} %key_hbm.3, bf16[2,192,768]{2,1,0:T(8,128)(2,1)S(1)} %fold.1.after_ref.fold_ref, bf16[2,16,768]{2,1,0:T(8,128)(2,1)S(1)} %pad.9.head_ref), custom_call_target="tpu_custom_call" | custom-call | flops 12000000000 | bytes 8000000 | tf_op jit(solution)/shard_map/decode/pallas_call | solution.py:434
  107.5 0.6 all-to-all-done.1
  108.1 0.0 copy-done
  108.1 0.0 copy-start.1
  108.1 0.0 copy-start.2
  108.1 6.8 %decode.3 = (f32[8,4,192]{2,1,0:T(4,128)}, bf16[256,256]{1,0:T(8,128)(2,1)}) custom-call(bf16[768,384]{1,0:T(8,128)(2,1)S(1)} %bitcast.29, bf16[2,768,768]{2,1,0:T(8,128)(2,1)} %query_hbm.3, bf16[2,768,1536]{2,1,0:T(8,128)(2,1)} %key_hbm.3, bf16[2,192,768]{2,1,0:T(8,128)(2,1)S(1)} %fold.1.after_ref.fold_ref, bf16[2,16,768]{2,1,0:T(8,128)(2,1)S(1)} %pad.9.head_ref, ...), custom_call_target="tpu_custom_call" | custom-call | flops 4000000000 | bytes 8000000 | tf_op jit(solution)/shard_map/decode/pallas_call | solution.py:434
  114.9 8.7 %all-to-all-start.3 = ((bf16[32,8,256]{2,1,0:T(8,128)(2,1)}), bf16[32,8,256]{2,1,0:T(8,128)(2,1)S(1)}, u32[]{:S(2)}, u32[]{:S(2)}) async-start(bf16[32,8,256]{2,1,0:T(8,128)(2,1)} %bitcast.15), calls=%async_computation.3 | async-start | bytes 262144 | tf_op jit(solution)/shard_map/all_to_all | solution.py:353
  123.6 0.1 reshape_reshape_squeeze.3.graph_ref
  123.7 9.0 %all-to-all-done.3 = bf16[32,8,256]{2,1,0:T(8,128)(2,1)S(1)} async-done(((bf16[32,8,256]{2,1,0:T(8,128)(2,1)}), bf16[32,8,256]{2,1,0:T(8,128)(2,1)S(1)}, u32[]{:S(2)}, u32[]{:S(2)}) %all-to-all-start.3) | async-done | bytes 131104 | tf_op jit(solution)/shard_map/all_to_all | solution.py:353
  132.7 0.4 combine.1
  133.1 11.9 %all_to_all.55 = f32[8,1,128]{2,1,0:T(1,128)S(1)} all-to-all(f32[8,1,128]{2,1,0:T(1,128)S(1)} %bitcast.37), channel_id=1, replica_groups=mesh['grp'=8,'dev'=32] {'grp'}, dimensions={0} | all-to-all | bytes 8192 | tf_op jit(solution)/shard_map/all_to_all | solution.py:353
  145.0 0.0 copy-done.1
  145.0 0.0 copy-done.2
  145.0 0.7 update.1
  (4 shorter events, 0.0 us)
Async XLA Ops:
  0.6 16.1 %copy-start.4 = (s32[1,128,2]{1,2,0:T(2,128)S(1)}, s32[1,128,2]{1,2,0:T(2,128)}, u32[]{:S(2)}) copy-start(s32[1,128,2]{1,2,0:T(2,128)} %param.15) | copy-start | bytes 3076
  4.6 13.2 %copy-start.3 = (bf16[2,768,4]{1,2,0:T(4,128)(2,1)S(1)}, bf16[2,768,4]{1,2,0:T(4,128)(2,1)}, u32[]{:S(2)}) copy-start(bf16[2,768,4]{1,2,0:T(4,128)(2,1)} %param.21) | copy-start | bytes 36868
  4.7 28.4 %all-to-all-start = ((bf16[32,8,1280]{2,1,0:T(8,128)(2,1)}), bf16[32,8,1280]{2,1,0:T(8,128)(2,1)S(1)}, u32[]{:S(2)}, u32[]{:S(2)}) async-start(bf16[32,8,1280]{2,1,0:T(8,128)(2,1)} %bitcast.3), calls=%async_computation | async-start | bytes 1310720 | tf_op jit(solution)/shard_map/all_to_all | solution.py:353
  36.0 49.7 %all-to-all-start.2 = ((bf16[32,72,384]{2,1,0:T(8,128)(2,1)}), bf16[32,72,384]{2,1,0:T(8,128)(2,1)S(1)}, u32[]{:S(2)}, u32[]{:S(2)}) async-start(bf16[32,72,384]{2,1,0:T(8,128)(2,1)} %bitcast.9), calls=%async_computation.2 | async-start | bytes 3538944 | tf_op jit(solution)/shard_map/all_to_all | solution.py:353
  85.7 22.4 %all-to-all-start.1 = ((bf16[32,24,384]{2,1,0:T(8,128)(2,1)}), bf16[32,24,384]{2,1,0:T(8,128)(2,1)S(1)}, u32[]{:S(2)}, u32[]{:S(2)}) async-start(bf16[32,24,384]{2,1,0:T(8,128)(2,1)} %bitcast.7), calls=%async_computation.1 | async-start | bytes 1179648 | tf_op jit(solution)/shard_map/all_to_all | solution.py:353
  93.2 14.9 %copy-start = (f32[1,4,13]{2,1,0:T(4,128)S(1)}, f32[1,4,13]{2,1,0:T(4,128)}, u32[]{:S(2)}) copy-start(f32[1,4,13]{2,1,0:T(4,128)} %param.16) | copy-start | bytes 628
  108.1 36.9 %copy-start.1 = (bf16[1,2,192]{2,1,0:T(2,128)(2,1)S(1)}, bf16[1,2,192]{2,1,0:T(2,128)(2,1)}, u32[]{:S(2)}) copy-start(bf16[1,2,192]{2,1,0:T(2,128)(2,1)} %param.13) | copy-start | bytes 2308
  108.1 36.9 %copy-start.2 = (bf16[1,2,12]{2,1,0:T(2,128)(2,1)S(1)}, bf16[1,2,12]{2,1,0:T(2,128)(2,1)}, u32[]{:S(2)}) copy-start(bf16[1,2,12]{2,1,0:T(2,128)(2,1)} %param.14) | copy-start | bytes 148
  114.9 17.8 %all-to-all-start.3 = ((bf16[32,8,256]{2,1,0:T(8,128)(2,1)}), bf16[32,8,256]{2,1,0:T(8,128)(2,1)S(1)}, u32[]{:S(2)}, u32[]{:S(2)}) async-start(bf16[32,8,256]{2,1,0:T(8,128)(2,1)} %bitcast.15), calls=%async_computation.3 | async-start | bytes 262144 | tf_op jit(solution)/shard_map/all_to_all | solution.py:353

commit v4 on v3

--- a/solution.py
+++ b/solution.py
@@ -16,7 +16,6 @@
 PEERS = 32
 REFS = 8
 PAIRS = 4
-SPLIT = (3, 1)
 PIECE = 12
 WIDE = 384
 GROUPS = 3
@@ -52,38 +51,36 @@
     row = lax.broadcasted_iota(jnp.int32, (64, TOK), 0)
     slot = group * 8 + (row & 7)
     first = (row >> 3) * PIECE + slot
-    source = jnp.where(slot < PIECE, first, first + (96 - PIECE))
+    second = first + jnp.where(slot < 16, 92, 80)
+    source = jnp.where(slot < PIECE, first, second)
     return one_hot(source == lax.broadcasted_iota(jnp.int32, (64, TOK), 1))
 
 
-def gather_order(images):
-    size = 8 * images * PIECE
+def gather_order():
+    size = 4 * REFS * PIECE
     row = lax.broadcasted_iota(jnp.int32, (size, size), 0)
-    image = (row * 683) >> 16
-    rest = row - image * 96
+    image = (row * 1366) >> 16
+    rest = row - image * 48
     source = (rest * 43) >> 9
-    came = source * (images * PIECE) + image * PIECE + rest - source * PIECE
+    inner = rest - source * PIECE
+    came = source * (REFS * PIECE) + jnp.where(inner < 8, image * 8 + inner, REFS * 8 + image * 4 + inner - 8)
     return one_hot(came == lax.broadcasted_iota(jnp.int32, (size, size), 1))
 
 
-def embed_kernel(tokens_hbm, weight_hbm, depth_hbm, camera_hbm, focal_hbm, out_ref,
-                 tokens_ref, weight_ref, depth_ref, camera_ref, focal_ref, emb_ref, sems):
-    depth_of = weight_hbm.shape[0] // 2
-    parts = [pl.ds(0, depth_of), pl.ds(depth_of, depth_of)]
+def embed_kernel(tokens_hbm, weight_hbm, depth_hbm, camera_hbm, focal_hbm, out_hbm,
+                 tokens_ref, weight_ref, depth_ref, camera_ref, focal_ref, emb_ref, out_ref, sems):
     copies = [
-        pltpu.make_async_copy(depth_hbm, depth_ref, sems.at[0]),
-        pltpu.make_async_copy(camera_hbm, camera_ref, sems.at[1]),
-        pltpu.make_async_copy(focal_hbm, focal_ref, sems.at[2]),
-        pltpu.make_async_copy(tokens_hbm, tokens_ref, sems.at[3]),
-    ]
-    copies += [
-        pltpu.make_async_copy(weight_hbm.at[part], weight_ref.at[part], sems.at[4 + i])
-        for i, part in enumerate(parts)
+        pltpu.make_async_copy(tokens_hbm, tokens_ref, sems.at[0]),
+        pltpu.make_async_copy(weight_hbm.at[:, pl.ds(0, WIDE)], weight_ref.at[0], sems.at[1]),
+        pltpu.make_async_copy(weight_hbm.at[:, pl.ds(WIDE, WIDE)], weight_ref.at[1], sems.at[2]),
+        pltpu.make_async_copy(depth_hbm, depth_ref, sems.at[3]),
+        pltpu.make_async_copy(camera_hbm, camera_ref, sems.at[4]),
+        pltpu.make_async_copy(focal_hbm, focal_ref, sems.at[5]),
     ]
     for copy in copies:
         copy.start()
     orders = [spread_order(group) for group in range(GROUPS)]
-    for copy in copies[:3]:
+    for copy in copies[3:]:
         copy.wait()
     depth = depth_ref[...].astype(F32)
     tail = jnp.concatenate([depth[:, 128:TOK], jnp.zeros((2, 64), F32)], axis=1)
@@ -99,40 +96,49 @@
     geo = jnp.concatenate([geo, geo], axis=0).astype(BF16)
     for two in range(PEERS // 2):
         out_ref[two * 16 : two * 16 + 16, GROUPS * WIDE :] = geo
-    copies[3].wait()
-    copies[4].wait()
-    first = dot(tokens_ref[:, 0:depth_of], weight_ref[0:depth_of])
-    copies[5].wait()
-    emb_ref[...] = (first + dot(tokens_ref[:, depth_of:], weight_ref[depth_of:])).astype(BF16)
-    for part in range(4):
-        cols = slice((part // 2) * WIDE, (part // 2 + 1) * WIDE)
-        at = (part % 2) * 96
-        rows = jnp.concatenate([emb_ref[at : at + 96, cols], emb_ref[TOK + at : TOK + at + 96, cols]], axis=0)
-        for group in range(GROUPS):
-            out_ref[part * 64 : part * 64 + 64, group * WIDE : (group + 1) * WIDE] = dot(orders[group], rows).astype(BF16)
-
-
-def select_kernel(with_geo, rows_ref, where_ref, own_ref, after_ref, *rest):
-    if with_geo:
-        out_hbm, geo_ref, out_ref, sems = rest
-    else:
-        out_hbm, out_ref, sems = rest
+    copies[0].wait()
+    sends = []
+    for half in range(2):
+        copies[1 + half].wait()
+        emb_ref[...] = dot(tokens_ref[...], weight_ref[half]).astype(BF16)
+        for part in range(2):
+            at = part * 96
+            rows = jnp.concatenate([emb_ref[at : at + 96], emb_ref[TOK + at : TOK + at + 96]], axis=0)
+            to = pl.ds((2 * half + part) * 64, 64)
+            for group in range(GROUPS):
+                out_ref[to, group * WIDE : (group + 1) * WIDE] = dot(orders[group], rows).astype(BF16)
+            sends.append(pltpu.make_async_copy(out_ref.at[to], out_hbm.at[to], sems.at[6 + 2 * half + part]))
+            sends[-1].start()
+    for send in sends:
+        send.wait()
+
+
+def select_kernel(rows_ref, long_ref, short_ref, own_ref, after_ref, out_hbm, geo_ref, out_ref, sems):
     total = rows_ref.shape[0]
-    rows = jnp.concatenate([rows_ref[:, group * WIDE : (group + 1) * WIDE] for group in range(GROUPS)], axis=0)
-    lane = lax.broadcasted_iota(jnp.int32, (TOK, GROUPS * total), 1)
+    outer = jnp.concatenate([rows_ref[:, 0:WIDE], rows_ref[:, 2 * WIDE : 3 * WIDE]], axis=0)
+    middle = rows_ref[:, WIDE : 2 * WIDE]
+    outer_lane = lax.broadcasted_iota(jnp.int32, (64 * REFS, 2 * total), 1)
+    middle_lane = lax.broadcasted_iota(jnp.int32, (32 * REFS, total), 1)
+    size = 8 * REFS * PIECE
     copies = []
-    for step in range(out_ref.shape[0] // TOK):
-        at = pl.ds(step * TOK, TOK)
-        pick = one_hot(where_ref[at, :][:, :1] == lane)
-        out_ref[at, :] = dot(pick, rows).astype(BF16)
+    for step in range(PEERS // 8):
+        long_at = long_ref[step * 64 * REFS : (step + 1) * 64 * REFS]
+        short_at = short_ref[step * 32 * REFS : (step + 1) * 32 * REFS]
+        long = dot(one_hot(long_at == outer_lane), outer)
+        short = dot(one_hot(short_at == middle_lane), middle)
+        pieces = []
+        for peer in range(8):
+            pieces.append(long[peer * 8 * REFS : (peer + 1) * 8 * REFS])
+            pieces.append(short[peer * 4 * REFS : (peer + 1) * 4 * REFS])
+        at = pl.ds(step * size, size)
+        out_ref[at, :] = jnp.concatenate(pieces, axis=0).astype(BF16)
         copies.append(pltpu.make_async_copy(out_ref.at[at], out_hbm.at[at], sems.at[step]))
         copies[-1].start()
-    if with_geo:
-        own_lane = lax.broadcasted_iota(jnp.int32, (16, total), 1)
-        own = own_ref[...][:, :1]
-        for half in range(2):
-            found = dot(one_hot(own + half == own_lane), rows_ref[:, GROUPS * WIDE :])
-            geo_ref[:, half * 128 : half * 128 + 128] = found[0:REFS]
+    own_lane = lax.broadcasted_iota(jnp.int32, (16, total), 1)
+    own = own_ref[...]
+    for half in range(2):
+        found = dot(one_hot(own + half == own_lane), rows_ref[:, GROUPS * WIDE :])
+        geo_ref[:, half * 128 : half * 128 + 128] = found[0:REFS]
     for copy in copies:
         copy.wait()
 
@@ -205,15 +211,10 @@
     return grad_depth, tail
 
 
-def decode_kernel(last, pairs, rows_ref, query_hbm, key_hbm, fold_ref, head_ref, *rest):
-    if last:
-        past_ref = None
-        if pairs < PAIRS:
-            past_ref, *rest = rest
-        geo_ref, par_ref, points_ref, grad_ref, o_ref, *rest = rest
-    else:
-        o_ref, *rest = rest
-    query_ref, key_ref, x_ref, n_ref, q_ref, k_ref, u_ref, e_ref, sems = rest
+def decode_kernel(
+    rows_ref, query_hbm, key_hbm, fold_ref, head_ref, geo_ref, par_ref,
+    points_ref, grad_ref, o_ref, query_ref, key_ref, x_ref, n_ref, q_ref, k_ref, u_ref, e_ref, sems,
+):
     copies = []
     for view in range(2):
         copies.append(pltpu.make_async_copy(query_hbm.at[view], query_ref.at[view], sems.at[2 * view]))
@@ -222,17 +223,17 @@
         )
     for copy in copies:
         copy.start()
-    order = gather_order(2 * pairs)
-    size = 8 * 2 * pairs * PIECE
-    for part in range(4):
+    order = gather_order()
+    size = 4 * REFS * PIECE
+    for part in range(PEERS // 4):
         mixed = dot(order, rows_ref[part * size : (part + 1) * size]).astype(BF16)
-        cols = slice((part // 2) * WIDE, (part // 2 + 1) * WIDE)
-        for image in range(2 * pairs):
-            at = (image // 2) * TOK + (part % 2) * 96
-            x_ref[image % 2, at : at + 96, cols] = mixed[image * 96 : image * 96 + 96]
+        cols = slice((part // 4) * WIDE, (part // 4 + 1) * WIDE)
+        for image in range(REFS):
+            at = (image // 2) * TOK + (part % 4) * 48
+            x_ref[image % 2, at : at + 48, cols] = mixed[image * 48 : image * 48 + 48]
 
     for slot in range(2):
-        for pair in range(pairs):
+        for pair in range(PAIRS):
             at = pl.ds(pair * TOK, TOK)
             wide = x_ref[slot, at, :].astype(F32)
             centred = wide - jnp.mean(wide, axis=-1, keepdims=True)
@@ -241,11 +242,7 @@
 
     ones_row = jnp.where(lax.broadcasted_iota(jnp.int32, (8, TOK), 0) == 4, 1.0, 0.0)
     for view in range(2):
-        copies[2 * view].wait()
-        q_ref[view] = dot(n_ref[view], query_ref[view]).astype(BF16)
-        copies[2 * view + 1].wait()
-        k_ref[view] = dot(n_ref[1 - view], key_ref[view]).astype(BF16)
-        for pair in range(pairs):
+        for pair in range(PAIRS):
             at = pl.ds(pair * TOK, TOK)
             value = dot_nt(fold_ref[view], n_ref[1 - view, at, :])
             for head in range(HEADS):
@@ -255,46 +252,73 @@
                 ).astype(BF16)
             e_ref[view, pair] = dot_nt(head_ref[view], x_ref[view, at, :])[0:8]
 
-    four_of = lax.broadcasted_iota(jnp.int32, (TOK, 4 * HD), 1) // HD
+    half_of = lax.broadcasted_iota(jnp.int32, (TOK, 2 * HD), 1) // HD
     block_of = lax.broadcasted_iota(jnp.int32, (8, 4 * TOK), 1) // TOK
     factor = math.log2(math.e) / math.sqrt(HD)
-    for view in range(2):
-        @pl.loop(0, pairs, unroll=True)
-        def _(pair):
-            at = pl.ds(pl.multiple_of(pair * TOK, TOK), TOK)
-            acc = jnp.zeros((8, 4 * TOK), F32)
-            for four in range(HEADS // 4):
-                cols = slice(four * 4 * HD, (four + 1) * 4 * HD)
-                keys = k_ref[view, at, cols]
-                queries = q_ref[view, at, cols]
-                blocks = jnp.concatenate(
-                    [jnp.where(four_of == head, queries, jnp.zeros_like(queries)) for head in range(4)], axis=0
-                )
-                scores = dot_nt(keys, blocks)
-                top = jnp.max(scores, axis=0, keepdims=True)
-                probs = jnp.exp2((scores - top) * factor).astype(BF16)
-                mixed = dot(u_ref[view, pair, four * 64 : four * 64 + 64], probs)
-                own = mixed[0:8]
-                for head in range(1, 4):
-                    own = jnp.where(block_of == head, mixed[head * 16 : head * 16 + 8], own)
-                acc = acc + own * (1.0 / own[4:5])
-            acc = acc[:, 0:TOK] + acc[:, TOK : 2 * TOK] + acc[:, 2 * TOK : 3 * TOK] + acc[:, 3 * TOK :]
-            acc = acc + e_ref[view, pair]
-            sub = lax.broadcasted_iota(jnp.int32, (8, TOK), 0)
-            acc = jnp.where(sub == 3, 1.0 + jnp.exp(acc), acc)
-            for c in range(4):
-                o_ref[c, pl.ds(2 * pair + view, 1), :] = acc[c : c + 1]
-
-    if last:
-        outs = [o_ref[c] if past_ref is None else jnp.concatenate([past_ref[c], o_ref[c]], axis=0) for c in range(4)]
+
+    def project(view):
+        copies[2 * view].wait()
+        q_ref[view] = dot(n_ref[view], query_ref[view]).astype(BF16)
+        copies[2 * view + 1].wait()
+        k_ref[view] = dot(n_ref[1 - view], key_ref[view]).astype(BF16)
+
+    def scores_of(view, pair, four):
+        at = pl.ds(pair * TOK, TOK)
+        parts = []
+        for two in range(2 * four, 2 * four + 2):
+            side = slice(two * 2 * HD, (two + 1) * 2 * HD)
+            queries = q_ref[view, at, side]
+            blocks = jnp.concatenate(
+                [jnp.where(half_of == head, queries, jnp.zeros_like(queries)) for head in range(2)], axis=0
+            )
+            parts.append(dot_nt(k_ref[view, at, side], blocks))
+        return jnp.concatenate(parts, axis=1)
+
+    def probs_of(scores):
+        top = jnp.max(scores, axis=0, keepdims=True)
+        return jnp.exp2((scores - top) * factor).astype(BF16)
+
+    def context_of(unit, probs):
+        view, pair, four = unit
+        mixed = dot(u_ref[view, pair, four * 64 : four * 64 + 64], probs)
+        own = mixed[0:8]
+        for head in range(1, 4):
+            own = jnp.where(block_of == head, mixed[head * 16 : head * 16 + 8], own)
+        sums[view, pair] = sums.get((view, pair), 0.0) + own * (1.0 / own[4:5])
+
+    units = [(view, pair, four) for view in range(2) for pair in range(PAIRS) for four in range(HEADS // 4)]
+    sums = {}
+    project(0)
+    ahead = [scores_of(*unit) for unit in units[:2]]
+    probs = None
+    for i, unit in enumerate(units):
+        if i == 2:
+            project(1)
+        scores = ahead.pop(0)
+        if i + 2 < len(units):
+            ahead.append(scores_of(*units[i + 2]))
+        behind = probs
+        probs = probs_of(scores)
+        if i > 0:
+            context_of(units[i - 1], behind)
+    context_of(units[-1], probs)
+    for (view, pair), acc in sums.items():
+        acc = acc[:, 0:TOK] + acc[:, TOK : 2 * TOK] + acc[:, 2 * TOK : 3 * TOK] + acc[:, 3 * TOK :]
+        acc = acc + e_ref[view, pair]
+        sub = lax.broadcasted_iota(jnp.int32, (8, TOK), 0)
+        acc = jnp.where(sub == 3, 1.0 + jnp.exp(acc), acc)
         for c in range(4):
-            for view in range(REFS):
-                points_ref[view, c : c + 1] = outs[c][view : view + 1]
-        grad_depth, tail = view_gradients(outs, geo_ref[...], par_ref[...])
-        both = jnp.concatenate([grad_depth, tail], axis=1)
-        twice = jnp.concatenate([both, both], axis=0).astype(BF16)
-        for peer in range(0, PEERS, 2):
-            grad_ref[peer * REFS : (peer + 2) * REFS] = twice
+            o_ref[c, 2 * pair + view : 2 * pair + view + 1, :] = acc[c : c + 1]
+
+    outs = [o_ref[c] for c in range(4)]
+    for c in range(4):
+        for view in range(REFS):
+            points_ref[view, c : c + 1] = outs[c][view : view + 1]
+    grad_depth, tail = view_gradients(outs, geo_ref[...], par_ref[...])
+    both = jnp.concatenate([grad_depth, tail], axis=1)
+    twice = jnp.concatenate([both, both], axis=0).astype(BF16)
+    for peer in range(0, PEERS, 2):
+        grad_ref[peer * REFS : (peer + 2) * REFS] = twice
 
 
 def combine_kernel(me_ref, graph_ref, grad_ref, own_ref, square_ref):
@@ -353,19 +377,21 @@
         return lax.all_to_all(x, axis, split_axis=0, concat_axis=0, tiled=True)
 
     tokens = enc_tokens[0].reshape(2 * TOK, -1)
+    message_dims = (PEERS * 8, GROUPS * WIDE + 128)
     message = pl.pallas_call(
         embed_kernel,
         in_specs=[outside] * 5,
-        out_specs=inside,
-        out_shape=shape((PEERS * 8, GROUPS * WIDE + 128), BF16),
+        out_specs=outside,
+        out_shape=shape(message_dims, BF16),
         scratch_shapes=[
             pltpu.VMEM(tokens.shape, BF16),
-            pltpu.VMEM(embed_weight.shape, BF16),
+            pltpu.VMEM((2, embed_weight.shape[0], WIDE), BF16),
             pltpu.VMEM((2, TOK), BF16),
             pltpu.VMEM((2, 12), BF16),
             pltpu.VMEM((1, 2), BF16),
-            pltpu.VMEM((2 * TOK, DD), BF16),
-            pltpu.SemaphoreType.DMA((6,)),
+            pltpu.VMEM((2 * TOK, WIDE), BF16),
+            pltpu.VMEM(message_dims, BF16),
+            pltpu.SemaphoreType.DMA((10,)),
         ],
         compiler_params=params_for(24),
         name="embed",
@@ -389,59 +415,45 @@
     )(head_rows, hbm(cross_out), hbm(cross_keyval))
 
     graph = pair_graph[0].reshape(PEERS * REFS)
-    slot = (graph % 2)[:, None] * PIECE + jnp.arange(PIECE, dtype=jnp.int32)
-    where = (slot // 8) * (PEERS * 8) + (graph // 2)[:, None] * 8 + slot % 8
-    where = where.reshape(PEERS, REFS, PIECE)
+    base = (graph // 2) * 8
+    long_rows = (base + (graph % 2) * (PEERS * 8))[:, None] + jnp.arange(8, dtype=jnp.int32)
+    short_rows = (base + (graph % 2) * 4)[:, None] + jnp.arange(4, dtype=jnp.int32)
     mine = lax.dynamic_slice_in_dim(graph, me * REFS, REFS)
     own = jnp.pad((mine // 2) * 8 + 2 * (mine % 2), (0, 8))[:, None]
-    rows = []
-    done = 0
-    for pairs in SPLIT:
-        count = PEERS * 2 * pairs * PIECE
-        last = done + pairs == PAIRS
-        moved = shape((count, WIDE), BF16)
-        outgoing = pl.pallas_call(
-            functools.partial(select_kernel, last),
-            in_specs=[inside] * 3 + [pl.BlockSpec(memory_space=pl.ANY)],
-            out_specs=(outside, inside) if last else outside,
-            out_shape=(moved, shape((REFS, 256), F32)) if last else moved,
-            scratch_shapes=[pltpu.VMEM((count, WIDE), BF16), pltpu.SemaphoreType.DMA((count // TOK,))],
-            compiler_params=params_for(20),
-            cost_estimate=pl.CostEstimate(flops=count * 800000, bytes_accessed=4 * count * WIDE, transcendentals=0),
-            name="select",
-        )(spread, where[:, 2 * done : 2 * (done + pairs)].reshape(count, 1), own, fold)
-        if last:
-            outgoing, my_geo = outgoing
-        rows.append(exchange(outgoing, "dev"))
-        done += pairs
-
-    view_par = jnp.repeat(pair_params[0], 2, axis=0)
-    past = ()
-    for part, pairs in enumerate(SPLIT):
-        last = part == len(SPLIT) - 1
-        weights = pltpu.VMEM((2, DD, DD), BF16)
-        tokens_of = pltpu.VMEM((2, pairs * TOK, DD), BF16)
-        scratch = [weights] * 2 + [tokens_of] * 4
-        scratch += [pltpu.VMEM((2, pairs, HEADS * 16, TOK), BF16), pltpu.VMEM((2, pairs, 8, TOK), F32)]
-        scratch.append(pltpu.SemaphoreType.DMA((4,)))
-        if last:
-            extra = (*past, my_geo, view_par)
-            outs = (shape((REFS, 4, TOK), F32), shape((PEERS * REFS, 256), BF16))
-            scratch = [pltpu.VMEM((4, 2 * pairs, TOK), F32)] + scratch
-        else:
-            extra = ()
-            outs = (shape((4, 2 * pairs, TOK), F32),)
-        past = pl.pallas_call(
-            functools.partial(decode_kernel, last, pairs),
-            in_specs=[inside] + [outside] * 2 + [inside] * (2 + len(extra)),
-            out_specs=(inside,) * len(outs),
-            out_shape=outs,
-            scratch_shapes=scratch,
-            compiler_params=params_for(28),
-            cost_estimate=pl.CostEstimate(flops=4000000000 * pairs, bytes_accessed=8000000, transcendentals=0),
-            name="decode",
-        )(rows[part], hbm(cross_query), hbm(cross_keyval), fold, head_rows, *extra)
-    points, grads = past
+    count = PEERS * REFS * PIECE
+    outgoing, my_geo = pl.pallas_call(
+        select_kernel,
+        in_specs=[inside] * 4 + [pl.BlockSpec(memory_space=pl.ANY)],
+        out_specs=(outside, inside),
+        out_shape=(shape((count, WIDE), BF16), shape((REFS, 256), F32)),
+        scratch_shapes=[pltpu.VMEM((count, WIDE), BF16), pltpu.SemaphoreType.DMA((PEERS // 8,))],
+        compiler_params=params_for(20),
+        name="select",
+    )(spread, long_rows.reshape(-1, 1), short_rows.reshape(-1, 1), own, fold)
+    rows = exchange(outgoing, "dev")
+
+    weights = pltpu.VMEM((2, DD, DD), BF16)
+    tokens_of = pltpu.VMEM((2, PAIRS * TOK, DD), BF16)
+    points, grads = pl.pallas_call(
+        decode_kernel,
+        in_specs=[inside] + [outside] * 2 + [inside] * 4,
+        out_specs=(inside, inside),
+        out_shape=(shape((REFS, 4, TOK), F32), shape((PEERS * REFS, 256), BF16)),
+        scratch_shapes=[
+            pltpu.VMEM((4, REFS, TOK), F32),
+            weights,
+            weights,
+            tokens_of,
+            tokens_of,
+            tokens_of,
+            tokens_of,
+            pltpu.VMEM((2, PAIRS, HEADS * 16, TOK), BF16),
+            pltpu.VMEM((2, PAIRS, 8, TOK), F32),
+            pltpu.SemaphoreType.DMA((4,)),
+        ],
+        compiler_params=params_for(32),
+        name="decode",
+    )(rows, hbm(cross_query), hbm(cross_keyval), fold, head_rows, my_geo, jnp.repeat(pair_params[0], 2, axis=0))
 
     own_grad, square = pl.pallas_call(
         combine_kernel,

time: 146 us -> 141 us (0.966)
  blocking collectives: 11.9 us -> 72.8 us
  waiting for transfers between devices: 59.4 us -> 20.6 us
  starting transfers between devices: 36.6 us -> 20 us
  Pallas kernels: 34.2 us -> 25.3 us
  local copies, waits for them, and re-layouts: 2.5 us -> 1 us
    all_to_all x1 -> x2, blocking collectives: 11.9 us -> 72.8 us  [exchange(): return lax.all_to_all(x, axis, split_axis=0, concat_axis=0, tiled=True)]
    all_to_all x4 -> x2, waiting for transfers between devices: 59.4 us -> 20.6 us  [exchange(): return lax.all_to_all(x, axis, split_axis=0, concat_axis=0, tiled=True)]
    all_to_all x4 -> x2, starting transfers between devices: 36.6 us -> 20 us  [exchange(): return lax.all_to_all(x, axis, split_axis=0, concat_axis=0, tiled=True)]
    pallas_call x5 -> x3, Pallas kernels: 29.5 us -> 20.6 us  [the longest x1 13.7 us: on_device(): pl.pallas_call(decode_kernel, in_specs=[inside] + [outside] * 2 + [inside...]
  transfers between devices with their start and end apart: 4 -> 2, of which waited for: 4 -> 2; matrix products, arithmetic and copies ran while one was open for 2% -> 1% of each run, Pallas kernels for 13% -> 3%
where the time goes in v4:
time: 141 us
  blocking collectives  72.8 us (52%)
  Pallas kernels  25.3 us (18%)
  waiting for transfers between devices  20.6 us (15%)
  starting transfers between devices  20 us (14%)
    all_to_all x2, blocking collectives, exchange(): return lax.all_to_all(x, axis, split_axis=0, concat_axis=0, tiled=True)  72.8 us
    all_to_all x2, waiting for transfers between devices, exchange(): return lax.all_to_all(x, axis, split_axis=0, concat_axis=0, tiled=True)  20.6 us
    all_to_all x2, starting transfers between devices, exchange(): return lax.all_to_all(x, axis, split_axis=0, concat_axis=0, tiled=True)  20 us
    pallas_call x1, Pallas kernels, on_device(): pl.pallas_call(decode_kernel, in_specs=[inside] + [outside] * 2 + [inside...  13.7 us
    pallas_call x1, Pallas kernels, on_device(): pl.pallas_call(embed_kernel, in_specs=[outside] * 5, out_specs=outside, o...  4.01 us
    pallas_call x1, Pallas kernels, on_device(): pl.pallas_call(fold_kernel, in_specs=[inside, outside, outside], out_spec...  3.59 us
    pallas_call x1, Pallas kernels, on_device(): pl.pallas_call(select_kernel, in_specs=[inside] * 4 + [pl.BlockSpec(memor...  2.92 us
  transfers between devices with their start and end apart: 2, of which 2 were waited for; matrix products, arithmetic and copies ran while one was open for 1% of the time, Pallas kernels for 3%

profile of v4, /device:TPU:1, one launch (start us, length us, event | category | flops | bytes accessed | tf_op | source)
XLA Modules:
  0.0 140.8 jit_solution(10193539699965510030)
XLA Ops:
  0.6 0.0 copy-start.4
  0.6 4.0 %embed.1 = bf16[256,1280]{1,0:T(8,128)(2,1)} custom-call(bf16[384,1024]{1,0:T(8,128)(2,1)} %bitcast.36, bf16[1024,768]{1,0:T(8,128)(2,1)} %weight_hbm.1, bf16[2,192]{1,0:T(2,128)(2,1)} %bitcast.31, bf16[2,12]{1,0:T(2,128)(2,1)} %bitcast.34, bf16[1,2]{1,0:T(2,128)(2,1)} %focal_hbm.1), custom_call_target="tpu_custom_call" | custom-call | tf_op jit(solution)/shard_map/embed/pallas_call | solution.py:381
  4.7 0.0 copy-start.3
  4.7 12.0 %all-to-all-start = ((bf16[32,8,1280]{2,1,0:T(8,128)(2,1)}), bf16[32,8,1280]{2,1,0:T(8,128)(2,1)S(1)}, u32[]{:S(2)}, u32[]{:S(2)}) async-start(bf16[32,8,1280]{2,1,0:T(8,128)(2,1)} %bitcast.3), calls=%async_computation | async-start | bytes 1310720 | tf_op jit(solution)/shard_map/all_to_all | solution.py:377
  16.7 0.0 copy-done.4
  16.7 0.1 copy.22
  16.9 0.1 reshape_squeeze.7
  17.0 0.1 fusion.2
  17.1 0.1 copy.25.own_ref
  17.2 0.1 iota_add_fusion
  17.3 0.2 add.115.short_ref
  17.5 0.1 iota_add_fusion.1
  17.6 0.3 add.114.long_ref
  17.9 0.0 copy-done.3
  17.9 3.6 %fold.1.after_ref.fold_ref = bf16[2,192,768]{2,1,0:T(8,128)(2,1)S(1)} custom-call(bf16[2,16,768]{2,1,0:T(8,128)(2,1)S(1)} %pad.9.head_ref, bf16[2,768,768]{2,1,0:T(8,128)(2,1)} %out_hbm.1, bf16[2,768,1536]{2,1,0:T(8,128)(2,1)} %key_hbm.1), custom_call_target="tpu_custom_call" | custom-call | flops 2000000000 | bytes 6000000 | tf_op jit(solution)/shard_map/fold/pallas_call | solution.py:402
  21.5 11.6 %all-to-all-done = bf16[32,8,1280]{2,1,0:T(8,128)(2,1)S(1)} async-done(((bf16[32,8,1280]{2,1,0:T(8,128)(2,1)}), bf16[32,8,1280]{2,1,0:T(8,128)(2,1)S(1)}, u32[]{:S(2)}, u32[]{:S(2)}) %all-to-all-start) | async-done | bytes 655392 | tf_op jit(solution)/shard_map/all_to_all | solution.py:377
  33.1 2.9 %select.48 = (bf16[3072,384]{1,0:T(8,128)(2,1)S(1)}, f32[8,256]{1,0:T(8,128)S(1)}) custom-call(bf16[256,1280]{1,0:T(8,128)(2,1)S(1)} %bitcast.24, s32[2048,1]{1,0:T(8,128)S(1)} %add.114.long_ref, s32[1024,1]{1,0:T(8,128)S(1)} %add.115.short_ref, s32[16,1]{1,0:T(8,128)S(1)} %copy.25.own_ref, bf16[2,192,768]{2,1,0:T(8,128)(2,1)S(1)} %fold.1.after_ref.fold_ref), custom_call_target="tpu_custom_call" | custom-call | tf_op jit(solution)/shard_map/select/pallas_call | solution.py:424
  36.0 0.0 copy-start
  36.0 61.8 %all_to_all.44 = bf16[32,96,384]{2,1,0:T(8,128)(2,1)S(1)} all-to-all(bf16[32,96,384]{2,1,0:T(8,128)(2,1)S(1)} %bitcast.25), channel_id=1, replica_groups=mesh['grp'=8,'dev'=32] {'dev'}, dimensions={0} | all-to-all | bytes 4718592 | tf_op jit(solution)/shard_map/all_to_all | solution.py:377
  97.9 0.0 copy-done
  97.9 0.0 copy-start.1
  97.9 0.0 copy-start.2
  97.9 13.7 %decode.1 = (f32[8,4,192]{2,1,0:T(4,128)}, bf16[256,256]{1,0:T(8,128)(2,1)}) custom-call(bf16[3072,384]{1,0:T(8,128)(2,1)S(1)} %bitcast.23, bf16[2,768,768]{2,1,0:T(8,128)(2,1)} %query_hbm.1, bf16[2,768,1536]{2,1,0:T(8,128)(2,1)} %key_hbm.1, bf16[2,192,768]{2,1,0:T(8,128)(2,1)S(1)} %fold.1.after_ref.fold_ref, bf16[2,16,768]{2,1,0:T(8,128)(2,1)S(1)} %pad.9.head_ref, ...), custom_call_target="tpu_custom_call" | custom-call | tf_op jit(solution)/shard_map/decode/pallas_call | solution.py:437
  111.5 8.0 %all-to-all-start.2 = ((bf16[32,8,256]{2,1,0:T(8,128)(2,1)}), bf16[32,8,256]{2,1,0:T(8,128)(2,1)S(1)}, u32[]{:S(2)}, u32[]{:S(2)}) async-start(bf16[32,8,256]{2,1,0:T(8,128)(2,1)} %bitcast.13), calls=%async_computation.2 | async-start | bytes 262144 | tf_op jit(solution)/shard_map/all_to_all | solution.py:377
  119.5 0.1 reshape_reshape_squeeze.3.graph_ref
  119.7 9.0 %all-to-all-done.2 = bf16[32,8,256]{2,1,0:T(8,128)(2,1)S(1)} async-done(((bf16[32,8,256]{2,1,0:T(8,128)(2,1)}), bf16[32,8,256]{2,1,0:T(8,128)(2,1)S(1)}, u32[]{:S(2)}, u32[]{:S(2)}) %all-to-all-start.2) | async-done | bytes 131104 | tf_op jit(solution)/shard_map/all_to_all | solution.py:377
  128.7 0.4 combine.1
  129.1 10.9 %all_to_all.45 = f32[8,1,128]{2,1,0:T(1,128)S(1)} all-to-all(f32[8,1,128]{2,1,0:T(1,128)S(1)} %bitcast.33), channel_id=1, replica_groups=mesh['grp'=8,'dev'=32] {'grp'}, dimensions={0} | all-to-all | bytes 8192 | tf_op jit(solution)/shard_map/all_to_all | solution.py:377
  140.0 0.0 copy-done.1
  140.0 0.0 copy-done.2
  140.0 0.7 update.1
  (5 shorter events, 0.0 us)
Async XLA Ops:
  0.6 16.1 %copy-start.4 = (s32[1,128,2]{1,2,0:T(2,128)S(1)}, s32[1,128,2]{1,2,0:T(2,128)}, u32[]{:S(2)}) copy-start(s32[1,128,2]{1,2,0:T(2,128)} %param.15) | copy-start | bytes 3076
  4.7 13.3 %copy-start.3 = (bf16[2,768,4]{1,2,0:T(4,128)(2,1)S(1)}, bf16[2,768,4]{1,2,0:T(4,128)(2,1)}, u32[]{:S(2)}) copy-start(bf16[2,768,4]{1,2,0:T(4,128)(2,1)} %param.21) | copy-start | bytes 36868
  4.7 28.4 %all-to-all-start = ((bf16[32,8,1280]{2,1,0:T(8,128)(2,1)}), bf16[32,8,1280]{2,1,0:T(8,128)(2,1)S(1)}, u32[]{:S(2)}, u32[]{:S(2)}) async-start(bf16[32,8,1280]{2,1,0:T(8,128)(2,1)} %bitcast.3), calls=%async_computation | async-start | bytes 1310720 | tf_op jit(solution)/shard_map/all_to_all | solution.py:377
  36.0 61.8 %copy-start = (f32[1,4,13]{2,1,0:T(4,128)S(1)}, f32[1,4,13]{2,1,0:T(4,128)}, u32[]{:S(2)}) copy-start(f32[1,4,13]{2,1,0:T(4,128)} %param.16) | copy-start | bytes 628
  97.9 42.2 %copy-start.1 = (bf16[1,2,192]{2,1,0:T(2,128)(2,1)S(1)}, bf16[1,2,192]{2,1,0:T(2,128)(2,1)}, u32[]{:S(2)}) copy-start(bf16[1,2,192]{2,1,0:T(2,128)(2,1)} %param.13) | copy-start | bytes 2308
  97.9 42.2 %copy-start.2 = (bf16[1,2,12]{2,1,0:T(2,128)(2,1)S(1)}, bf16[1,2,12]{2,1,0:T(2,128)(2,1)}, u32[]{:S(2)}) copy-start(bf16[1,2,12]{2,1,0:T(2,128)(2,1)} %param.14) | copy-start | bytes 148
  111.5 17.2 %all-to-all-start.2 = ((bf16[32,8,256]{2,1,0:T(8,128)(2,1)}), bf16[32,8,256]{2,1,0:T(8,128)(2,1)S(1)}, u32[]{:S(2)}, u32[]{:S(2)}) async-start(bf16[32,8,256]{2,1,0:T(8,128)(2,1)} %bitcast.13), calls=%async_computation.2 | async-start | bytes 262144 | tf_op jit(solution)/shard_map/all_to_all | solution.py:377

commit v5 on v4

--- a/solution.py
+++ b/solution.py
@@ -47,13 +47,13 @@
     return jnp.where(pick, 1.0, 0.0).astype(BF16)
 
 
-def spread_order(group):
-    row = lax.broadcasted_iota(jnp.int32, (64, TOK), 0)
-    slot = group * 8 + (row & 7)
-    first = (row >> 3) * PIECE + slot
+def spread_order():
+    row = lax.broadcasted_iota(jnp.int32, (64 * GROUPS, TOK), 0)
+    slot = (row >> 6) * 8 + (row & 7)
+    first = ((row >> 3) & 7) * PIECE + slot
     second = first + jnp.where(slot < 16, 92, 80)
     source = jnp.where(slot < PIECE, first, second)
-    return one_hot(source == lax.broadcasted_iota(jnp.int32, (64, TOK), 1))
+    return one_hot(source == lax.broadcasted_iota(jnp.int32, (64 * GROUPS, TOK), 1))
 
 
 def gather_order():
@@ -79,7 +79,7 @@
     ]
     for copy in copies:
         copy.start()
-    orders = [spread_order(group) for group in range(GROUPS)]
+    order = spread_order()
     for copy in copies[3:]:
         copy.wait()
     depth = depth_ref[...].astype(F32)
@@ -105,8 +105,9 @@
             at = part * 96
             rows = jnp.concatenate([emb_ref[at : at + 96], emb_ref[TOK + at : TOK + at + 96]], axis=0)
             to = pl.ds((2 * half + part) * 64, 64)
+            mixed = dot(order, rows).astype(BF16)
             for group in range(GROUPS):
-                out_ref[to, group * WIDE : (group + 1) * WIDE] = dot(orders[group], rows).astype(BF16)
+                out_ref[to, group * WIDE : (group + 1) * WIDE] = mixed[group * 64 : group * 64 + 64]
             sends.append(pltpu.make_async_copy(out_ref.at[to], out_hbm.at[to], sems.at[6 + 2 * half + part]))
             sends[-1].start()
     for send in sends:
@@ -117,17 +118,17 @@
     total = rows_ref.shape[0]
     outer = jnp.concatenate([rows_ref[:, 0:WIDE], rows_ref[:, 2 * WIDE : 3 * WIDE]], axis=0)
     middle = rows_ref[:, WIDE : 2 * WIDE]
-    outer_lane = lax.broadcasted_iota(jnp.int32, (64 * REFS, 2 * total), 1)
-    middle_lane = lax.broadcasted_iota(jnp.int32, (32 * REFS, total), 1)
-    size = 8 * REFS * PIECE
+    outer_lane = lax.broadcasted_iota(jnp.int32, (128 * REFS, 2 * total), 1)
+    middle_lane = lax.broadcasted_iota(jnp.int32, (64 * REFS, total), 1)
+    size = 16 * REFS * PIECE
     copies = []
-    for step in range(PEERS // 8):
-        long_at = long_ref[step * 64 * REFS : (step + 1) * 64 * REFS]
-        short_at = short_ref[step * 32 * REFS : (step + 1) * 32 * REFS]
+    for step in range(PEERS // 16):
+        long_at = long_ref[step * 128 * REFS : (step + 1) * 128 * REFS]
+        short_at = short_ref[step * 64 * REFS : (step + 1) * 64 * REFS]
         long = dot(one_hot(long_at == outer_lane), outer)
         short = dot(one_hot(short_at == middle_lane), middle)
         pieces = []
-        for peer in range(8):
+        for peer in range(16):
             pieces.append(long[peer * 8 * REFS : (peer + 1) * 8 * REFS])
             pieces.append(short[peer * 4 * REFS : (peer + 1) * 4 * REFS])
         at = pl.ds(step * size, size)
@@ -143,18 +144,22 @@
         copy.wait()
 
 
-def fold_kernel(head_ref, out_hbm, value_hbm, fold_ref, out_ref, value_ref, sems):
+def fold_kernel(head_ref, out_hbm, keyval_hbm, query_hbm, fold_ref, query_ref, key_ref, out_ref, value_ref, sems):
     copies = []
     for view in range(2):
         copies.append(pltpu.make_async_copy(out_hbm.at[view], out_ref.at[view], sems.at[2 * view]))
         copies.append(
-            pltpu.make_async_copy(value_hbm.at[view, :, pl.ds(DD, DD)], value_ref.at[view], sems.at[2 * view + 1])
+            pltpu.make_async_copy(keyval_hbm.at[view, :, pl.ds(DD, DD)], value_ref.at[view], sems.at[2 * view + 1])
+        )
+        copies.append(pltpu.make_async_copy(query_hbm.at[view], query_ref.at[view], sems.at[4 + 2 * view]))
+        copies.append(
+            pltpu.make_async_copy(keyval_hbm.at[view, :, pl.ds(0, DD)], key_ref.at[view], sems.at[5 + 2 * view])
         )
     for copy in copies:
         copy.start()
     lane = lax.broadcasted_iota(jnp.int32, (16, DD), 1)
     for view in range(2):
-        copies[2 * view].wait()
+        copies[4 * view].wait()
         both = dot_nt(head_ref[view], out_ref[view])
         high = both.astype(BF16).astype(F32)
         low = (both - high).astype(BF16).astype(F32)
@@ -162,13 +167,16 @@
         left = jnp.concatenate(
             [jnp.where(lane // HD == head, pair, 0.0).astype(BF16) for head in range(HEADS)], axis=0
         )
-        copies[2 * view + 1].wait()
+        copies[4 * view + 1].wait()
         full = dot_nt(left, value_ref[view])
         for head in range(HEADS):
             term = full[head * 16 : head * 16 + 8] + full[head * 16 + 8 : head * 16 + 16]
             top = term.astype(BF16).astype(F32)
             rest = term - top
             fold_ref[view, head * 16 : head * 16 + 16] = jnp.concatenate([top, rest], axis=0).astype(BF16)
+    for view in range(2):
+        copies[4 * view + 2].wait()
+        copies[4 * view + 3].wait()
 
 
 def view_gradients(outs, geo, par):
@@ -212,17 +220,9 @@
 
 
 def decode_kernel(
-    rows_ref, query_hbm, key_hbm, fold_ref, head_ref, geo_ref, par_ref,
-    points_ref, grad_ref, o_ref, query_ref, key_ref, x_ref, n_ref, q_ref, k_ref, u_ref, e_ref, sems,
+    rows_ref, query_ref, key_ref, fold_ref, head_ref, geo_ref, par_ref,
+    points_ref, grad_ref, o_ref, x_ref, n_ref, q_ref, k_ref, u_ref, e_ref,
 ):
-    copies = []
-    for view in range(2):
-        copies.append(pltpu.make_async_copy(query_hbm.at[view], query_ref.at[view], sems.at[2 * view]))
-        copies.append(
-            pltpu.make_async_copy(key_hbm.at[view, :, pl.ds(0, DD)], key_ref.at[view], sems.at[2 * view + 1])
-        )
-    for copy in copies:
-        copy.start()
     order = gather_order()
     size = 4 * REFS * PIECE
     for part in range(PEERS // 4):
@@ -257,9 +257,7 @@
     factor = math.log2(math.e) / math.sqrt(HD)
 
     def project(view):
-        copies[2 * view].wait()
         q_ref[view] = dot(n_ref[view], query_ref[view]).astype(BF16)
-        copies[2 * view + 1].wait()
         k_ref[view] = dot(n_ref[1 - view], key_ref[view]).astype(BF16)
 
     def scores_of(view, pair, four):
@@ -399,20 +397,21 @@
     spread = exchange(message, "dev")
 
     head_rows = jnp.pad(jnp.swapaxes(point_heads, 1, 2), ((0, 0), (0, 12), (0, 0)))
-    fold = pl.pallas_call(
+    square = shape((2, DD, DD), BF16)
+    fold, query, key = pl.pallas_call(
         fold_kernel,
-        in_specs=[inside, outside, outside],
-        out_specs=inside,
-        out_shape=shape((2, HEADS * 16, DD), BF16),
+        in_specs=[inside, outside, outside, outside],
+        out_specs=(inside, inside, inside),
+        out_shape=(shape((2, HEADS * 16, DD), BF16), square, square),
         scratch_shapes=[
             pltpu.VMEM((2, DD, DD), BF16),
             pltpu.VMEM((2, DD, DD), BF16),
-            pltpu.SemaphoreType.DMA((4,)),
+            pltpu.SemaphoreType.DMA((8,)),
         ],
         compiler_params=params_for(20),
         cost_estimate=pl.CostEstimate(flops=2000000000, bytes_accessed=6000000, transcendentals=0),
         name="fold",
-    )(head_rows, hbm(cross_out), hbm(cross_keyval))
+    )(head_rows, hbm(cross_out), hbm(cross_keyval), hbm(cross_query))
 
     graph = pair_graph[0].reshape(PEERS * REFS)
     base = (graph // 2) * 8
@@ -426,34 +425,30 @@
         in_specs=[inside] * 4 + [pl.BlockSpec(memory_space=pl.ANY)],
         out_specs=(outside, inside),
         out_shape=(shape((count, WIDE), BF16), shape((REFS, 256), F32)),
-        scratch_shapes=[pltpu.VMEM((count, WIDE), BF16), pltpu.SemaphoreType.DMA((PEERS // 8,))],
+        scratch_shapes=[pltpu.VMEM((count, WIDE), BF16), pltpu.SemaphoreType.DMA((PEERS // 16,))],
         compiler_params=params_for(20),
         name="select",
     )(spread, long_rows.reshape(-1, 1), short_rows.reshape(-1, 1), own, fold)
     rows = exchange(outgoing, "dev")
 
-    weights = pltpu.VMEM((2, DD, DD), BF16)
     tokens_of = pltpu.VMEM((2, PAIRS * TOK, DD), BF16)
     points, grads = pl.pallas_call(
         decode_kernel,
-        in_specs=[inside] + [outside] * 2 + [inside] * 4,
+        in_specs=[inside] * 7,
         out_specs=(inside, inside),
         out_shape=(shape((REFS, 4, TOK), F32), shape((PEERS * REFS, 256), BF16)),
         scratch_shapes=[
             pltpu.VMEM((4, REFS, TOK), F32),
-            weights,
-            weights,
             tokens_of,
             tokens_of,
             tokens_of,
             tokens_of,
             pltpu.VMEM((2, PAIRS, HEADS * 16, TOK), BF16),
             pltpu.VMEM((2, PAIRS, 8, TOK), F32),
-            pltpu.SemaphoreType.DMA((4,)),
         ],
-        compiler_params=params_for(32),
+        compiler_params=params_for(28),
         name="decode",
-    )(rows, hbm(cross_query), hbm(cross_keyval), fold, head_rows, my_geo, jnp.repeat(pair_params[0], 2, axis=0))
+    )(rows, query, key, fold, head_rows, my_geo, jnp.repeat(pair_params[0], 2, axis=0))
 
     own_grad, square = pl.pallas_call(
         combine_kernel,

time: 141 us -> 139 us (0.986)
  waiting for transfers between devices: 20.6 us -> 17.4 us
  local copies, waits for them, and re-layouts: 1 us -> 3.83 us
  Pallas kernels: 25.3 us -> 23.3 us
    all_to_all x2, waiting for transfers between devices: 20.6 us -> 17.4 us  [exchange(): return lax.all_to_all(x, axis, split_axis=0, concat_axis=0, tiled=True)]
    unnamed x11 -> x19, local copies, waits for them, and re-layouts: 0.14 us -> 2.98 us
    pallas_call x2, Pallas kernels: 17.2 us -> 15.7 us  [the longest x1 11.8 us: on_device(): pl.pallas_call(decode_kernel, in_specs=[inside] * 7, out_specs=(inside, i...]
where the time goes in v5:
time: 139 us
  blocking collectives  73 us (53%)
  Pallas kernels  23.3 us (17%)
  starting transfers between devices  20 us (14%)
  waiting for transfers between devices  17.4 us (13%)
  local copies, waits for them, and re-layouts  3.83 us (3%)
    all_to_all x2, blocking collectives, exchange(): return lax.all_to_all(x, axis, split_axis=0, concat_axis=0, tiled=True)  73 us
    all_to_all x2, starting transfers between devices, exchange(): return lax.all_to_all(x, axis, split_axis=0, concat_axis=0, tiled=True)  20 us
    all_to_all x2, waiting for transfers between devices, exchange(): return lax.all_to_all(x, axis, split_axis=0, concat_axis=0, tiled=True)  17.4 us
    pallas_call x1, Pallas kernels, on_device(): pl.pallas_call(decode_kernel, in_specs=[inside] * 7, out_specs=(inside, i...  11.8 us
    pallas_call x1, Pallas kernels, on_device(): pl.pallas_call(fold_kernel, in_specs=[inside, outside, outside, outside],...  3.92 us
    pallas_call x1, Pallas kernels, on_device(): pl.pallas_call(embed_kernel, in_specs=[outside] * 5, out_specs=outside, o...  3.9 us
    unnamed x19, local copies, waits for them, and re-layouts  2.98 us
  transfers between devices with their start and end apart: 2, of which 2 were waited for; matrix products, arithmetic and copies ran while one was open for 1% of the time, Pallas kernels for 3%

profile of v5, /device:TPU:1, one launch (start us, length us, event | category | flops | bytes accessed | tf_op | source)
XLA Modules:
  0.0 138.7 jit_solution(14007720551851544870)
XLA Ops:
  0.6 0.0 copy-start.8
  0.6 3.9 %embed.1 = bf16[256,1280]{1,0:T(8,128)(2,1)} custom-call(bf16[384,1024]{1,0:T(8,128)(2,1)} %bitcast.36, bf16[1024,768]{1,0:T(8,128)(2,1)} %weight_hbm.1, bf16[2,192]{1,0:T(2,128)(2,1)} %bitcast.31, bf16[2,12]{1,0:T(2,128)(2,1)} %bitcast.34, bf16[1,2]{1,0:T(2,128)(2,1)} %focal_hbm.1), custom_call_target="tpu_custom_call" | custom-call | tf_op jit(solution)/shard_map/embed/pallas_call | solution.py:379
  4.5 0.0 copy-start.7
  4.6 12.0 %all-to-all-start = ((bf16[32,8,1280]{2,1,0:T(8,128)(2,1)}), bf16[32,8,1280]{2,1,0:T(8,128)(2,1)S(1)}, u32[]{:S(2)}, u32[]{:S(2)}) async-start(bf16[32,8,1280]{2,1,0:T(8,128)(2,1)} %bitcast.3), calls=%async_computation | async-start | bytes 1310720 | tf_op jit(solution)/shard_map/all_to_all | solution.py:375
  16.6 0.0 copy-done.8
  16.6 0.1 copy.22
  16.7 0.1 reshape_squeeze.7
  16.9 0.1 fusion.2
  17.0 0.1 copy.25.own_ref
  17.1 0.1 iota_add_fusion
  17.2 0.2 add.115.short_ref
  17.4 0.1 iota_add_fusion.1
  17.5 0.3 add.114.long_ref
  17.8 0.0 copy-done.7
  17.8 3.9 %fold.1 = (bf16[2,192,768]{2,1,0:T(8,128)(2,1)S(1)}, bf16[2,768,768]{2,1,0:T(8,128)(2,1)S(1)}, bf16[2,768,768]{2,1,0:T(8,128)(2,1)S(1)}) custom-call(bf16[2,16,768]{2,1,0:T(8,128)(2,1)S(1)} %pad.9.head_ref, bf16[2,768,768]{2,1,0:T(8,128)(2,1)} %out_hbm.1, bf16[2,768,1536]{2,1,0:T(8,128)(2,1)} %keyval_hbm.1, bf16[2,768,768]{2,1,0:T(8,128)(2,1)} %query_hbm.1), custom_call_target="tpu_custom_call" | custom-call | flops 2000000000 | bytes 6000000 | tf_op jit(solution)/shard_map/fold/pallas_call | solution.py:401
  21.8 0.0 copy-start
  21.8 1.4 %copy-done = bf16[2,768,768]{2,1,0:T(8,128)(2,1)} copy-done((bf16[2,768,768]{2,1,0:T(8,128)(2,1)}, bf16[2,768,768]{2,1,0:T(8,128)(2,1)S(1)}, u32[]{:S(2)}) %copy-start) | copy-done | bytes 2359320
  23.2 0.0 copy-start.2
  23.2 1.4 %copy-done.2 = bf16[2,768,768]{2,1,0:T(8,128)(2,1)} copy-done((bf16[2,768,768]{2,1,0:T(8,128)(2,1)}, bf16[2,768,768]{2,1,0:T(8,128)(2,1)S(1)}, u32[]{:S(2)}) %copy-start.2) | copy-done | bytes 2359320
  24.6 8.4 %all-to-all-done = bf16[32,8,1280]{2,1,0:T(8,128)(2,1)S(1)} async-done(((bf16[32,8,1280]{2,1,0:T(8,128)(2,1)}), bf16[32,8,1280]{2,1,0:T(8,128)(2,1)S(1)}, u32[]{:S(2)}, u32[]{:S(2)}) %all-to-all-start) | async-done | bytes 655392 | tf_op jit(solution)/shard_map/all_to_all | solution.py:375
  33.0 0.0 copy-start.4
  33.0 2.5 %select.48 = (bf16[3072,384]{1,0:T(8,128)(2,1)S(1)}, f32[8,256]{1,0:T(8,128)S(1)}) custom-call(bf16[256,1280]{1,0:T(8,128)(2,1)S(1)} %bitcast.24, s32[2048,1]{1,0:T(8,128)S(1)} %add.114.long_ref, s32[1024,1]{1,0:T(8,128)S(1)} %add.115.short_ref, s32[16,1]{1,0:T(8,128)S(1)} %copy.25.own_ref, bf16[2,192,768]{2,1,0:T(8,128)(2,1)S(1)} %get-tuple-element.16.after_ref.fold_ref), custom_call_target="tpu_custom_call" | custom-call | tf_op jit(solution)/shard_map/select/pallas_call | solution.py:423
  35.5 0.0 copy-start.1
  35.5 0.0 copy-start.3
  35.5 62.0 %all_to_all.44 = bf16[32,96,384]{2,1,0:T(8,128)(2,1)S(1)} all-to-all(bf16[32,96,384]{2,1,0:T(8,128)(2,1)S(1)} %bitcast.25), channel_id=1, replica_groups=mesh['grp'=8,'dev'=32] {'dev'}, dimensions={0} | all-to-all | bytes 4718592 | tf_op jit(solution)/shard_map/all_to_all | solution.py:375
  97.6 0.0 copy-done.4
  97.6 0.0 copy-done.1
  97.6 0.0 copy-done.3
  97.6 0.0 copy-start.5
  97.6 0.0 copy-start.6
  97.6 11.8 %decode.1 = (f32[8,4,192]{2,1,0:T(4,128)}, bf16[256,256]{1,0:T(8,128)(2,1)}) custom-call(bf16[3072,384]{1,0:T(8,128)(2,1)S(1)} %bitcast.23, bf16[2,768,768]{2,1,0:T(8,128)(2,1)S(1)} %copy-done.1, bf16[2,768,768]{2,1,0:T(8,128)(2,1)S(1)} %copy-done.3, bf16[2,192,768]{2,1,0:T(8,128)(2,1)S(1)} %get-tuple-element.16.after_ref.fold_ref, ...), custom_call_target="tpu_custom_call" | custom-call | tf_op jit(solution)/shard_map/decode/pallas_call | solution.py:435
  109.4 8.0 %all-to-all-start.2 = ((bf16[32,8,256]{2,1,0:T(8,128)(2,1)}), bf16[32,8,256]{2,1,0:T(8,128)(2,1)S(1)}, u32[]{:S(2)}, u32[]{:S(2)}) async-start(bf16[32,8,256]{2,1,0:T(8,128)(2,1)} %bitcast.13), calls=%async_computation.2 | async-start | bytes 262144 | tf_op jit(solution)/shard_map/all_to_all | solution.py:375
  117.4 0.1 reshape_reshape_squeeze.3.graph_ref
  117.6 9.0 %all-to-all-done.2 = bf16[32,8,256]{2,1,0:T(8,128)(2,1)S(1)} async-done(((bf16[32,8,256]{2,1,0:T(8,128)(2,1)}), bf16[32,8,256]{2,1,0:T(8,128)(2,1)S(1)}, u32[]{:S(2)}, u32[]{:S(2)}) %all-to-all-start.2) | async-done | bytes 131104 | tf_op jit(solution)/shard_map/all_to_all | solution.py:375
  126.6 0.4 combine.1
  127.0 10.9 %all_to_all.45 = f32[8,1,128]{2,1,0:T(1,128)S(1)} all-to-all(f32[8,1,128]{2,1,0:T(1,128)S(1)} %bitcast.33), channel_id=1, replica_groups=mesh['grp'=8,'dev'=32] {'grp'}, dimensions={0} | all-to-all | bytes 8192 | tf_op jit(solution)/shard_map/all_to_all | solution.py:375
  137.9 0.0 copy-done.5
  137.9 0.0 copy-done.6
  137.9 0.7 update.1
  (5 shorter events, 0.0 us)
Async XLA Ops:
  0.6 16.0 %copy-start.8 = (s32[1,128,2]{1,2,0:T(2,128)S(1)}, s32[1,128,2]{1,2,0:T(2,128)}, u32[]{:S(2)}) copy-start(s32[1,128,2]{1,2,0:T(2,128)} %param.15) | copy-start | bytes 3076
  4.5 13.3 %copy-start.7 = (bf16[2,768,4]{1,2,0:T(4,128)(2,1)S(1)}, bf16[2,768,4]{1,2,0:T(4,128)(2,1)}, u32[]{:S(2)}) copy-start(bf16[2,768,4]{1,2,0:T(4,128)(2,1)} %param.21) | copy-start | bytes 36868
  4.6 28.4 %all-to-all-start = ((bf16[32,8,1280]{2,1,0:T(8,128)(2,1)}), bf16[32,8,1280]{2,1,0:T(8,128)(2,1)S(1)}, u32[]{:S(2)}, u32[]{:S(2)}) async-start(bf16[32,8,1280]{2,1,0:T(8,128)(2,1)} %bitcast.3), calls=%async_computation | async-start | bytes 1310720 | tf_op jit(solution)/shard_map/all_to_all | solution.py:375
  21.8 1.4 %copy-start = (bf16[2,768,768]{2,1,0:T(8,128)(2,1)}, bf16[2,768,768]{2,1,0:T(8,128)(2,1)S(1)}, u32[]{:S(2)}) copy-start(bf16[2,768,768]{2,1,0:T(8,128)(2,1)S(1)} %get-tuple-element.18.query_ref) | copy-start | bytes 7077892
  23.2 1.4 %copy-start.2 = (bf16[2,768,768]{2,1,0:T(8,128)(2,1)}, bf16[2,768,768]{2,1,0:T(8,128)(2,1)S(1)}, u32[]{:S(2)}) copy-start(bf16[2,768,768]{2,1,0:T(8,128)(2,1)S(1)} %get-tuple-element.19.key_ref) | copy-start | bytes 7077892
  33.0 64.6 %copy-start.4 = (f32[1,4,13]{2,1,0:T(4,128)S(1)}, f32[1,4,13]{2,1,0:T(4,128)}, u32[]{:S(2)}) copy-start(f32[1,4,13]{2,1,0:T(4,128)} %param.16) | copy-start | bytes 628
  35.5 62.1 %copy-start.1 = (bf16[2,768,768]{2,1,0:T(8,128)(2,1)S(1)}, bf16[2,768,768]{2,1,0:T(8,128)(2,1)}, u32[]{:S(2)}) copy-start(bf16[2,768,768]{2,1,0:T(8,128)(2,1)} %copy-done) | copy-start | bytes 7077892
  35.5 62.1 %copy-start.3 = (bf16[2,768,768]{2,1,0:T(8,128)(2,1)S(1)}, bf16[2,768,768]{2,1,0:T(8,128)(2,1)}, u32[]{:S(2)}) copy-start(bf16[2,768,768]{2,1,0:T(8,128)(2,1)} %copy-done.2) | copy-start | bytes 7077892
  97.6 40.3 %copy-start.5 = (bf16[1,2,192]{2,1,0:T(2,128)(2,1)S(1)}, bf16[1,2,192]{2,1,0:T(2,128)(2,1)}, u32[]{:S(2)}) copy-start(bf16[1,2,192]{2,1,0:T(2,128)(2,1)} %param.13) | copy-start | bytes 2308
  97.6 40.3 %copy-start.6 = (bf16[1,2,12]{2,1,0:T(2,128)(2,1)S(1)}, bf16[1,2,12]{2,1,0:T(2,128)(2,1)}, u32[]{:S(2)}) copy-start(bf16[1,2,12]{2,1,0:T(2,128)(2,1)} %param.14) | copy-start | bytes 148
  109.4 17.1 %all-to-all-start.2 = ((bf16[32,8,256]{2,1,0:T(8,128)(2,1)}), bf16[32,8,256]{2,1,0:T(8,128)(2,1)S(1)}, u32[]{:S(2)}, u32[]{:S(2)}) async-start(bf16[32,8,256]{2,1,0:T(8,128)(2,1)} %bitcast.13), calls=%async_computation.2 | async-start | bytes 262144 | tf_op jit(solution)/shard_map/all_to_all | solution.py:375

commit v6 on v5

--- a/solution.py
+++ b/solution.py
@@ -3,9 +3,11 @@
 
 import jax
 import jax.numpy as jnp
+import numpy as np
 from jax import lax
 from jax.experimental import pallas as pl
 from jax.experimental.pallas import tpu as pltpu
+from jax.sharding import Mesh
 from jax.sharding import PartitionSpec as P
 
 HEADS = 12
@@ -21,6 +23,9 @@
 GROUPS = 3
 LOW = 32
 
+PLANE = ("x", "c", "y")
+HOME = [(rank * 8 + z, z * PEERS + rank) for rank in range(PEERS) for z in range(8)]
+
 norm_eps = 1e-06
 stat_eps = 1e-06
 step_rate = 0.3
@@ -67,8 +72,8 @@
     return one_hot(came == lax.broadcasted_iota(jnp.int32, (size, size), 1))
 
 
-def embed_kernel(tokens_hbm, weight_hbm, depth_hbm, camera_hbm, focal_hbm, out_hbm,
-                 tokens_ref, weight_ref, depth_ref, camera_ref, focal_ref, emb_ref, out_ref, sems):
+def embed_kernel(tokens_hbm, weight_hbm, depth_hbm, camera_hbm, focal_hbm, graph_hbm, par_hbm, out_hbm,
+                 tokens_ref, weight_ref, depth_ref, camera_ref, focal_ref, graph_ref, par_ref, emb_ref, out_ref, sems):
     copies = [
         pltpu.make_async_copy(tokens_hbm, tokens_ref, sems.at[0]),
         pltpu.make_async_copy(weight_hbm.at[:, pl.ds(0, WIDE)], weight_ref.at[0], sems.at[1]),
@@ -76,6 +81,8 @@
         pltpu.make_async_copy(depth_hbm, depth_ref, sems.at[3]),
         pltpu.make_async_copy(camera_hbm, camera_ref, sems.at[4]),
         pltpu.make_async_copy(focal_hbm, focal_ref, sems.at[5]),
+        pltpu.make_async_copy(graph_hbm, graph_ref, sems.at[10]),
+        pltpu.make_async_copy(par_hbm, par_ref, sems.at[11]),
     ]
     for copy in copies:
         copy.start()
@@ -92,7 +99,14 @@
         tail = jnp.where(lane == 64 + i, camera[:, i : i + 1], tail)
     tail = jnp.where(lane == 76, jnp.where(upper, focal[:, 0:1], focal[:, 1:2]), tail)
     head = depth[:, 0:128]
-    geo = jnp.concatenate([head[0:1], tail[0:1], head[1:2], tail[1:2], jnp.zeros((4, 128), F32)], axis=0)
+    par = jnp.concatenate([par_ref[...], jnp.zeros((PAIRS, 3), F32)], axis=1)
+    par = jnp.concatenate([par[pair : pair + 1] for pair in range(PAIRS)], axis=1)
+    high = par.astype(BF16).astype(F32)
+    middle = (par - high).astype(BF16).astype(F32)
+    last = jnp.concatenate([par - high - middle, jnp.zeros((1, 64), F32)], axis=1)
+    par = jnp.concatenate([high, middle], axis=1)
+    pairs = graph_ref[...].astype(F32)
+    geo = jnp.concatenate([head[0:1], tail[0:1], head[1:2], tail[1:2], pairs, par, last], axis=0)
     geo = jnp.concatenate([geo, geo], axis=0).astype(BF16)
     for two in range(PEERS // 2):
         out_ref[two * 16 : two * 16 + 16, GROUPS * WIDE :] = geo
@@ -114,8 +128,38 @@
         send.wait()
 
 
-def select_kernel(rows_ref, long_ref, short_ref, own_ref, after_ref, out_hbm, geo_ref, out_ref, sems):
+def index_kernel(rank_ref, tile_ref, long_ref, short_ref, own_ref, graph_ref):
+    rank = rank_ref[0]
+    total = PEERS * 8
+    ids = tile_ref[...].astype(F32)[4:6].astype(jnp.int32)
+    owner = ids >> 1
+    place = (owner & 7) * 4 + (owner >> 3)
+    odd = ids & 1
+    table = jnp.concatenate([place * 8 + odd * total, place * 8 + odd * 4, place * 8 + odd * 2, ids], axis=0)
+    table = jnp.concatenate([table, table], axis=0).astype(F32).astype(BF16)
+
+    def looked_up(first, count, per_pair, shift, column):
+        row = lax.broadcasted_iota(jnp.int32, (count, 128), 0) + first
+        lane = lax.broadcasted_iota(jnp.int32, (count, 128), 1)
+        found = dot_nt(one_hot((row >> per_pair) == lane), table)
+        slot = (lax.broadcasted_iota(jnp.int32, (count, 1), 0) >> shift) & 1
+        return jnp.where(slot == 1, found[:, column + 1 : column + 2], found[:, column : column + 1]).astype(jnp.int32)
+
+    long_row = lax.broadcasted_iota(jnp.int32, (8 * total, 1), 0) & 7
+    short_row = lax.broadcasted_iota(jnp.int32, (4 * total, 1), 0) & 3
+    long_ref[...] = looked_up(0, 8 * total, 4, 3, 0) + long_row
+    short_ref[...] = looked_up(0, 4 * total, 3, 2, 2) + short_row
+    own_ref[...] = looked_up(rank * REFS, 16, 1, 0, 4)
+    lane = lax.broadcasted_iota(jnp.int32, (128, 256), 1)
+    pair = lax.broadcasted_iota(jnp.int32, (128, 256), 0)
+    spread = [dot(table, one_hot(lane == 2 * pair + slot))[6 + slot : 7 + slot] for slot in range(2)]
+    graph_ref[...] = (spread[0] + spread[1]).astype(jnp.int32)
+
+
+def select_kernel(rank_ref, rows_ref, long_ref, short_ref, own_ref, after_ref, out_hbm, geo_ref, par_ref, out_ref, sems):
+    rank = rank_ref[0]
     total = rows_ref.shape[0]
+    tile = rows_ref[:, GROUPS * WIDE :]
     outer = jnp.concatenate([rows_ref[:, 0:WIDE], rows_ref[:, 2 * WIDE : 3 * WIDE]], axis=0)
     middle = rows_ref[:, WIDE : 2 * WIDE]
     outer_lane = lax.broadcasted_iota(jnp.int32, (128 * REFS, 2 * total), 1)
@@ -138,8 +182,16 @@
     own_lane = lax.broadcasted_iota(jnp.int32, (16, total), 1)
     own = own_ref[...]
     for half in range(2):
-        found = dot(one_hot(own + half == own_lane), rows_ref[:, GROUPS * WIDE :])
+        found = dot(one_hot(own + half == own_lane), tile)
         geo_ref[:, half * 128 : half * 128 + 128] = found[0:REFS]
+    mine = ((rank & 7) * 4 + (rank >> 3)) * 8 + 6
+    row = lax.broadcasted_iota(jnp.int32, (16, total), 0)
+    par = dot(one_hot((row < 2) & (own_lane == mine + row)), tile)
+    par = par[0:1] + pltpu.roll(par[0:1], 64, 1) + par[1:2]
+    views = []
+    for pair in range(PAIRS):
+        views += [par if pair == 0 else pltpu.roll(par, 128 - 16 * pair, 1)] * 2
+    par_ref[...] = jnp.concatenate(views, axis=0)
     for copy in copies:
         copy.wait()
 
@@ -345,7 +397,10 @@
     own_ref[...] = summed(own_image | own_pair)[0]
 
 
-def update_kernel(count, square_ref, own_ref, depth_ref, camera_ref, par_ref, depth_out, camera_out, par_out):
+def update_kernel(
+    count, square_ref, own_ref, depth_ref, camera_ref, par_ref, points_ref, depth_out, camera_out, par_out, points_out
+):
+    points_out[...] = points_ref[...]
     total = jnp.sum(square_ref[...], axis=0, keepdims=True)[:, 0:1]
     step = step_rate / jnp.sqrt(total / count + stat_eps)
     depth_out[...] = depth_ref[...].astype(F32) - step * own_ref[0:2, 0:TOK]
@@ -365,8 +420,8 @@
     enc_tokens, focal_len, depth_map, cameras, pair_graph, pair_params,
     embed_weight, cross_query, cross_keyval, cross_out, point_heads,
 ):
-    me = lax.axis_index("dev")
-    groups = lax.axis_size("grp")
+    rank = lax.axis_index(PLANE)
+    groups = lax.axis_size("z")
     inside = pl.BlockSpec(memory_space=pltpu.VMEM)
     outside = pl.BlockSpec(memory_space=pltpu.HBM)
     scalar = pl.BlockSpec(memory_space=pltpu.SMEM)
@@ -378,7 +433,7 @@
     message_dims = (PEERS * 8, GROUPS * WIDE + 128)
     message = pl.pallas_call(
         embed_kernel,
-        in_specs=[outside] * 5,
+        in_specs=[outside] * 7,
         out_specs=outside,
         out_shape=shape(message_dims, BF16),
         scratch_shapes=[
@@ -387,14 +442,33 @@
             pltpu.VMEM((2, TOK), BF16),
             pltpu.VMEM((2, 12), BF16),
             pltpu.VMEM((1, 2), BF16),
+            pltpu.VMEM((2, 128), jnp.int32),
+            pltpu.VMEM((PAIRS, 13), F32),
             pltpu.VMEM((2 * TOK, WIDE), BF16),
             pltpu.VMEM(message_dims, BF16),
-            pltpu.SemaphoreType.DMA((10,)),
+            pltpu.SemaphoreType.DMA((12,)),
         ],
         compiler_params=params_for(24),
         name="embed",
-    )(hbm(tokens), hbm(embed_weight), hbm(depth_map[0]), hbm(cameras[0]), hbm(focal_len))
-    spread = exchange(message, "dev")
+    )(hbm(tokens), hbm(embed_weight), hbm(depth_map[0]), hbm(cameras[0]), hbm(focal_len),
+      hbm(jnp.swapaxes(pair_graph[0], 0, 1)), hbm(pair_params[0]))
+    across = exchange(message, ("x", "c"))
+    tile = lax.dynamic_slice(across, (lax.axis_index("z") * PEERS, GROUPS * WIDE), (8, 128))
+    spread = exchange(across, ("z", "y"))
+    long_rows, short_rows, own, graph = pl.pallas_call(
+        index_kernel,
+        in_specs=[scalar, inside],
+        out_specs=(inside,) * 4,
+        out_shape=(
+            shape((PEERS * REFS * 8, 1), jnp.int32),
+            shape((PEERS * REFS * 4, 1), jnp.int32),
+            shape((16, 1), jnp.int32),
+            shape((1, PEERS * REFS), jnp.int32),
+        ),
+        compiler_params=params_for(20),
+        cost_estimate=pl.CostEstimate(flops=500000000, bytes_accessed=2000000, transcendentals=0),
+        name="index",
+    )(rank.reshape(1), tile)
 
     head_rows = jnp.pad(jnp.swapaxes(point_heads, 1, 2), ((0, 0), (0, 12), (0, 0)))
     square = shape((2, DD, DD), BF16)
@@ -413,23 +487,21 @@
         name="fold",
     )(head_rows, hbm(cross_out), hbm(cross_keyval), hbm(cross_query))
 
-    graph = pair_graph[0].reshape(PEERS * REFS)
-    base = (graph // 2) * 8
-    long_rows = (base + (graph % 2) * (PEERS * 8))[:, None] + jnp.arange(8, dtype=jnp.int32)
-    short_rows = (base + (graph % 2) * 4)[:, None] + jnp.arange(4, dtype=jnp.int32)
-    mine = lax.dynamic_slice_in_dim(graph, me * REFS, REFS)
-    own = jnp.pad((mine // 2) * 8 + 2 * (mine % 2), (0, 8))[:, None]
     count = PEERS * REFS * PIECE
-    outgoing, my_geo = pl.pallas_call(
+    outgoing, my_geo, view_par = pl.pallas_call(
         select_kernel,
-        in_specs=[inside] * 4 + [pl.BlockSpec(memory_space=pl.ANY)],
-        out_specs=(outside, inside),
-        out_shape=(shape((count, WIDE), BF16), shape((REFS, 256), F32)),
+        in_specs=[scalar] + [inside] * 4 + [pl.BlockSpec(memory_space=pl.ANY)],
+        out_specs=(outside, inside, inside),
+        out_shape=(
+            shape((count, WIDE), BF16),
+            shape((REFS, 256), F32),
+            shape((REFS, 128), F32),
+        ),
         scratch_shapes=[pltpu.VMEM((count, WIDE), BF16), pltpu.SemaphoreType.DMA((PEERS // 16,))],
-        compiler_params=params_for(20),
+        compiler_params=params_for(28),
         name="select",
-    )(spread, long_rows.reshape(-1, 1), short_rows.reshape(-1, 1), own, fold)
-    rows = exchange(outgoing, "dev")
+    )(rank.reshape(1), spread, long_rows, short_rows, own, fold)
+    rows = exchange(outgoing, PLANE)
 
     tokens_of = pltpu.VMEM((2, PAIRS * TOK, DD), BF16)
     points, grads = pl.pallas_call(
@@ -448,7 +520,7 @@
         ],
         compiler_params=params_for(28),
         name="decode",
-    )(rows, query, key, fold, head_rows, my_geo, jnp.repeat(pair_params[0], 2, axis=0))
+    )(rows, query, key, fold, head_rows, my_geo, view_par)
 
     own_grad, square = pl.pallas_call(
         combine_kernel,
@@ -456,14 +528,16 @@
         out_shape=(shape((16, 256), F32), shape((groups, 128), F32)),
         compiler_params=params_for(16),
         name="combine",
-    )(me.reshape(1), graph.reshape(1, -1), exchange(grads, "dev"))
+    )(rank.reshape(1), graph, exchange(grads, PLANE))
+    own_grad = lax.ppermute(own_grad, PLANE + ("z",), HOME)
+    points = lax.ppermute(points, PLANE + ("z",), HOME)
     total = groups * PEERS * (2 * (TOK + 12) + 13 * PAIRS)
-    new_depth, new_cameras, new_params = pl.pallas_call(
+    new_depth, new_cameras, new_params, points = pl.pallas_call(
         functools.partial(update_kernel, float(total)),
-        out_shape=(shape((2, TOK), F32), shape((2, 12), F32), shape((PAIRS, 13), F32)),
+        out_shape=(shape((2, TOK), F32), shape((2, 12), F32), shape((PAIRS, 13), F32), shape(points.shape, F32)),
         compiler_params=params_for(16),
         name="update",
-    )(exchange(square, "grp"), own_grad, depth_map[0], cameras[0], pair_params[0])
+    )(exchange(square, "z"), own_grad, depth_map[0], cameras[0], pair_params[0], points)
     return (
         points.reshape(1, PAIRS, 2, 4, TOK),
         new_depth[None],
@@ -473,13 +547,16 @@
 
 
 def solution(mesh):
+    axes = ("x", "c", "y", "z")
+    split = Mesh(np.asarray(mesh.devices).reshape(4, 2, 4, 8), axes)
+    grp, dev = ("x", "c"), ("y", "z")
     placed = (
-        P("grp", "dev", None, None),
-        P("grp", "dev"),
-        P("grp", "dev", None),
-        P("grp", "dev", None),
-        P("grp", None, None),
-        P("grp", "dev", None),
+        P(grp, dev, None, None),
+        P(grp, dev),
+        P(grp, dev, None),
+        P(grp, dev, None),
+        P(grp, None, None),
+        P(grp, dev, None),
         P(),
         P(),
         P(),
@@ -488,13 +565,13 @@
     )
     return jax.shard_map(
         on_device,
-        mesh=mesh,
+        mesh=split,
         in_specs=placed,
         out_specs=(
-            P("grp", "dev", None, None, None),
-            P("grp", "dev", None),
-            P("grp", "dev", None),
-            P("grp", "dev", None),
+            P(grp, dev, None, None, None),
+            P(grp, dev, None),
+            P(grp, dev, None),
+            P(grp, dev, None),
         ),
         check_vma=False,
     )

time: 139 us -> 135 us (0.971)
  blocking collectives: 73 us -> 56 us
  starting transfers between devices: 20 us -> 26.4 us
  waiting for transfers between devices: 17.4 us -> 21.2 us
  Pallas kernels: 23.3 us -> 25.7 us
    all_to_all x2, blocking collectives: 73 us -> 56 us  [exchange(): return lax.all_to_all(x, axis, split_axis=0, concat_axis=0, tiled=True)]
    ppermute x0 -> x2, starting transfers between devices: none -> 7.75 us  [the longest x1 4.74 us: on_device(): own_grad = lax.ppermute(own_grad, PLANE + ('z',), HOME)]
    all_to_all x2 -> x3, waiting for transfers between devices: 17.4 us -> 21.2 us  [exchange(): return lax.all_to_all(x, axis, split_axis=0, concat_axis=0, tiled=True)]
    pallas_call x2 -> x3, Pallas kernels: 6.42 us -> 8.29 us  [the longest x1 4.51 us: on_device(): pl.pallas_call(embed_kernel, in_specs=[outside] * 7, out_specs=outside, o...]
    all_to_all x2 -> x3, starting transfers between devices: 20 us -> 18.7 us  [exchange(): return lax.all_to_all(x, axis, split_axis=0, concat_axis=0, tiled=True)]
    unnamed x19 -> x16, local copies, waits for them, and re-layouts: 2.98 us -> 2.88 us
  transfers between devices with their start and end apart: 2 -> 5, of which waited for: 2 -> 3; matrix products, arithmetic and copies ran while one was open for 1% -> 1% of each run, Pallas kernels for 3% -> 5%
where the time goes in v6:
time: 135 us; the launch traced here: 134 us
  blocking collectives  56 us (41%)
  starting transfers between devices  26.4 us (20%)
  Pallas kernels  25.7 us (19%)
  waiting for transfers between devices  21.2 us (16%)
  local copies, waits for them, and re-layouts  3.57 us (3%)
    all_to_all x2, blocking collectives, exchange(): return lax.all_to_all(x, axis, split_axis=0, concat_axis=0, tiled=True)  56 us
    all_to_all x3, waiting for transfers between devices, exchange(): return lax.all_to_all(x, axis, split_axis=0, concat_axis=0, tiled=True)  21.2 us
    all_to_all x3, starting transfers between devices, exchange(): return lax.all_to_all(x, axis, split_axis=0, concat_axis=0, tiled=True)  18.7 us
    pallas_call x1, Pallas kernels, on_device(): pl.pallas_call(decode_kernel, in_specs=[inside] * 7, out_specs=(inside, i...  11.8 us
    ppermute x1, starting transfers between devices, on_device(): own_grad = lax.ppermute(own_grad, PLANE + ('z',), HOME)  4.74 us
    pallas_call x1, Pallas kernels, on_device(): pl.pallas_call(embed_kernel, in_specs=[outside] * 7, out_specs=outside, o...  4.51 us
    pallas_call x1, Pallas kernels, on_device(): pl.pallas_call(fold_kernel, in_specs=[inside, outside, outside, outside],...  3.92 us
    ppermute x1, starting transfers between devices, on_device(): points = lax.ppermute(points, PLANE + ('z',), HOME)  3.01 us
  transfers between devices with their start and end apart: 5, of which 3 were waited for; matrix products, arithmetic and copies ran while one was open for 1% of the time, Pallas kernels for 5%

profile of v6, /device:TPU:1, one launch (start us, length us, event | category | flops | bytes accessed | tf_op | source)
XLA Modules:
  0.0 133.7 jit_solution(13594547853444540329)
XLA Ops:
  0.6 0.0 copy-start.7
  0.6 4.5 %embed.1 = bf16[256,1280]{1,0:T(8,128)(2,1)S(1)} custom-call(bf16[384,1024]{1,0:T(8,128)(2,1)} %bitcast.37, bf16[1024,768]{1,0:T(8,128)(2,1)} %weight_hbm.1, bf16[2,192]{1,0:T(2,128)(2,1)} %bitcast.33, bf16[2,12]{1,0:T(2,128)(2,1)} %bitcast.35, bf16[1,2]{1,0:T(2,128)(2,1)} %focal_hbm.1, s32[2,128]{1,0:T(2,128)} %bitcast.39, f32[4,13]{1,0:T(4,128)} %bitcast.31), custom_call_target="tpu_custom_call" | custom-call | tf_op jit(solution)/shard_map/embed/pallas_call | solution.py:434
  5.2 17.3 %all_to_all.56 = bf16[8,32,1280]{2,1,0:T(8,128)(2,1)} all-to-all(bf16[8,32,1280]{2,1,0:T(8,128)(2,1)S(1)} %bitcast.27), channel_id=1, replica_groups=mesh['x'=4,'c'=2,'y'=4,'z'=8] {'x','c'}, dimensions={0} | all-to-all | bytes 1310720 | tf_op jit(solution)/shard_map/all_to_all | solution.py:430
  22.4 10.6 %all-to-all-start.1 = ((bf16[32,8,1280]{2,1,0:T(8,128)(2,1)}), bf16[32,8,1280]{2,1,0:T(8,128)(2,1)S(1)}, u32[]{:S(2)}, u32[]{:S(2)}) async-start(bf16[32,8,1280]{2,1,0:T(8,128)(2,1)} %bitcast.9), calls=%async_computation.1 | async-start | bytes 1310720 | tf_op jit(solution)/shard_map/all_to_all | solution.py:430
  33.0 0.0 copy-done.7
  33.0 3.9 %fold.1 = (bf16[2,192,768]{2,1,0:T(8,128)(2,1)S(1)}, bf16[2,768,768]{2,1,0:T(8,128)(2,1)S(1)}, bf16[2,768,768]{2,1,0:T(8,128)(2,1)S(1)}) custom-call(bf16[2,16,768]{2,1,0:T(8,128)(2,1)S(1)} %pad.4.head_ref, bf16[2,768,768]{2,1,0:T(8,128)(2,1)} %out_hbm.1, bf16[2,768,1536]{2,1,0:T(8,128)(2,1)} %keyval_hbm.1, bf16[2,768,768]{2,1,0:T(8,128)(2,1)} %query_hbm.1), custom_call_target="tpu_custom_call" | custom-call | flops 2000000000 | bytes 6000000 | tf_op jit(solution)/shard_map/fold/pallas_call | solution.py:475
  37.0 0.0 copy-start
  37.0 1.4 %copy-done = bf16[2,768,768]{2,1,0:T(8,128)(2,1)} copy-done((bf16[2,768,768]{2,1,0:T(8,128)(2,1)}, bf16[2,768,768]{2,1,0:T(8,128)(2,1)S(1)}, u32[]{:S(2)}) %copy-start) | copy-done | bytes 2359320
  38.4 0.0 copy-start.2
  38.4 1.4 %copy-done.2 = bf16[2,768,768]{2,1,0:T(8,128)(2,1)} copy-done((bf16[2,768,768]{2,1,0:T(8,128)(2,1)}, bf16[2,768,768]{2,1,0:T(8,128)(2,1)S(1)}, u32[]{:S(2)}) %copy-start.2) | copy-done | bytes 2359320
  39.8 0.7 constant_dynamic-slice_fusion.tile_ref
  40.5 1.1 index.1
  41.6 10.1 %all-to-all-done.1 = bf16[32,8,1280]{2,1,0:T(8,128)(2,1)S(1)} async-done(((bf16[32,8,1280]{2,1,0:T(8,128)(2,1)}), bf16[32,8,1280]{2,1,0:T(8,128)(2,1)S(1)}, u32[]{:S(2)}, u32[]{:S(2)}) %all-to-all-start.1) | async-done | bytes 655392 | tf_op jit(solution)/shard_map/all_to_all | solution.py:430
  51.8 2.7 %select.2 = (bf16[3072,384]{1,0:T(8,128)(2,1)S(1)}, f32[8,256]{1,0:T(8,128)S(1)}, f32[8,128]{1,0:T(8,128)S(1)}) custom-call(s32[1]{0:T(128)} %bitcast.rank_ref.me_ref, bf16[256,1280]{1,0:T(8,128)(2,1)S(1)} %bitcast.26, s32[2048,1]{1,0:T(8,128)S(1)} %get-tuple-element.23.long_ref, s32[1024,1]{1,0:T(8,128)S(1)} %get-tuple-element.24.short_ref, ...), custom_call_target="tpu_custom_call" | custom-call | tf_op jit(solution)/shard_map/select/pallas_call | solution.py:491
  54.4 0.0 copy-start.1
  54.4 0.0 copy-start.3
  54.5 38.7 %all_to_all.57 = bf16[32,96,384]{2,1,0:T(8,128)(2,1)S(1)} all-to-all(bf16[32,96,384]{2,1,0:T(8,128)(2,1)S(1)} %bitcast.28), channel_id=1, replica_groups=mesh['x'=4,'c'=2,'y'=4,'z'=8] {'x','c','y'}, dimensions={0} | all-to-all | bytes 4718592 | tf_op jit(solution)/shard_map/all_to_all | solution.py:430
  93.1 0.0 copy-done.1
  93.1 0.0 copy-done.3
  93.1 0.0 copy-start.4
  93.1 0.0 copy-start.5
  93.2 0.0 copy-start.6
  93.2 11.8 %decode.1 = (f32[8,4,192]{2,1,0:T(4,128)S(1)}, bf16[256,256]{1,0:T(8,128)(2,1)}) custom-call(bf16[3072,384]{1,0:T(8,128)(2,1)S(1)} %bitcast.25, bf16[2,768,768]{2,1,0:T(8,128)(2,1)S(1)} %copy-done.1, bf16[2,768,768]{2,1,0:T(8,128)(2,1)S(1)} %copy-done.3, bf16[2,192,768]{2,1,0:T(8,128)(2,1)S(1)} %get-tuple-element.26.after_ref.fold_ref, ...), custom_call_target="tpu_custom_call" | custom-call | tf_op jit(solution)/shard_map/decode/pallas_call | solution.py:507
  105.0 4.1 %all-to-all-start.3 = ((bf16[32,8,256]{2,1,0:T(8,128)(2,1)}), bf16[32,8,256]{2,1,0:T(8,128)(2,1)S(1)}, u32[]{:S(2)}, u32[]{:S(2)}) async-start(bf16[32,8,256]{2,1,0:T(8,128)(2,1)} %bitcast.14), calls=%async_computation.3 | async-start | bytes 262144 | tf_op jit(solution)/shard_map/all_to_all | solution.py:430
  109.1 3.0 %collective-permute-start.1 = (f32[8,4,192]{2,1,0:T(4,128)S(1)}, f32[8,4,192]{2,1,0:T(4,128)S(1)}, u32[]{:S(2)}, u32[]{:S(2)}) collective-permute-start(f32[8,4,192]{2,1,0:T(4,128)S(1)} %get-tuple-element.35), channel_id=1, source_target_pairs={{0,0},{1,32},{2,64},{3,96},{4,128},{5,160},{6,192},{7,224},{8,1},{... | collective-permute-start | bytes 73736 | tf_op jit(solution)/shard_map/ppermute | solution.py:533
  112.1 4.7 %all-to-all-done.3 = bf16[32,8,256]{2,1,0:T(8,128)(2,1)S(1)} async-done(((bf16[32,8,256]{2,1,0:T(8,128)(2,1)}), bf16[32,8,256]{2,1,0:T(8,128)(2,1)S(1)}, u32[]{:S(2)}, u32[]{:S(2)}) %all-to-all-start.3) | async-done | bytes 131104 | tf_op jit(solution)/shard_map/all_to_all | solution.py:430
  116.8 1.0 combine.1
  117.8 4.7 %collective-permute-start = (f32[16,256]{1,0:T(8,128)S(1)}, f32[16,256]{1,0:T(8,128)S(1)}, u32[]{:S(2)}, u32[]{:S(2)}) collective-permute-start(f32[16,256]{1,0:T(8,128)S(1)} %get-tuple-element.34), channel_id=1, source_target_pairs={{0,0},{1,32},{2,64},{3,96},{4,128},{5,160},{6,192},{7,224},{8,1},{... | collective-permute-start | bytes 49160 | tf_op jit(solution)/shard_map/ppermute | solution.py:532
  122.5 4.0 %all-to-all-start.4 = ((f32[8,1,128]{2,1,0:T(1,128)}), f32[8,1,128]{2,1,0:T(1,128)S(1)}, u32[]{:S(2)}, u32[]{:S(2)}) async-start(f32[8,1,128]{2,1,0:T(1,128)} %bitcast.17), calls=%async_computation.4 | async-start | bytes 8192 | tf_op jit(solution)/shard_map/all_to_all | solution.py:430
  126.5 0.0 collective-permute-done.1.points_ref
  126.5 6.4 %all-to-all-done.4 = f32[8,1,128]{2,1,0:T(1,128)S(1)} async-done(((f32[8,1,128]{2,1,0:T(1,128)}), f32[8,1,128]{2,1,0:T(1,128)S(1)}, u32[]{:S(2)}, u32[]{:S(2)}) %all-to-all-start.4) | async-done | bytes 4128 | tf_op jit(solution)/shard_map/all_to_all | solution.py:430
  133.0 0.0 collective-permute-done.own_ref
  133.0 0.0 copy-done.4
  133.0 0.0 copy-done.5
  133.0 0.0 copy-done.6
  133.0 0.7 update.1
  (1 shorter events, 0.0 us)
Async XLA Ops:
  0.6 32.4 %copy-start.7 = (bf16[2,768,4]{1,2,0:T(4,128)(2,1)S(1)}, bf16[2,768,4]{1,2,0:T(4,128)(2,1)}, u32[]{:S(2)}) copy-start(bf16[2,768,4]{1,2,0:T(4,128)(2,1)} %param.21) | copy-start | bytes 36868
  22.4 29.3 %all-to-all-start.1 = ((bf16[32,8,1280]{2,1,0:T(8,128)(2,1)}), bf16[32,8,1280]{2,1,0:T(8,128)(2,1)S(1)}, u32[]{:S(2)}, u32[]{:S(2)}) async-start(bf16[32,8,1280]{2,1,0:T(8,128)(2,1)} %bitcast.9), calls=%async_computation.1 | async-start | bytes 1310720 | tf_op jit(solution)/shard_map/all_to_all | solution.py:430
  37.0 1.4 %copy-start = (bf16[2,768,768]{2,1,0:T(8,128)(2,1)}, bf16[2,768,768]{2,1,0:T(8,128)(2,1)S(1)}, u32[]{:S(2)}) copy-start(bf16[2,768,768]{2,1,0:T(8,128)(2,1)S(1)} %get-tuple-element.28.query_ref) | copy-start | bytes 7077892
  38.4 1.4 %copy-start.2 = (bf16[2,768,768]{2,1,0:T(8,128)(2,1)}, bf16[2,768,768]{2,1,0:T(8,128)(2,1)S(1)}, u32[]{:S(2)}) copy-start(bf16[2,768,768]{2,1,0:T(8,128)(2,1)S(1)} %get-tuple-element.29.key_ref) | copy-start | bytes 7077892
  54.4 38.7 %copy-start.1 = (bf16[2,768,768]{2,1,0:T(8,128)(2,1)S(1)}, bf16[2,768,768]{2,1,0:T(8,128)(2,1)}, u32[]{:S(2)}) copy-start(bf16[2,768,768]{2,1,0:T(8,128)(2,1)} %copy-done) | copy-start | bytes 7077892
  54.4 38.7 %copy-start.3 = (bf16[2,768,768]{2,1,0:T(8,128)(2,1)S(1)}, bf16[2,768,768]{2,1,0:T(8,128)(2,1)}, u32[]{:S(2)}) copy-start(bf16[2,768,768]{2,1,0:T(8,128)(2,1)} %copy-done.2) | copy-start | bytes 7077892
  93.1 39.8 %copy-start.4 = (f32[1,4,13]{2,1,0:T(4,128)S(1)}, f32[1,4,13]{2,1,0:T(4,128)}, u32[]{:S(2)}) copy-start(f32[1,4,13]{2,1,0:T(4,128)} %param.16) | copy-start | bytes 628
  93.1 39.8 %copy-start.5 = (bf16[1,2,192]{2,1,0:T(2,128)(2,1)S(1)}, bf16[1,2,192]{2,1,0:T(2,128)(2,1)}, u32[]{:S(2)}) copy-start(bf16[1,2,192]{2,1,0:T(2,128)(2,1)} %param.13) | copy-start | bytes 2308
  93.2 39.8 %copy-start.6 = (bf16[1,2,12]{2,1,0:T(2,128)(2,1)S(1)}, bf16[1,2,12]{2,1,0:T(2,128)(2,1)}, u32[]{:S(2)}) copy-start(bf16[1,2,12]{2,1,0:T(2,128)(2,1)} %param.14) | copy-start | bytes 148
  105.0 11.8 %all-to-all-start.3 = ((bf16[32,8,256]{2,1,0:T(8,128)(2,1)}), bf16[32,8,256]{2,1,0:T(8,128)(2,1)S(1)}, u32[]{:S(2)}, u32[]{:S(2)}) async-start(bf16[32,8,256]{2,1,0:T(8,128)(2,1)} %bitcast.14), calls=%async_computation.3 | async-start | bytes 262144 | tf_op jit(solution)/shard_map/all_to_all | solution.py:430
  109.1 17.4 %collective-permute-start.1 = (f32[8,4,192]{2,1,0:T(4,128)S(1)}, f32[8,4,192]{2,1,0:T(4,128)S(1)}, u32[]{:S(2)}, u32[]{:S(2)}) collective-permute-start(f32[8,4,192]{2,1,0:T(4,128)S(1)} %get-tuple-element.35), channel_id=1, source_target_pairs={{0,0},{1,32},{2,64},{3,96},{4,128},{5,160},{6,192},{7,224},{8,1},{... | collective-permute-start | bytes 73736 | tf_op jit(solution)/shard_map/ppermute | solution.py:533
  117.8 15.2 %collective-permute-start = (f32[16,256]{1,0:T(8,128)S(1)}, f32[16,256]{1,0:T(8,128)S(1)}, u32[]{:S(2)}, u32[]{:S(2)}) collective-permute-start(f32[16,256]{1,0:T(8,128)S(1)} %get-tuple-element.34), channel_id=1, source_target_pairs={{0,0},{1,32},{2,64},{3,96},{4,128},{5,160},{6,192},{7,224},{8,1},{... | collective-permute-start | bytes 49160 | tf_op jit(solution)/shard_map/ppermute | solution.py:532
  122.5 10.4 %all-to-all-start.4 = ((f32[8,1,128]{2,1,0:T(1,128)}), f32[8,1,128]{2,1,0:T(1,128)S(1)}, u32[]{:S(2)}, u32[]{:S(2)}) async-start(f32[8,1,128]{2,1,0:T(1,128)} %bitcast.17), calls=%async_computation.4 | async-start | bytes 8192 | tf_op jit(solution)/shard_map/all_to_all | solution.py:430

commit v7 on v6

--- a/solution.py
+++ b/solution.py
@@ -84,7 +84,7 @@
         pltpu.make_async_copy(graph_hbm, graph_ref, sems.at[10]),
         pltpu.make_async_copy(par_hbm, par_ref, sems.at[11]),
     ]
-    for copy in copies:
+    for copy in copies[3:] + copies[:3]:
         copy.start()
     order = spread_order()
     for copy in copies[3:]:
@@ -162,17 +162,17 @@
     tile = rows_ref[:, GROUPS * WIDE :]
     outer = jnp.concatenate([rows_ref[:, 0:WIDE], rows_ref[:, 2 * WIDE : 3 * WIDE]], axis=0)
     middle = rows_ref[:, WIDE : 2 * WIDE]
-    outer_lane = lax.broadcasted_iota(jnp.int32, (128 * REFS, 2 * total), 1)
-    middle_lane = lax.broadcasted_iota(jnp.int32, (64 * REFS, total), 1)
-    size = 16 * REFS * PIECE
+    outer_lane = lax.broadcasted_iota(jnp.int32, (256 * REFS, 2 * total), 1)
+    middle_lane = lax.broadcasted_iota(jnp.int32, (128 * REFS, total), 1)
+    size = 32 * REFS * PIECE
     copies = []
-    for step in range(PEERS // 16):
-        long_at = long_ref[step * 128 * REFS : (step + 1) * 128 * REFS]
-        short_at = short_ref[step * 64 * REFS : (step + 1) * 64 * REFS]
+    for step in range(PEERS // 32):
+        long_at = long_ref[step * 256 * REFS : (step + 1) * 256 * REFS]
+        short_at = short_ref[step * 128 * REFS : (step + 1) * 128 * REFS]
         long = dot(one_hot(long_at == outer_lane), outer)
         short = dot(one_hot(short_at == middle_lane), middle)
         pieces = []
-        for peer in range(16):
+        for peer in range(32):
             pieces.append(long[peer * 8 * REFS : (peer + 1) * 8 * REFS])
             pieces.append(short[peer * 4 * REFS : (peer + 1) * 4 * REFS])
         at = pl.ds(step * size, size)
@@ -277,12 +277,12 @@
 ):
     order = gather_order()
     size = 4 * REFS * PIECE
-    for part in range(PEERS // 4):
-        mixed = dot(order, rows_ref[part * size : (part + 1) * size]).astype(BF16)
-        cols = slice((part // 4) * WIDE, (part // 4 + 1) * WIDE)
+    for part in range(PEERS // 8):
+        sides = [rows_ref[(part + 4 * side) * size : (part + 4 * side + 1) * size] for side in range(2)]
+        mixed = dot(order, jnp.concatenate(sides, axis=1)).astype(BF16)
         for image in range(REFS):
-            at = (image // 2) * TOK + (part % 4) * 48
-            x_ref[image % 2, at : at + 48, cols] = mixed[image * 48 : image * 48 + 48]
+            at = (image // 2) * TOK + part * 48
+            x_ref[image % 2, at : at + 48] = mixed[image * 48 : image * 48 + 48]
 
     for slot in range(2):
         for pair in range(PAIRS):
@@ -497,7 +497,7 @@
             shape((REFS, 256), F32),
             shape((REFS, 128), F32),
         ),
-        scratch_shapes=[pltpu.VMEM((count, WIDE), BF16), pltpu.SemaphoreType.DMA((PEERS // 16,))],
+        scratch_shapes=[pltpu.VMEM((count, WIDE), BF16), pltpu.SemaphoreType.DMA((PEERS // 32,))],
         compiler_params=params_for(28),
         name="select",
     )(rank.reshape(1), spread, long_rows, short_rows, own, fold)

time: 135 us -> 134 us (level)
  no operation moved by 1% of the time
where the time goes in v7:
time: 134 us; the launch traced here: 133 us
  blocking collectives  55.9 us (42%)
  starting transfers between devices  26.5 us (20%)
  Pallas kernels  24.8 us (19%)
  waiting for transfers between devices  21.2 us (16%)
  local copies, waits for them, and re-layouts  3.57 us (3%)
    all_to_all x2, blocking collectives, exchange(): return lax.all_to_all(x, axis, split_axis=0, concat_axis=0, tiled=True)  55.9 us
    all_to_all x3, waiting for transfers between devices, exchange(): return lax.all_to_all(x, axis, split_axis=0, concat_axis=0, tiled=True)  21.2 us
    all_to_all x3, starting transfers between devices, exchange(): return lax.all_to_all(x, axis, split_axis=0, concat_axis=0, tiled=True)  18.7 us
    pallas_call x1, Pallas kernels, on_device(): pl.pallas_call(decode_kernel, in_specs=[inside] * 7, out_specs=(inside, i...  11.6 us
    ppermute x1, starting transfers between devices, on_device(): own_grad = lax.ppermute(own_grad, PLANE + ('z',), HOME)  4.74 us
    pallas_call x1, Pallas kernels, on_device(): pl.pallas_call(embed_kernel, in_specs=[outside] * 7, out_specs=outside, o...  4.34 us
    pallas_call x1, Pallas kernels, on_device(): pl.pallas_call(fold_kernel, in_specs=[inside, outside, outside, outside],...  3.91 us
    ppermute x1, starting transfers between devices, on_device(): points = lax.ppermute(points, PLANE + ('z',), HOME)  3.01 us
  transfers between devices with their start and end apart: 5, of which 3 were waited for; matrix products, arithmetic and copies ran while one was open for 1% of the time, Pallas kernels for 5%

profile of v7, /device:TPU:1, one launch (start us, length us, event | category | flops | bytes accessed | tf_op | source)
XLA Modules:
  0.0 132.8 jit_solution(4063231728757622581)
XLA Ops:
  0.6 0.0 copy-start.7
  0.6 4.3 %embed.1 = bf16[256,1280]{1,0:T(8,128)(2,1)S(1)} custom-call(bf16[384,1024]{1,0:T(8,128)(2,1)} %bitcast.37, bf16[1024,768]{1,0:T(8,128)(2,1)} %weight_hbm.1, bf16[2,192]{1,0:T(2,128)(2,1)} %bitcast.33, bf16[2,12]{1,0:T(2,128)(2,1)} %bitcast.35, bf16[1,2]{1,0:T(2,128)(2,1)} %focal_hbm.1, s32[2,128]{1,0:T(2,128)} %bitcast.39, f32[4,13]{1,0:T(4,128)} %bitcast.31), custom_call_target="tpu_custom_call" | custom-call | tf_op jit(solution)/shard_map/embed/pallas_call | solution.py:434
  5.0 17.3 %all_to_all.56 = bf16[8,32,1280]{2,1,0:T(8,128)(2,1)} all-to-all(bf16[8,32,1280]{2,1,0:T(8,128)(2,1)S(1)} %bitcast.27), channel_id=1, replica_groups=mesh['x'=4,'c'=2,'y'=4,'z'=8] {'x','c'}, dimensions={0} | all-to-all | bytes 1310720 | tf_op jit(solution)/shard_map/all_to_all | solution.py:430
  22.2 10.6 %all-to-all-start.1 = ((bf16[32,8,1280]{2,1,0:T(8,128)(2,1)}), bf16[32,8,1280]{2,1,0:T(8,128)(2,1)S(1)}, u32[]{:S(2)}, u32[]{:S(2)}) async-start(bf16[32,8,1280]{2,1,0:T(8,128)(2,1)} %bitcast.9), calls=%async_computation.1 | async-start | bytes 1310720 | tf_op jit(solution)/shard_map/all_to_all | solution.py:430
  32.9 0.0 copy-done.7
  32.9 3.9 %fold.1 = (bf16[2,192,768]{2,1,0:T(8,128)(2,1)S(1)}, bf16[2,768,768]{2,1,0:T(8,128)(2,1)S(1)}, bf16[2,768,768]{2,1,0:T(8,128)(2,1)S(1)}) custom-call(bf16[2,16,768]{2,1,0:T(8,128)(2,1)S(1)} %pad.4.head_ref, bf16[2,768,768]{2,1,0:T(8,128)(2,1)} %out_hbm.1, bf16[2,768,1536]{2,1,0:T(8,128)(2,1)} %keyval_hbm.1, bf16[2,768,768]{2,1,0:T(8,128)(2,1)} %query_hbm.1), custom_call_target="tpu_custom_call" | custom-call | flops 2000000000 | bytes 6000000 | tf_op jit(solution)/shard_map/fold/pallas_call | solution.py:475
  36.8 0.0 copy-start
  36.8 1.4 %copy-done = bf16[2,768,768]{2,1,0:T(8,128)(2,1)} copy-done((bf16[2,768,768]{2,1,0:T(8,128)(2,1)}, bf16[2,768,768]{2,1,0:T(8,128)(2,1)S(1)}, u32[]{:S(2)}) %copy-start) | copy-done | bytes 2359320
  38.2 0.0 copy-start.2
  38.2 1.4 %copy-done.2 = bf16[2,768,768]{2,1,0:T(8,128)(2,1)} copy-done((bf16[2,768,768]{2,1,0:T(8,128)(2,1)}, bf16[2,768,768]{2,1,0:T(8,128)(2,1)S(1)}, u32[]{:S(2)}) %copy-start.2) | copy-done | bytes 2359320
  39.7 0.7 constant_dynamic-slice_fusion.tile_ref
  40.4 1.1 index.1
  41.5 10.1 %all-to-all-done.1 = bf16[32,8,1280]{2,1,0:T(8,128)(2,1)S(1)} async-done(((bf16[32,8,1280]{2,1,0:T(8,128)(2,1)}), bf16[32,8,1280]{2,1,0:T(8,128)(2,1)S(1)}, u32[]{:S(2)}, u32[]{:S(2)}) %all-to-all-start.1) | async-done | bytes 655392 | tf_op jit(solution)/shard_map/all_to_all | solution.py:430
  51.6 2.1 %select.2 = (bf16[3072,384]{1,0:T(8,128)(2,1)S(1)}, f32[8,256]{1,0:T(8,128)S(1)}, f32[8,128]{1,0:T(8,128)S(1)}) custom-call(s32[1]{0:T(128)} %bitcast.rank_ref.me_ref, bf16[256,1280]{1,0:T(8,128)(2,1)S(1)} %bitcast.26, s32[2048,1]{1,0:T(8,128)S(1)} %get-tuple-element.23.long_ref, s32[1024,1]{1,0:T(8,128)S(1)} %get-tuple-element.24.short_ref, ...), custom_call_target="tpu_custom_call" | custom-call | tf_op jit(solution)/shard_map/select/pallas_call | solution.py:491
  53.7 0.0 copy-start.1
  53.7 0.0 copy-start.3
  53.8 38.7 %all_to_all.57 = bf16[32,96,384]{2,1,0:T(8,128)(2,1)S(1)} all-to-all(bf16[32,96,384]{2,1,0:T(8,128)(2,1)S(1)} %bitcast.28), channel_id=1, replica_groups=mesh['x'=4,'c'=2,'y'=4,'z'=8] {'x','c','y'}, dimensions={0} | all-to-all | bytes 4718592 | tf_op jit(solution)/shard_map/all_to_all | solution.py:430
  92.4 0.0 copy-done.1
  92.4 0.0 copy-done.3
  92.4 0.0 copy-start.4
  92.4 0.0 copy-start.5
  92.4 0.0 copy-start.6
  92.4 11.6 %decode.1 = (f32[8,4,192]{2,1,0:T(4,128)S(1)}, bf16[256,256]{1,0:T(8,128)(2,1)}) custom-call(bf16[3072,384]{1,0:T(8,128)(2,1)S(1)} %bitcast.25, bf16[2,768,768]{2,1,0:T(8,128)(2,1)S(1)} %copy-done.1, bf16[2,768,768]{2,1,0:T(8,128)(2,1)S(1)} %copy-done.3, bf16[2,192,768]{2,1,0:T(8,128)(2,1)S(1)} %get-tuple-element.26.after_ref.fold_ref, ...), custom_call_target="tpu_custom_call" | custom-call | tf_op jit(solution)/shard_map/decode/pallas_call | solution.py:507
  104.1 4.1 %all-to-all-start.3 = ((bf16[32,8,256]{2,1,0:T(8,128)(2,1)}), bf16[32,8,256]{2,1,0:T(8,128)(2,1)S(1)}, u32[]{:S(2)}, u32[]{:S(2)}) async-start(bf16[32,8,256]{2,1,0:T(8,128)(2,1)} %bitcast.14), calls=%async_computation.3 | async-start | bytes 262144 | tf_op jit(solution)/shard_map/all_to_all | solution.py:430
  108.2 3.0 %collective-permute-start.1 = (f32[8,4,192]{2,1,0:T(4,128)S(1)}, f32[8,4,192]{2,1,0:T(4,128)S(1)}, u32[]{:S(2)}, u32[]{:S(2)}) collective-permute-start(f32[8,4,192]{2,1,0:T(4,128)S(1)} %get-tuple-element.35), channel_id=1, source_target_pairs={{0,0},{1,32},{2,64},{3,96},{4,128},{5,160},{6,192},{7,224},{8,1},{... | collective-permute-start | bytes 73736 | tf_op jit(solution)/shard_map/ppermute | solution.py:533
  111.2 4.7 %all-to-all-done.3 = bf16[32,8,256]{2,1,0:T(8,128)(2,1)S(1)} async-done(((bf16[32,8,256]{2,1,0:T(8,128)(2,1)}), bf16[32,8,256]{2,1,0:T(8,128)(2,1)S(1)}, u32[]{:S(2)}, u32[]{:S(2)}) %all-to-all-start.3) | async-done | bytes 131104 | tf_op jit(solution)/shard_map/all_to_all | solution.py:430
  115.9 1.0 combine.1
  116.9 4.7 %collective-permute-start = (f32[16,256]{1,0:T(8,128)S(1)}, f32[16,256]{1,0:T(8,128)S(1)}, u32[]{:S(2)}, u32[]{:S(2)}) collective-permute-start(f32[16,256]{1,0:T(8,128)S(1)} %get-tuple-element.34), channel_id=1, source_target_pairs={{0,0},{1,32},{2,64},{3,96},{4,128},{5,160},{6,192},{7,224},{8,1},{... | collective-permute-start | bytes 49160 | tf_op jit(solution)/shard_map/ppermute | solution.py:532
  121.6 4.0 %all-to-all-start.4 = ((f32[8,1,128]{2,1,0:T(1,128)}), f32[8,1,128]{2,1,0:T(1,128)S(1)}, u32[]{:S(2)}, u32[]{:S(2)}) async-start(f32[8,1,128]{2,1,0:T(1,128)} %bitcast.17), calls=%async_computation.4 | async-start | bytes 8192 | tf_op jit(solution)/shard_map/all_to_all | solution.py:430
  125.6 0.0 collective-permute-done.1.points_ref
  125.6 6.4 %all-to-all-done.4 = f32[8,1,128]{2,1,0:T(1,128)S(1)} async-done(((f32[8,1,128]{2,1,0:T(1,128)}), f32[8,1,128]{2,1,0:T(1,128)S(1)}, u32[]{:S(2)}, u32[]{:S(2)}) %all-to-all-start.4) | async-done | bytes 4128 | tf_op jit(solution)/shard_map/all_to_all | solution.py:430
  132.0 0.0 collective-permute-done.own_ref
  132.0 0.0 copy-done.4
  132.1 0.0 copy-done.5
  132.1 0.0 copy-done.6
  132.1 0.7 update.1
  (1 shorter events, 0.0 us)
Async XLA Ops:
  0.6 32.2 %copy-start.7 = (bf16[2,768,4]{1,2,0:T(4,128)(2,1)S(1)}, bf16[2,768,4]{1,2,0:T(4,128)(2,1)}, u32[]{:S(2)}) copy-start(bf16[2,768,4]{1,2,0:T(4,128)(2,1)} %param.21) | copy-start | bytes 36868
  22.2 29.4 %all-to-all-start.1 = ((bf16[32,8,1280]{2,1,0:T(8,128)(2,1)}), bf16[32,8,1280]{2,1,0:T(8,128)(2,1)S(1)}, u32[]{:S(2)}, u32[]{:S(2)}) async-start(bf16[32,8,1280]{2,1,0:T(8,128)(2,1)} %bitcast.9), calls=%async_computation.1 | async-start | bytes 1310720 | tf_op jit(solution)/shard_map/all_to_all | solution.py:430
  36.8 1.4 %copy-start = (bf16[2,768,768]{2,1,0:T(8,128)(2,1)}, bf16[2,768,768]{2,1,0:T(8,128)(2,1)S(1)}, u32[]{:S(2)}) copy-start(bf16[2,768,768]{2,1,0:T(8,128)(2,1)S(1)} %get-tuple-element.28.query_ref) | copy-start | bytes 7077892
  38.2 1.4 %copy-start.2 = (bf16[2,768,768]{2,1,0:T(8,128)(2,1)}, bf16[2,768,768]{2,1,0:T(8,128)(2,1)S(1)}, u32[]{:S(2)}) copy-start(bf16[2,768,768]{2,1,0:T(8,128)(2,1)S(1)} %get-tuple-element.29.key_ref) | copy-start | bytes 7077892
  53.7 38.7 %copy-start.1 = (bf16[2,768,768]{2,1,0:T(8,128)(2,1)S(1)}, bf16[2,768,768]{2,1,0:T(8,128)(2,1)}, u32[]{:S(2)}) copy-start(bf16[2,768,768]{2,1,0:T(8,128)(2,1)} %copy-done) | copy-start | bytes 7077892
  53.7 38.7 %copy-start.3 = (bf16[2,768,768]{2,1,0:T(8,128)(2,1)S(1)}, bf16[2,768,768]{2,1,0:T(8,128)(2,1)}, u32[]{:S(2)}) copy-start(bf16[2,768,768]{2,1,0:T(8,128)(2,1)} %copy-done.2) | copy-start | bytes 7077892
  92.4 39.6 %copy-start.4 = (f32[1,4,13]{2,1,0:T(4,128)S(1)}, f32[1,4,13]{2,1,0:T(4,128)}, u32[]{:S(2)}) copy-start(f32[1,4,13]{2,1,0:T(4,128)} %param.16) | copy-start | bytes 628
  92.4 39.6 %copy-start.5 = (bf16[1,2,192]{2,1,0:T(2,128)(2,1)S(1)}, bf16[1,2,192]{2,1,0:T(2,128)(2,1)}, u32[]{:S(2)}) copy-start(bf16[1,2,192]{2,1,0:T(2,128)(2,1)} %param.13) | copy-start | bytes 2308
  92.4 39.6 %copy-start.6 = (bf16[1,2,12]{2,1,0:T(2,128)(2,1)S(1)}, bf16[1,2,12]{2,1,0:T(2,128)(2,1)}, u32[]{:S(2)}) copy-start(bf16[1,2,12]{2,1,0:T(2,128)(2,1)} %param.14) | copy-start | bytes 148
  104.1 11.8 %all-to-all-start.3 = ((bf16[32,8,256]{2,1,0:T(8,128)(2,1)}), bf16[32,8,256]{2,1,0:T(8,128)(2,1)S(1)}, u32[]{:S(2)}, u32[]{:S(2)}) async-start(bf16[32,8,256]{2,1,0:T(8,128)(2,1)} %bitcast.14), calls=%async_computation.3 | async-start | bytes 262144 | tf_op jit(solution)/shard_map/all_to_all | solution.py:430
  108.2 17.4 %collective-permute-start.1 = (f32[8,4,192]{2,1,0:T(4,128)S(1)}, f32[8,4,192]{2,1,0:T(4,128)S(1)}, u32[]{:S(2)}, u32[]{:S(2)}) collective-permute-start(f32[8,4,192]{2,1,0:T(4,128)S(1)} %get-tuple-element.35), channel_id=1, source_target_pairs={{0,0},{1,32},{2,64},{3,96},{4,128},{5,160},{6,192},{7,224},{8,1},{... | collective-permute-start | bytes 73736 | tf_op jit(solution)/shard_map/ppermute | solution.py:533
  116.9 15.2 %collective-permute-start = (f32[16,256]{1,0:T(8,128)S(1)}, f32[16,256]{1,0:T(8,128)S(1)}, u32[]{:S(2)}, u32[]{:S(2)}) collective-permute-start(f32[16,256]{1,0:T(8,128)S(1)} %get-tuple-element.34), channel_id=1, source_target_pairs={{0,0},{1,32},{2,64},{3,96},{4,128},{5,160},{6,192},{7,224},{8,1},{... | collective-permute-start | bytes 49160 | tf_op jit(solution)/shard_map/ppermute | solution.py:532
  121.6 10.4 %all-to-all-start.4 = ((f32[8,1,128]{2,1,0:T(1,128)}), f32[8,1,128]{2,1,0:T(1,128)S(1)}, u32[]{:S(2)}, u32[]{:S(2)}) async-start(f32[8,1,128]{2,1,0:T(1,128)} %bitcast.17), calls=%async_computation.4 | async-start | bytes 8192 | tf_op jit(solution)/shard_map/all_to_all | solution.py:430
